TPU v7x, 512 devices: a whole 4x4x16 slice. The times are simulated.
512 devices in a mesh: rep: 4 (over y), ep: 128 (over x, z, core).
Axes of the slice: x: 4, y: 4, z: 16, core: 2. Of those that a mesh axis runs over, the one named last changes fastest.
Arguments:
- queries: bfloat16 [16384, 4096], P('ep', 'rep'), may hold values from -8 to 8
- keys: bfloat16 [16384, 512], P('ep', 'rep'), may hold values from -8 to 8
- values: bfloat16 [16384, 512], P('ep', 'rep'), may hold values from -6 to 6
- doc_start: int32 [16384], P('ep'), may hold values from 0 to 16383, as said below
- residual: bfloat16 [128, 128, 2048], P('ep', 'rep'), may hold values from -6 to 6
- out_weight: bfloat16 [4096, 2048], P(('rep', 'ep')), may hold values from -0.09375 to 0.09375
- norm_gain: float32 [2048], replicated, may hold values from 0.1 to 1.9
- gate_weight: bfloat16 [128, 768, 2048], P('ep', 'rep'), may hold values from -0.125 to 0.125
- up_weight: bfloat16 [128, 768, 2048], P('ep', 'rep'), may hold values from -0.125 to 0.125
- down_weight: bfloat16 [128, 768, 2048], P('ep', None, 'rep'), may hold values from -0.21875 to 0.21875
- route_ids: int32 [128, 128, 8], P('ep', 'rep'), may hold values from 0 to 127, all different within a row; in each aligned block of 32 rows (0 to 31, 32 to 63, ..., all dimensions but the last counted through in order) at most 3 rows name the same one
- route_weights: bfloat16 [128, 128, 8], P('ep', 'rep'), may hold values from 0.099609375 to 0.3984375
Outputs:
- updated: bfloat16 [128, 128, 2048], P('ep', 'rep')
Inputs may be any that keep to these rules, and one draw needn't show every extreme that they name: `doc_start`: each token's document is a run of consecutive positions of at most 512 tokens that begins at this value; one document has exactly that length. `route_ids`: a token names 8 different experts; in each aligned block of 32 tokens no expert is named more than 3 times, a bound that some block reaches.
All inputs are finite; a program needn't handle non-finite values.
Results may differ from a plain program's by a relative error of at most 0.005.
Values may be sent and summed in bfloat16 or wider, within the bound.
No kernel may reach another device: no remote copies, remote signals or barrier semaphores. Data moves between devices by JAX's collectives and lax.ppermute only.
A program may use at most 64 MiB of HBM per device.

v0:
```python
import jax
import jax.numpy as jnp
from jax import lax
from jax.sharding import PartitionSpec as P

HS = 128
HOPS = 4


def passed_along(value, axis, by):
    devices = lax.axis_size(axis)
    pairs = [(i, i + by) for i in range(devices) if 0 <= i + by < devices]
    return lax.ppermute(value, axis, pairs)


def contract_rows(left, right):
    return lax.dot_general(
        left, right, (((1,), (1,)), ((), ())), preferred_element_type=jnp.float32
    )


def on_device(
    queries,
    keys,
    values,
    doc_start,
    residual,
    out_weight,
    norm_gain,
    gate_weight,
    up_weight,
    down_weight,
    route_ids,
    route_weights,
):
    tok_ep = queries.shape[0]
    group_size = queries.shape[1] // HS
    score_scale = 1.0 / HS**0.5
    offset = lax.axis_index("ep") * tok_ep
    blocks = [((keys, values), 0)]
    moving = (keys, values)
    for hop_count in range(1, HOPS + 1):
        moving = passed_along((moving[0], moving[1]), "ep", 1)
        blocks.append((moving, hop_count))
    ordered = blocks[::-1]
    key_all = jnp.concatenate([entry_pair[0][0] for entry_pair in ordered], 0)
    value_all = jnp.concatenate([entry_pair[0][1] for entry_pair in ordered], 0)
    key_pos = jnp.concatenate(
        [
            offset - entry_pair[1] * tok_ep + jnp.arange(tok_ep, dtype=jnp.int32)
            for entry_pair in ordered
        ],
        0,
    )
    query_pos = offset + jnp.arange(tok_ep, dtype=jnp.int32)
    key_mask = (key_pos[None, :] <= query_pos[:, None]) & (key_pos[None, :] >= doc_start[:, None])
    query_heads = queries.reshape(tok_ep, group_size, HS)
    score_vals = (
        jnp.einsum("igd,jd->gij", query_heads, key_all, preferred_element_type=jnp.float32)
        * score_scale
    )
    score_vals = jnp.where(key_mask[None], score_vals, -jnp.inf)
    row_peak = jnp.max(score_vals, axis=-1, keepdims=True)
    prob_vals = jnp.exp(score_vals - row_peak)
    row_total = jnp.sum(prob_vals, axis=-1, keepdims=True)
    weighted = jnp.einsum(
        "gij,jd->igd", prob_vals.astype(jnp.bfloat16), value_all, preferred_element_type=jnp.float32
    )
    attended = (
        (weighted / jnp.transpose(row_total, (1, 0, 2)))
        .reshape(tok_ep, group_size * HS)
        .astype(jnp.bfloat16)
    )
    width = out_weight.shape[1]
    partial_value = jnp.dot(
        attended,
        lax.all_gather(out_weight, "ep", axis=0, tiled=True),
        preferred_element_type=jnp.float32,
    )
    head_total = lax.psum_scatter(partial_value, "rep", scatter_dimension=0, tiled=True)
    hidden_sum = residual[0].astype(jnp.float32) + head_total
    inverse_rms = lax.rsqrt(jnp.mean(hidden_sum * hidden_sum, axis=-1, keepdims=True) + 1e-06)
    normed = (hidden_sum * inverse_rms * norm_gain).astype(jnp.bfloat16)
    expert_ids = route_ids[0]
    gate_vals = route_weights[0]
    tok_sub = expert_ids.shape[0]
    top_count = expert_ids.shape[1]
    experts = gate_weight.shape[0] * lax.axis_size("ep")
    capacity = min(tok_sub, max(2, tok_sub * top_count // experts + 1))
    flat_ids = expert_ids.reshape(-1)
    onehot = (flat_ids[:, None] == jnp.arange(experts, dtype=jnp.int32)[None, :]).astype(jnp.int32)
    before = jnp.cumsum(onehot, axis=0) - onehot
    slot_rank = jnp.sum(before * onehot, axis=1).reshape(tok_sub, top_count)
    target = expert_ids * capacity + slot_rank
    slot_lanes = jnp.arange(experts * capacity, dtype=jnp.int32)
    slot_hit = target[None, :, :] == slot_lanes[:, None, None]
    spread = jnp.any(slot_hit, axis=-1).astype(jnp.bfloat16)
    gather_back = jnp.sum(
        jnp.where(slot_hit, gate_vals[None].astype(jnp.float32), 0.0), axis=-1
    ).astype(jnp.bfloat16)
    send_rows = jnp.dot(spread, normed, preferred_element_type=jnp.float32).astype(jnp.bfloat16)
    send_rows = send_rows.reshape(experts, capacity, width)
    received = lax.all_to_all(send_rows, "ep", split_axis=0, concat_axis=0, tiled=True)
    segment = lax.all_gather(received, "rep", axis=0, tiled=True)
    seg_rows = segment.reshape(-1, segment.shape[2])
    gate_act = contract_rows(seg_rows, gate_weight[0])
    up_act = contract_rows(seg_rows, up_weight[0])
    hidden_act = (jax.nn.silu(gate_act) * up_act).astype(jnp.bfloat16)
    hidden_vals = hidden_act.reshape(segment.shape[0], segment.shape[1], -1)
    hidden_flat = hidden_vals.reshape(-1, hidden_vals.shape[2])
    local_cols = down_weight.shape[2]
    weight_rows = down_weight[0]
    column_out = jnp.dot(
        lax.all_gather(hidden_flat, "rep", axis=1, tiled=True),
        weight_rows,
        preferred_element_type=jnp.float32,
    )
    column_out = column_out.astype(jnp.bfloat16).reshape(
        lax.axis_size("rep"), lax.axis_size("ep"), capacity, local_cols
    )
    returned = lax.all_to_all(
        lax.all_to_all(column_out, "rep", split_axis=0, concat_axis=3, tiled=True),
        "ep",
        split_axis=1,
        concat_axis=1,
        tiled=True,
    ).reshape(-1, width)
    expert_mix = jnp.einsum("st,sd->td", gather_back, returned, preferred_element_type=jnp.float32)
    return (hidden_sum + expert_mix).astype(jnp.bfloat16)[None]


def solution(mesh):
    placed = (
        P("ep", "rep"),
        P("ep", "rep"),
        P("ep", "rep"),
        P("ep"),
        P("ep", "rep", None),
        P(("rep", "ep"), None),
        P(),
        P("ep", "rep", None),
        P("ep", "rep", None),
        P("ep", None, "rep"),
        P("ep", "rep", None),
        P("ep", "rep", None),
    )
    return jax.shard_map(
        on_device, mesh=mesh, in_specs=placed, out_specs=P("ep", "rep", None), check_vma=False
    )
```

profile of v0, /device:TPU:1, one launch (start us, length us, event | category | flops | bytes accessed | tf_op | source)
XLA Modules:
  0.0 623.7 jit_solution(13817674593973605570)
XLA Ops:
  7.3 4.9 collective-permute-start.4
  13.1 1.9 collective-permute-start
  15.1 1.3 collective-permute-done.4
  16.4 2.7 collective-permute-start.5
  19.1 1.9 collective-permute-start.1
  21.0 3.9 collective-permute-start.6
  25.0 1.9 collective-permute-start.2
  26.9 5.1 collective-permute-start.7
  32.9 1.9 collective-permute-start.3
  36.1 1.5 fusion.5
  38.9 119.3 %all-gather.4.cloned.1.call-done = bf16[1024,2048]{1,0:T(8,128)(2,1)} async-done(((bf16[8,2048]{1,0:T(8,128)(2,1)}), bf16[1024,2048]{1,0:T(8,128)(2,1)}) %all-gather.4.cloned.1.call-update) | async-done | bytes 4194320 | tf_op jit(solution)/shard_map/all_gather | solution.py:77
  158.2 3.9 fusion.38
  163.4 24.6 %reduce-scatter.2.cloned.1.call-done = f32[32,2048]{1,0:T(8,128)} async-done(((f32[128,2048]{1,0:T(8,128)}), f32[32,2048]{1,0:T(8,128)}) %reduce-scatter.2.cloned.1.call-update) | async-done | bytes 262160 | tf_op jit(solution)/shard_map/reduce_scatter | solution.py:80
  189.1 2.7 convolution_convert_fusion.1
  191.8 4.0 reshape.111
  195.8 116.7 %all_to_all.28 = bf16[128,3,2048]{2,1,0:T(4,128)(2,1)S(1)} all-to-all(bf16[128,3,2048]{2,1,0:T(4,128)(2,1)S(1)} %reshape.111), channel_id=1, replica_groups=mesh['rep'=4,'ep'=128] {'ep'}, dimensions={0} | all-to-all | bytes 3145728 | tf_op jit(solution)/shard_map/all_to_all | solution.py:103
  312.5 2.3 copy.56
  315.1 65.2 %all-gather.6.cloned.1.call-done = bf16[512,3,2048]{2,0,1:T(8,128)(2,1)} async-done(((bf16[128,3,2048]{2,0,1:T(8,128)(2,1)}), bf16[512,3,2048]{2,0,1:T(8,128)(2,1)}) %all-gather.6.cloned.1.call-update) | async-done | bytes 6291472 | tf_op jit(solution)/shard_map/all_gather | solution.py:104
  380.2 11.4 %copy.57 = bf16[512,3,2048]{2,1,0:T(4,128)(2,1)} copy(bf16[512,3,2048]{2,0,1:T(8,128)(2,1)} %all-gather.6.cloned.1.call-done) | data formatting | bytes 12582912 | tf_op jit(solution)/shard_map/all_gather | solution.py:104
  391.6 16.4 %reshape.112 = bf16[1536,2048]{1,0:T(8,128)(2,1)} reshape(bf16[512,3,2048]{2,1,0:T(4,128)(2,1)} %copy.57) | data formatting | bytes 12582912 | tf_op jit(solution)/shard_map/reshape | solution.py:105
  408.1 5.2 fusion.20
  413.2 3.2 fusion
  416.4 41.6 %all-gather.8.cloned.1.call-done = bf16[1536,768]{0,1:T(8,128)(2,1)} async-done(((bf16[1536,192]{0,1:T(8,128)(2,1)}), bf16[1536,768]{0,1:T(8,128)(2,1)}) %all-gather.8.cloned.1.call-update) | async-done | bytes 2359312 | tf_op jit(solution)/shard_map/all_gather | solution.py:114
  458.0 4.2 convolution_convert_fusion
  462.3 4.0 reshape.113
  466.7 22.4 %all_to_all.29 = bf16[4,128,3,512]{3,1,2,0:T(8,128)(2,1)S(1)} all-to-all(bf16[4,128,3,512]{3,1,2,0:T(8,128)(2,1)S(1)} %copy.58), channel_id=1, replica_groups=mesh['rep'=4,'ep'=128] {'rep'}, dimensions={0} | all-to-all | bytes 3145728 | tf_op jit(solution)/shard_map/all_to_all | solution.py:122
  489.1 1.6 copy.59
  490.6 4.5 copy.60
  495.2 17.9 %all-to-all-start.2 = ((bf16[1,128,3,2048]{3,2,0,1:T(4,128)(2,1)}), bf16[1,128,3,2048]{3,2,0,1:T(4,128)(2,1)S(1)}, u32[]{:S(2)}, u32[]{:S(2)}) async-start(bf16[1,128,3,2048]{3,2,0,1:T(4,128)(2,1)} %copy.60), calls=%async_computation.3 | async-start | bytes 4194304 | tf_op jit(solution)/shard_map/all_to_all | solution.py:121
  513.4 98.8 %all-to-all-done.2 = bf16[1,128,3,2048]{3,2,0,1:T(4,128)(2,1)S(1)} async-done(((bf16[1,128,3,2048]{3,2,0,1:T(4,128)(2,1)}), bf16[1,128,3,2048]{3,2,0,1:T(4,128)(2,1)S(1)}, u32[]{:S(2)}, u32[]{:S(2)}) %all-to-all-start.2) | async-done | bytes 1572896 | tf_op jit(solution)/shard_map/all_to_all | solution.py:121
  612.2 2.5 reshape.114
  614.8 2.4 fusion.4
  (74 shorter events, 8.2 us)
Async XLA Ops:
  6.5 451.5 %copy-start = (bf16[1,768,512]{2,1,0:T(8,128)(2,1)S(1)}, bf16[1,768,512]{2,1,0:T(8,128)(2,1)}, u32[]{:S(2)}) copy-start(bf16[1,768,512]{2,1,0:T(8,128)(2,1)} %param.21) | copy-start | bytes 2359300
  6.5 151.7 %all-gather.4.cloned.1.call-start = ((), (), s32[]{:S(2)}) async-start(), calls=%async_computation.4 | async-start | bytes 4227072 | tf_op jit(solution)/shard_map/all_gather | solution.py:77
  7.3 180.7 %reduce-scatter.2.cloned.1.call-start = ((), (), s32[]{:S(2)}) async-start(), calls=%async_computation.5 | async-start | bytes 1310720 | tf_op jit(solution)/shard_map/reduce_scatter | solution.py:80
  7.3 9.1 %collective-permute-start.4 = (bf16[128,128]{1,0:T(8,128)(2,1)}, bf16[128,128]{1,0:T(8,128)(2,1)S(1)}, u32[]{:S(2)}, u32[]{:S(2)}) collective-permute-start(bf16[128,128]{1,0:T(8,128)(2,1)} %param.13), channel_id=1, source_target_pairs={{0,1},{1,2},{2,3},{3,4},{4,5},{5,6},{6,7},{7,8},{8,9},{9,10},{10,1... | collective-permute-start | bytes 98312 | tf_op jit(solution)/shard_map/ppermute | solution.py:13
  13.1 6.0 collective-permute-start
  16.4 4.6 collective-permute-start.5
  19.1 5.9 collective-permute-start.1
  21.0 5.9 collective-permute-start.6
  25.0 7.9 %collective-permute-start.2 = (bf16[128,128]{0,1:T(8,128)(2,1)S(1)}, bf16[128,128]{0,1:T(8,128)(2,1)S(1)}, u32[]{:S(2)}, u32[]{:S(2)}) collective-permute-start(bf16[128,128]{0,1:T(8,128)(2,1)S(1)} %collective-permute-done.1), channel_id=1, source_target_pairs={{0,1},{1,2},{2,3},{3,4},{4,5},{5,6},{6,7},{7,8},{8,9},{9,10},{10,1... | collective-permute-start | bytes 98312 | tf_op jit(solution)/shard_map/ppermute | solution.py:13
  26.9 7.9 %collective-permute-start.7 = (bf16[128,128]{1,0:T(8,128)(2,1)S(1)}, bf16[128,128]{1,0:T(8,128)(2,1)S(1)}, u32[]{:S(2)}, u32[]{:S(2)}) collective-permute-start(bf16[128,128]{1,0:T(8,128)(2,1)S(1)} %collective-permute-done.6), channel_id=1, source_target_pairs={{0,1},{1,2},{2,3},{3,4},{4,5},{5,6},{6,7},{7,8},{8,9},{9,10},{10,1... | collective-permute-start | bytes 98312 | tf_op jit(solution)/shard_map/ppermute | solution.py:13
  32.9 3.1 collective-permute-start.3
  158.2 4.0 copy-start.5
  158.2 29.8 %copy-start.3 = (bf16[1,32,2048]{2,1,0:T(8,128)(2,1)S(1)}, bf16[1,32,2048]{2,1,0:T(8,128)(2,1)}, u32[]{:S(2)}) copy-start(bf16[1,32,2048]{2,1,0:T(8,128)(2,1)} %param.16) | copy-start | bytes 393220
  158.2 30.9 %copy-start.4 = (f32[2048]{0:T(1024)S(1)}, f32[2048]{0:T(1024)}, u32[]{:S(2)}) copy-start(f32[2048]{0:T(1024)} %param.18) | copy-start | bytes 24580
  162.2 218.1 %all-gather.6.cloned.1.call-start = ((), (), s32[]{:S(2)}) async-start(), calls=%async_computation.6 | async-start | bytes 7864320 | tf_op jit(solution)/shard_map/all_gather | solution.py:104
  314.8 143.2 %all-gather.8.cloned.1.call-start = ((), (), s32[]{:S(2)}) async-start(), calls=%async_computation.7 | async-start | bytes 2949120 | tf_op jit(solution)/shard_map/all_gather | solution.py:114
  391.6 16.4 %copy-start.7 = (bf16[1,192,2048]{2,1,0:T(8,128)(2,1)S(1)}, bf16[1,192,2048]{2,1,0:T(8,128)(2,1)}, u32[]{:S(2)}) copy-start(bf16[1,192,2048]{2,1,0:T(8,128)(2,1)} %param.19) | copy-start | bytes 2359300
  408.0 5.2 copy-start.1
  408.0 5.2 copy-start.8
  495.2 17.9 %copy-start.6 = (bf16[1,32,8]{1,2,0:T(8,128)(2,1)S(1)}, bf16[1,32,8]{1,2,0:T(8,128)(2,1)}, u32[]{:S(2)}) copy-start(bf16[1,32,8]{1,2,0:T(8,128)(2,1)} %param.23) | copy-start | bytes 1540
  495.2 117.1 %all-to-all-start.2 = ((bf16[1,128,3,2048]{3,2,0,1:T(4,128)(2,1)}), bf16[1,128,3,2048]{3,2,0,1:T(4,128)(2,1)S(1)}, u32[]{:S(2)}, u32[]{:S(2)}) async-start(bf16[1,128,3,2048]{3,2,0,1:T(4,128)(2,1)} %copy.60), calls=%async_computation.3 | async-start | bytes 4194304 | tf_op jit(solution)/shard_map/all_to_all | solution.py:121
  513.1 101.6 %copy-start.2 = (f32[32,2048]{1,0:T(8,128)S(1)}, f32[32,2048]{1,0:T(8,128)}, u32[]{:S(2)}) copy-start(f32[32,2048]{1,0:T(8,128)} %reduce-scatter.2.cloned.1.call-done) | copy-start | bytes 786436
Sparse Core Ops, SparseCore 0:
  10.5 147.6 all-gather.3
  162.3 25.6 reduce-scatter.1
  315.0 65.2 all-gather.5
  416.5 41.4 all-gather.7
where the time goes:
time: 625 us; the launch traced here: 624 us
  waiting for transfers between devices  352 us (56%)
  blocking collectives  139 us (22%)
  local copies, waits for them, and re-layouts  49.4 us (8%)
  starting transfers between devices  42.6 us (7%)
  matrix products  23.9 us (4%)
  between operations  13.5 us (2%)
    all_gather x1, waiting for transfers between devices, on_device(): lax.all_gather(out_weight, 'ep', axis=0, tiled=True)  119 us
    all_to_all x1, blocking collectives, on_device(): lax.all_to_all(send_rows, 'ep', split_axis=0, concat_axis=0, tiled=True)  117 us
    all_to_all x1, waiting for transfers between devices, on_device(): lax.all_to_all(lax.all_to_all(column_out, 'rep', split_axis=0, concat_axi...  98.8 us
    all_gather x1, waiting for transfers between devices, on_device(): segment = lax.all_gather(received, 'rep', axis=0, tiled=True)  65.2 us
    all_gather x1, waiting for transfers between devices, on_device(): lax.all_gather(hidden_flat, 'rep', axis=1, tiled=True)  41.6 us
    reduce_scatter x1, waiting for transfers between devices, on_device(): lax.psum_scatter(partial_value, 'rep', scatter_dimension=0, tiled=True)  24.6 us
    ppermute x8, starting transfers between devices, passed_along(): return lax.ppermute(value, axis, pairs)  24.4 us
    all_to_all x1, blocking collectives, on_device(): lax.all_to_all(column_out, 'rep', split_axis=0, concat_axis=3, tiled=True)  22.4 us
  transfers between devices with their start and end apart: 13, of which 7 were waited for; matrix products, arithmetic and copies ran while one was open for 1% of the time, Pallas kernels for 0%

commit v1 on v0

v1 whole, which is shorter than its diff:
```python
import jax
import jax.numpy as jnp
from jax import lax
from jax.sharding import Mesh, PartitionSpec as P

HS = 128
HOPS = 4
CAP = 3
BF = jnp.bfloat16
F32 = jnp.float32
EP = ("x", "z", "core")
XC = ("x", "core")


def from_earlier(value, by):
    devices = lax.axis_size(EP)
    return lax.ppermute(value, EP, [(i, i + by) for i in range(devices - by)])


def contract(left, right, dims):
    return lax.dot_general(left, right, (dims, ((), ())), preferred_element_type=F32)


def attention(queries, keys, values, doc_start):
    tok_ep = queries.shape[0]
    group_size = queries.shape[1] // HS
    offset = lax.axis_index(EP) * tok_ep
    own = jnp.concatenate([keys, values], 0)
    blocks = [from_earlier(own, by) for by in range(HOPS, 0, -1)] + [own]
    key_all = jnp.concatenate([b[:tok_ep] for b in blocks], 0)
    value_all = jnp.concatenate([b[tok_ep:] for b in blocks], 0)
    key_pos = offset - HOPS * tok_ep + jnp.arange((HOPS + 1) * tok_ep, dtype=jnp.int32)
    query_pos = offset + jnp.arange(tok_ep, dtype=jnp.int32)
    key_mask = (key_pos[None, :] <= query_pos[:, None]) & (key_pos[None, :] >= doc_start[:, None])
    query_heads = queries.reshape(tok_ep, group_size, HS)
    score_vals = jnp.einsum("igd,jd->gij", query_heads, key_all, preferred_element_type=F32) * (
        1.0 / HS**0.5
    )
    score_vals = jnp.where(key_mask[None], score_vals, -jnp.inf)
    row_peak = jnp.max(score_vals, axis=-1, keepdims=True)
    prob_vals = jnp.exp(score_vals - row_peak)
    row_total = jnp.sum(prob_vals, axis=-1, keepdims=True)
    weighted = jnp.einsum("gij,jd->igd", prob_vals.astype(BF), value_all, preferred_element_type=F32)
    return (
        (weighted / jnp.transpose(row_total, (1, 0, 2))).reshape(tok_ep, group_size * HS).astype(BF)
    )


def on_device(
    queries,
    keys,
    values,
    doc_start,
    residual,
    out_weight,
    norm_gain,
    gate_weight,
    up_weight,
    down_weight,
    route_ids,
    route_weights,
):
    nx, nz, nc, nr = (lax.axis_size(a) for a in ("x", "z", "core", "rep"))
    width = out_weight.shape[1]
    rows8 = out_weight.shape[0]
    tok_sub, top = route_ids.shape[1], route_ids.shape[2]

    out_z = lax.all_gather(out_weight, "z", axis=0, tiled=True)
    out_all = lax.all_gather(out_z, XC, axis=0, tiled=True)

    attended = attention(queries, keys, values, doc_start)
    feats = attended.shape[1]
    place = jnp.arange(feats, dtype=jnp.int32)
    px, pc, pz, pi = (
        place // (nz * nc * rows8),
        (place // (nz * rows8)) % nc,
        (place // rows8) % nz,
        place % rows8,
    )
    source = ((px * nz + pz) * nc + pc) * rows8 + pi
    permute = (place[:, None] == source[None, :]).astype(BF)
    attended = jnp.dot(attended, permute, preferred_element_type=F32).astype(BF)

    gate_weight, up_weight, down_weight, attended = lax.optimization_barrier(
        (gate_weight, up_weight, down_weight, attended)
    )
    gate_all = lax.all_gather(gate_weight[0], "rep", axis=0, tiled=True)
    up_all = lax.all_gather(up_weight[0], "rep", axis=0, tiled=True)
    down_all = lax.all_gather(down_weight[0], "rep", axis=0, tiled=True)

    partial_value = jnp.dot(attended, out_all, preferred_element_type=F32).astype(BF)
    parts = lax.all_to_all(partial_value, "rep", split_axis=0, concat_axis=0, tiled=True)
    head_total = jnp.sum(parts.reshape(nr, tok_sub, width).astype(F32), axis=0)
    hidden_sum = residual[0].astype(F32) + head_total
    inverse_rms = lax.rsqrt(jnp.mean(hidden_sum * hidden_sum, axis=-1, keepdims=True) + 1e-06)
    normed = (hidden_sum * inverse_rms * norm_gain).astype(BF)

    extra = jnp.concatenate([route_ids[0].astype(BF), route_weights[0]], 1)
    extra = jnp.pad(extra, ((0, 0), (0, 128 - 2 * top)))
    column = lax.all_gather(jnp.concatenate([normed, extra], 1), "z", axis=0, tiled=True)
    tokens = column[:, :width]
    info = jnp.transpose(column[:, width : width + 2 * top].astype(F32))
    ids, gains = info[:top].astype(jnp.int32), info[top:]
    count = tokens.shape[0]
    slots = CAP * nz
    local = nx * nc
    lane = jnp.arange(local, dtype=jnp.int32)
    experts = ((lane // nc) * nz + lax.axis_index("z")) * nc + lane % nc
    match = ids[None] == experts[:, None, None]
    hit = jnp.any(match, axis=1)
    gain = jnp.sum(jnp.where(match, gains[None], 0.0), axis=1)
    step = jnp.arange(count, dtype=jnp.int32)
    before = (step[:, None] < step[None, :]).astype(BF)
    rank = jnp.dot(hit.astype(BF), before, preferred_element_type=F32).astype(jnp.int32)
    rank = jnp.where(hit, rank, -1)
    spread = rank[:, None, :] == jnp.arange(slots, dtype=jnp.int32)[None, :, None]
    send_pick = spread.astype(BF).reshape(local * slots, count)
    back_pick = jnp.where(spread, gain[:, None, :], 0.0).astype(BF).reshape(local * slots, count)

    send_rows = jnp.dot(send_pick, tokens, preferred_element_type=F32).astype(BF)
    rows = lax.all_to_all(send_rows, XC, split_axis=0, concat_axis=0, tiled=True)
    gate_act = contract(rows, gate_all, ((1,), (1,)))
    up_act = contract(rows, up_all, ((1,), (1,)))
    hidden_act = (jax.nn.silu(gate_act) * up_act).astype(BF)
    down_parts = down_all.reshape(nr, -1, down_all.shape[1])
    expert_out = jnp.concatenate(
        [
            jnp.dot(hidden_act, down_parts[r], preferred_element_type=F32).astype(BF)
            for r in range(nr)
        ],
        1,
    )
    returned = lax.all_to_all(expert_out, XC, split_axis=0, concat_axis=0, tiled=True)
    mixed = contract(back_pick, returned, ((0,), (0,))).astype(BF)
    expert_mix = lax.psum_scatter(mixed, "z", scatter_dimension=0, tiled=True)
    return (hidden_sum + expert_mix.astype(F32)).astype(BF)[None]


def solution(mesh):
    devices = mesh.devices
    split = Mesh(devices.reshape(4, 4, devices.shape[1] // 8, 2), ("rep",) + EP)
    placed = (
        P(EP, "rep"),
        P(EP, "rep"),
        P(EP, "rep"),
        P(EP),
        P(EP, "rep", None),
        P(("rep",) + EP, None),
        P(),
        P(EP, "rep", None),
        P(EP, "rep", None),
        P(EP, None, "rep"),
        P(EP, "rep", None),
        P(EP, "rep", None),
    )
    return jax.shard_map(
        on_device, mesh=split, in_specs=placed, out_specs=P(EP, "rep", None), check_vma=False
    )
```

time: 625 us -> 435 us (0.70)
  the two profiles are of different devices: /device:TPU:1 before, /device:TPU:8 now
where the time goes in v1:
time: 435 us; the launch traced here: 434 us
  waiting for transfers between devices  321 us (74%)
  blocking collectives  40.9 us (9%)
  matrix products  24.8 us (6%)
  starting transfers between devices  23.8 us (5%)
  between operations  13.8 us (3%)
  other arithmetic  5.88 us (1%)
    reduce_scatter x1, waiting for transfers between devices, on_device(): expert_mix = lax.psum_scatter(mixed, 'z', scatter_dimension=0, tiled=True)  72.8 us
    all_gather x1, waiting for transfers between devices, on_device(): lax.all_gather(jnp.concatenate([normed, extra], 1), 'z', axis=0, tiled=True)  71 us
    all_gather x1, waiting for transfers between devices, on_device(): down_all = lax.all_gather(down_weight[0], 'rep', axis=0, tiled=True)  45.8 us
    all_gather x1, waiting for transfers between devices, on_device(): up_all = lax.all_gather(up_weight[0], 'rep', axis=0, tiled=True)  45.1 us
    all_gather x1, blocking collectives, on_device(): out_z = lax.all_gather(out_weight, 'z', axis=0, tiled=True)  40.9 us
    all_gather x1, waiting for transfers between devices, on_device(): gate_all = lax.all_gather(gate_weight[0], 'rep', axis=0, tiled=True)  35.8 us
    all_to_all x1, waiting for transfers between devices, on_device(): lax.all_to_all(expert_out, XC, split_axis=0, concat_axis=0, tiled=True)  21.4 us
    all_gather x1, waiting for transfers between devices, on_device(): out_all = lax.all_gather(out_z, XC, axis=0, tiled=True)  19.4 us
  transfers between devices with their start and end apart: 13, of which 8 were waited for; matrix products, arithmetic and copies ran while one was open for 5% of the time, Pallas kernels for 0%

profile of v1, /device:TPU:8, one launch (start us, length us, event | category | flops | bytes accessed | tf_op | source)
XLA Modules:
  0.0 434.2 jit_solution(9876310331227653638)
XLA Ops:
  6.5 40.9 %all_gather.18 = bf16[128,2048]{1,0:T(8,128)(2,1)} all-gather(bf16[8,2048]{1,0:T(8,128)(2,1)} %param.17), channel_id=1, replica_groups=mesh['rep'=4,'x'=4,'z'=16,'core'=2] {'z'}, dimensions={0}, use_global_device_ids=true | all-gather | bytes 557056 | tf_op jit(solution)/shard_map/all_gather | solution.py:68
  47.5 0.8 constant_dynamic-update-slice_fusion.1
  48.2 0.8 constant_dynamic-update-slice_fusion
  49.0 2.1 collective-permute-start
  51.2 1.3 collective-permute-start.1
  52.5 1.9 collective-permute-start.2
  54.4 5.0 %collective-permute-start.3 = (bf16[256,128]{1,0:T(8,128)(2,1)S(1)}, bf16[256,128]{1,0:T(8,128)(2,1)S(1)}, u32[]{:S(2)}, u32[]{:S(2)}) collective-permute-start(bf16[256,128]{1,0:T(8,128)(2,1)S(1)} %constant_dynamic-update-slice_fusion), channel_id=1, source_target_pairs={{0,1},{1,2},{2,3},{3,4},{4,5},{5,6},{6,7},{7,8},{8,9},{9,10},{10,1... | collective-permute-start | bytes 196616 | tf_op jit(solution)/shard_map/ppermute | solution.py:17
  59.4 0.8 compare_and_fusion
  60.4 0.8 constant_dynamic-update-slice_fusion.2
  62.3 0.8 fusion.26
  63.0 0.9 fusion.22
  64.0 19.4 %all-gather.9.cloned.1.call-done = bf16[1024,2048]{1,0:T(8,128)(2,1)} async-done(((bf16[128,2048]{1,0:T(8,128)(2,1)}), bf16[1024,2048]{1,0:T(8,128)(2,1)}) %all-gather.9.cloned.1.call-update) | async-done | bytes 4194320 | tf_op jit(solution)/shard_map/all_gather | solution.py:69
  83.4 3.7 convolution_convert_fusion.1
  87.2 4.8 %all-to-all-start = ((bf16[4,32,2048]{2,1,0:T(8,128)(2,1)}), bf16[4,32,2048]{2,1,0:T(8,128)(2,1)S(1)}, u32[]{:S(2)}, u32[]{:S(2)}) async-start(bf16[4,32,2048]{2,1,0:T(8,128)(2,1)} %bitcast.9), calls=%async_computation | async-start | bytes 1048576 | tf_op jit(solution)/shard_map/all_to_all | solution.py:92
  92.2 8.2 %all-to-all-done = bf16[4,32,2048]{2,1,0:T(8,128)(2,1)S(1)} async-done(((bf16[4,32,2048]{2,1,0:T(8,128)(2,1)}), bf16[4,32,2048]{2,1,0:T(8,128)(2,1)S(1)}, u32[]{:S(2)}, u32[]{:S(2)}) %all-to-all-start) | async-done | bytes 524320 | tf_op jit(solution)/shard_map/all_to_all | solution.py:92
  103.5 71.0 %all-gather.11.cloned.1.call-done = bf16[512,2176]{1,0:T(8,128)(2,1)} async-done(((bf16[32,2176]{1,0:T(8,128)(2,1)}), bf16[512,2176]{1,0:T(8,128)(2,1)}) %all-gather.11.cloned.1.call-update) | async-done | bytes 2228240 | tf_op jit(solution)/shard_map/all_gather | solution.py:100
  174.5 0.9 slice.80
  176.0 3.8 convolution_convert_fusion
  179.8 4.3 all-to-all-start.1
  184.1 35.8 %all-gather.13.cloned.1.call-done = bf16[1,768,2048]{2,1,0:T(8,128)(2,1)} async-done(((bf16[1,192,2048]{2,1,0:T(8,128)(2,1)}), bf16[1,768,2048]{2,1,0:T(8,128)(2,1)}) %all-gather.13.cloned.1.call-update) | async-done | bytes 3145744 | tf_op jit(solution)/shard_map/all_gather | solution.py:87
  219.9 4.4 %fusion.3 = f32[384,768]{1,0:T(8,128)} fusion(bf16[384,2048]{1,0:T(8,128)(2,1)S(1)} %bitcast.103, bf16[1,768,2048]{2,1,0:T(8,128)(2,1)} %all-gather.13.cloned.1.call-done), kind=kOutput, calls=%fused_computation.5 | convolution fusion | flops 1207959552 | bytes 5898240 | tf_op jit(solution)/shard_map/dot_general | solution.py:21
  224.2 45.1 %all-gather.15.cloned.1.call-done = bf16[1,768,2048]{2,1,0:T(8,128)(2,1)} async-done(((bf16[1,192,2048]{2,1,0:T(8,128)(2,1)}), bf16[1,768,2048]{2,1,0:T(8,128)(2,1)}) %all-gather.15.cloned.1.call-update) | async-done | bytes 3145744 | tf_op jit(solution)/shard_map/all_gather | solution.py:88
  269.3 3.7 fusion.13
  273.0 45.8 %all-gather.17.cloned.1.call-done = bf16[1,3072,512]{2,1,0:T(8,128)(2,1)} async-done(((bf16[1,768,512]{2,1,0:T(8,128)(2,1)}), bf16[1,3072,512]{2,1,0:T(8,128)(2,1)}) %all-gather.17.cloned.1.call-update) | async-done | bytes 3145744 | tf_op jit(solution)/shard_map/all_gather | solution.py:89
  318.8 1.7 convolution_convert_fusion.5
  320.6 1.6 convolution_convert_fusion.4
  323.1 1.4 pad_maximum_fusion
  324.5 4.3 all-to-all-start.2
  328.9 21.4 %all-to-all-done.2 = bf16[8,48,2048]{2,1,0:T(8,128)(2,1)S(1)} async-done(((bf16[8,48,2048]{2,1,0:T(8,128)(2,1)}), bf16[8,48,2048]{2,1,0:T(8,128)(2,1)S(1)}, u32[]{:S(2)}, u32[]{:S(2)}) %all-to-all-start.2) | async-done | bytes 1572896 | tf_op jit(solution)/shard_map/all_to_all | solution.py:133
  350.3 2.6 bitcast_convert_fusion
  353.0 72.8 %reduce-scatter.4.cloned.1.call-done = bf16[32,2048]{1,0:T(8,128)(2,1)} async-done(((bf16[512,2048]{1,0:T(8,128)(2,1)}), bf16[32,2048]{1,0:T(8,128)(2,1)}) %reduce-scatter.4.cloned.1.call-update) | async-done | bytes 131088 | tf_op jit(solution)/shard_map/reduce_scatter | solution.py:135
  425.8 1.6 fusion.39
  (59 shorter events, 6.1 us)
Async XLA Ops:
  6.5 54.6 %copy-start = (bf16[128,1024]{1,0:T(8,128)(2,1)S(1)}, bf16[128,1024]{1,0:T(8,128)(2,1)}, u32[]{:S(2)}) copy-start(bf16[128,1024]{1,0:T(8,128)(2,1)} %param.12) | copy-start | bytes 786436
  6.5 76.9 %all-gather.9.cloned.1.call-start = ((), (), s32[]{:S(2)}) async-start(), calls=%async_computation.4 | async-start | bytes 4718592 | tf_op jit(solution)/shard_map/all_gather | solution.py:69
  49.0 11.2 %collective-permute-start = (bf16[256,128]{1,0:T(8,128)(2,1)S(1)}, bf16[256,128]{1,0:T(8,128)(2,1)S(1)}, u32[]{:S(2)}, u32[]{:S(2)}) collective-permute-start(bf16[256,128]{1,0:T(8,128)(2,1)S(1)} %constant_dynamic-update-slice_fusion), channel_id=1, source_target_pairs={{0,4},{1,5},{2,6},{3,7},{4,8},{5,9},{6,10},{7,11},{8,12},{9,13},{1... | collective-permute-start | bytes 196616 | tf_op jit(solution)/shard_map/ppermute | solution.py:17
  51.2 9.1 %collective-permute-start.1 = (bf16[256,128]{1,0:T(8,128)(2,1)S(1)}, bf16[256,128]{1,0:T(8,128)(2,1)S(1)}, u32[]{:S(2)}, u32[]{:S(2)}) collective-permute-start(bf16[256,128]{1,0:T(8,128)(2,1)S(1)} %constant_dynamic-update-slice_fusion), channel_id=1, source_target_pairs={{0,3},{1,4},{2,5},{3,6},{4,7},{5,8},{6,9},{7,10},{8,11},{9,12},{10... | collective-permute-start | bytes 196616 | tf_op jit(solution)/shard_map/ppermute | solution.py:17
  52.5 7.8 %collective-permute-start.2 = (bf16[256,128]{1,0:T(8,128)(2,1)S(1)}, bf16[256,128]{1,0:T(8,128)(2,1)S(1)}, u32[]{:S(2)}, u32[]{:S(2)}) collective-permute-start(bf16[256,128]{1,0:T(8,128)(2,1)S(1)} %constant_dynamic-update-slice_fusion), channel_id=1, source_target_pairs={{0,2},{1,3},{2,4},{3,5},{4,6},{5,7},{6,8},{7,9},{8,10},{9,11},{10,... | collective-permute-start | bytes 196616 | tf_op jit(solution)/shard_map/ppermute | solution.py:17
  54.4 6.0 %collective-permute-start.3 = (bf16[256,128]{1,0:T(8,128)(2,1)S(1)}, bf16[256,128]{1,0:T(8,128)(2,1)S(1)}, u32[]{:S(2)}, u32[]{:S(2)}) collective-permute-start(bf16[256,128]{1,0:T(8,128)(2,1)S(1)} %constant_dynamic-update-slice_fusion), channel_id=1, source_target_pairs={{0,1},{1,2},{2,3},{3,4},{4,5},{5,6},{6,7},{7,8},{8,9},{9,10},{10,1... | collective-permute-start | bytes 196616 | tf_op jit(solution)/shard_map/ppermute | solution.py:17
  64.0 28.0 %copy-start.3 = (s32[1,32,8]{1,2,0:T(8,128)S(1)}, s32[1,32,8]{1,2,0:T(8,128)}, u32[]{:S(2)}) copy-start(s32[1,32,8]{1,2,0:T(8,128)} %param.22) | copy-start | bytes 3076
  64.0 28.1 %copy-start.4 = (bf16[1,32,8]{1,2,0:T(8,128)(2,1)S(1)}, bf16[1,32,8]{1,2,0:T(8,128)(2,1)}, u32[]{:S(2)}) copy-start(bf16[1,32,8]{1,2,0:T(8,128)(2,1)} %param.23) | copy-start | bytes 1540
  64.0 36.5 %copy-start.1 = (bf16[1,32,2048]{2,1,0:T(8,128)(2,1)S(1)}, bf16[1,32,2048]{2,1,0:T(8,128)(2,1)}, u32[]{:S(2)}) copy-start(bf16[1,32,2048]{2,1,0:T(8,128)(2,1)} %param.16) | copy-start | bytes 393220
  64.0 36.7 %copy-start.2 = (f32[2048]{0:T(1024)S(1)}, f32[2048]{0:T(1024)}, u32[]{:S(2)}) copy-start(f32[2048]{0:T(1024)} %param.18) | copy-start | bytes 24580
  87.2 13.3 %all-to-all-start = ((bf16[4,32,2048]{2,1,0:T(8,128)(2,1)}), bf16[4,32,2048]{2,1,0:T(8,128)(2,1)S(1)}, u32[]{:S(2)}, u32[]{:S(2)}) async-start(bf16[4,32,2048]{2,1,0:T(8,128)(2,1)} %bitcast.9), calls=%async_computation | async-start | bytes 1048576 | tf_op jit(solution)/shard_map/all_to_all | solution.py:92
  92.0 82.5 %all-gather.11.cloned.1.call-start = ((), (), s32[]{:S(2)}) async-start(), calls=%async_computation.5 | async-start | bytes 2367488 | tf_op jit(solution)/shard_map/all_gather | solution.py:100
  101.5 118.4 %all-gather.13.cloned.1.call-start = ((), (), s32[]{:S(2)}) async-start(), calls=%async_computation.6 | async-start | bytes 3932160 | tf_op jit(solution)/shard_map/all_gather | solution.py:87
  102.2 167.1 %all-gather.15.cloned.1.call-start = ((), (), s32[]{:S(2)}) async-start(), calls=%async_computation.7 | async-start | bytes 3932160 | tf_op jit(solution)/shard_map/all_gather | solution.py:88
  102.8 216.0 %all-gather.17.cloned.1.call-start = ((), (), s32[]{:S(2)}) async-start(), calls=%async_computation.8 | async-start | bytes 3932160 | tf_op jit(solution)/shard_map/all_gather | solution.py:89
  179.8 40.0 %all-to-all-start.1 = ((bf16[8,48,2048]{2,1,0:T(8,128)(2,1)}), bf16[8,48,2048]{2,1,0:T(8,128)(2,1)S(1)}, u32[]{:S(2)}, u32[]{:S(2)}) async-start(bf16[8,48,2048]{2,1,0:T(8,128)(2,1)} %bitcast.105), calls=%async_computation.1 | async-start | bytes 3145728 | tf_op jit(solution)/shard_map/all_to_all | solution.py:121
  318.8 3.4 copy-start.5
  324.5 25.8 %all-to-all-start.2 = ((bf16[8,48,2048]{2,1,0:T(8,128)(2,1)}), bf16[8,48,2048]{2,1,0:T(8,128)(2,1)S(1)}, u32[]{:S(2)}, u32[]{:S(2)}) async-start(bf16[8,48,2048]{2,1,0:T(8,128)(2,1)} %bitcast.22), calls=%async_computation.2 | async-start | bytes 3145728 | tf_op jit(solution)/shard_map/all_to_all | solution.py:133
  328.7 97.0 %reduce-scatter.4.cloned.1.call-start = ((), (), s32[]{:S(2)}) async-start(), calls=%async_computation.9 | async-start | bytes 2228224 | tf_op jit(solution)/shard_map/reduce_scatter | solution.py:135
Sparse Core Ops, SparseCore 0:
  47.6 35.7 all-gather.8
  101.6 72.8 all-gather.10
  176.6 43.2 all-gather.12
  221.8 47.4 all-gather.14
  271.3 47.4 all-gather.16
  353.1 72.6 reduce-scatter.3

commit v2 on v1

v2 whole, which is shorter than its diff:
```python
import jax
import jax.numpy as jnp
from jax import lax
from jax.sharding import Mesh, PartitionSpec as P

HS = 128
HOPS = 4
CAP = 3
BF = jnp.bfloat16
F32 = jnp.float32
EP = ("x", "z", "core")
XC = ("x", "core")


def from_earlier(value, by):
    devices = lax.axis_size(EP)
    return lax.ppermute(value, EP, [(i, i + by) for i in range(devices - by)])


def shift(value, axis, by):
    devices = lax.axis_size(axis)
    return lax.ppermute(value, axis, [(i, (i + by) % devices) for i in range(devices)])


def other_core(value):
    return shift(value, "core", 1)


def contract(left, right, dims):
    return lax.dot_general(left, right, (dims, ((), ())), preferred_element_type=F32)


def gather_x(value):
    half = value.shape[0] // 2
    from_left, from_right = shift(value, "x", 1), shift(value, "x", -1)
    far_low, far_high = shift(from_left[:half], "x", 1), shift(from_right[half:], "x", -1)
    return jnp.concatenate([value, from_left, from_right, far_low, far_high], 0)


def ring_blocks(value, axis):
    devices = lax.axis_size(axis)
    blocks = {0: value}
    right = left = value
    for step in range(1, devices // 2 + 1):
        right = shift(right, axis, 1)
        blocks[devices - step] = right
        if step < devices - step:
            left = shift(left, axis, -1)
            blocks[step] = left
    return blocks


def attention(queries, keys, values, doc_start):
    tok_ep = queries.shape[0]
    group_size = queries.shape[1] // HS
    offset = lax.axis_index(EP) * tok_ep
    own = jnp.concatenate([keys, values], 0)
    blocks = [from_earlier(own, by) for by in range(HOPS, 0, -1)] + [own]
    key_all = jnp.concatenate([b[:tok_ep] for b in blocks], 0)
    value_all = jnp.concatenate([b[tok_ep:] for b in blocks], 0)
    key_pos = offset - HOPS * tok_ep + jnp.arange((HOPS + 1) * tok_ep, dtype=jnp.int32)
    query_pos = offset + jnp.arange(tok_ep, dtype=jnp.int32)
    key_mask = (key_pos[None, :] <= query_pos[:, None]) & (key_pos[None, :] >= doc_start[:, None])
    query_heads = queries.reshape(tok_ep, group_size, HS)
    score_vals = jnp.einsum("igd,jd->gij", query_heads, key_all, preferred_element_type=F32) * (
        1.0 / HS**0.5
    )
    score_vals = jnp.where(key_mask[None], score_vals, -jnp.inf)
    row_peak = jnp.max(score_vals, axis=-1, keepdims=True)
    prob_vals = jnp.exp(score_vals - row_peak)
    row_total = jnp.sum(prob_vals, axis=-1, keepdims=True)
    weighted = jnp.einsum("gij,jd->igd", prob_vals.astype(BF), value_all, preferred_element_type=F32)
    return (
        (weighted / jnp.transpose(row_total, (1, 0, 2))).reshape(tok_ep, group_size * HS).astype(BF)
    )


def picks(ids, gains, experts, slots):
    count = ids.shape[1]
    match = ids[None] == experts[:, None, None]
    hit = jnp.any(match, axis=1)
    gain = jnp.sum(jnp.where(match, gains[None], 0.0), axis=1)
    step = jnp.arange(count, dtype=jnp.int32)
    before = (step[:, None] < step[None, :]).astype(BF)
    rank = jnp.dot(hit.astype(BF), before, preferred_element_type=F32).astype(jnp.int32)
    rank = jnp.where(hit, rank, -1)
    spread = rank[:, None, :] == jnp.arange(slots, dtype=jnp.int32)[None, :, None]
    send = spread.astype(BF).reshape(-1, count)
    back = jnp.where(spread, gain[:, None, :], 0.0).astype(BF).reshape(-1, count)
    return send, back


def on_device(
    queries,
    keys,
    values,
    doc_start,
    residual,
    out_weight,
    norm_gain,
    gate_weight,
    up_weight,
    down_weight,
    route_ids,
    route_weights,
):
    nx, nz, nc, nr = (lax.axis_size(a) for a in ("x", "z", "core", "rep"))
    width = out_weight.shape[1]
    rows8 = out_weight.shape[0]
    tok_sub, top = route_ids.shape[1], route_ids.shape[2]
    here = lax.axis_index("z")

    gate_all = lax.all_gather(gate_weight[0], "rep", axis=0, tiled=True)
    up_all = lax.all_gather(up_weight[0], "rep", axis=0, tiled=True)
    down_all = lax.all_gather(down_weight[0], "rep", axis=0, tiled=True)

    info = jnp.concatenate([route_ids[0].astype(BF), route_weights[0]], 1)
    info = jnp.transpose(info).reshape(rows8, -1)
    info_width = info.shape[1]
    info = jnp.pad(info, ((0, 0), (0, -info_width % 128)))
    z_all = lax.all_gather(jnp.concatenate([out_weight, info], 1), "z", axis=0, tiled=True)
    z_rows = z_all[:, :width]
    z_rows, keys, values = lax.optimization_barrier((z_rows, keys, values))
    out_own = gather_x(z_rows)
    out_other = other_core(out_own)

    attended = attention(queries, keys, values, doc_start)
    feats = attended.shape[1]
    place = jnp.arange(feats, dtype=jnp.int32)
    block = nz * rows8
    hop = (place // block) % nx
    pc = place // (block * nx)
    pc = jnp.where(lax.axis_index("core") == 0, pc, nc - 1 - pc)
    px = (lax.axis_index("x") + nx + jnp.where(hop == 1, -1, jnp.where(hop == 2, 1, hop // 3 * 2))) % nx
    pz, pi = (place // rows8) % nz, place % rows8
    source = ((px * nz + pz) * nc + pc) * rows8 + pi
    permute = (place[:, None] == source[None, :]).astype(BF)
    attended = jnp.dot(attended, permute, preferred_element_type=F32).astype(BF)

    half = feats // 2
    partial_value = jnp.dot(attended[:, :half], out_own, preferred_element_type=F32)
    partial_value += jnp.dot(attended[:, half:], out_other, preferred_element_type=F32)
    partial_value = partial_value.astype(BF)
    parts = lax.all_to_all(partial_value, "rep", split_axis=0, concat_axis=0, tiled=True)
    head_total = jnp.sum(parts.reshape(nr, tok_sub, width).astype(F32), axis=0)
    hidden_sum = residual[0].astype(F32) + head_total
    inverse_rms = lax.rsqrt(jnp.mean(hidden_sum * hidden_sum, axis=-1, keepdims=True) + 1e-06)
    normed = (hidden_sum * inverse_rms * norm_gain).astype(BF)

    table = z_all[:, width : width + info_width].reshape(nz, 2 * top, tok_sub)
    table = lax.dynamic_slice_in_dim(jnp.concatenate([table, table], 0), here, nz, 0)
    table = jnp.transpose(table.astype(F32), (1, 0, 2))
    lane = jnp.arange(nx * nc, dtype=jnp.int32)
    experts = ((lane // nc) * nz + here) * nc + lane % nc
    near, quarter = [], nz // 4
    near = list(range(quarter)) + list(range(nz - quarter, nz))
    far = list(range(quarter, nz - quarter))
    groups = []
    for members in (near, far):
        part = jnp.concatenate([table[:, m] for m in members], 1)
        send, back = picks(part[:top].astype(jnp.int32), part[top:], experts, CAP * len(members))
        block_at = (here + jnp.array(members, jnp.int32)) % nz
        token_at = (block_at[:, None] * tok_sub + jnp.arange(tok_sub, dtype=jnp.int32)).reshape(-1)
        all_at = jnp.arange(nz * tok_sub, dtype=jnp.int32)
        reorder = (token_at[:, None] == all_at[None, :]).astype(BF)
        back = jnp.dot(back, reorder, preferred_element_type=F32).astype(BF)
        groups.append((members, send, back))

    blocks = ring_blocks(normed, "z")
    down_parts = down_all.reshape(nr, -1, down_all.shape[1])
    backs, returned = [], []
    for members, send, back in groups:
        tokens = jnp.concatenate([blocks[m] for m in members], 0)
        send_rows = jnp.dot(send, tokens, preferred_element_type=F32).astype(BF)
        rows = lax.all_to_all(send_rows, XC, split_axis=0, concat_axis=0, tiled=True)
        gate_act = contract(rows, gate_all, ((1,), (1,)))
        up_act = contract(rows, up_all, ((1,), (1,)))
        hidden_act = (jax.nn.silu(gate_act) * up_act).astype(BF)
        expert_out = jnp.concatenate(
            [
                jnp.dot(hidden_act, down_parts[r], preferred_element_type=F32).astype(BF)
                for r in range(nr)
            ],
            1,
        )
        returned.append(lax.all_to_all(expert_out, XC, split_axis=0, concat_axis=0, tiled=True))
        backs.append(back)
    mixed = contract(jnp.concatenate(backs, 0), jnp.concatenate(returned, 0), ((0,), (0,))).astype(BF)
    expert_mix = lax.psum_scatter(mixed, "z", scatter_dimension=0, tiled=True)
    return (hidden_sum + expert_mix.astype(F32)).astype(BF)[None]


def solution(mesh):
    devices = mesh.devices
    split = Mesh(devices.reshape(4, 4, devices.shape[1] // 8, 2), ("rep",) + EP)
    placed = (
        P(EP, "rep"),
        P(EP, "rep"),
        P(EP, "rep"),
        P(EP),
        P(EP, "rep", None),
        P(("rep",) + EP, None),
        P(),
        P(EP, "rep", None),
        P(EP, "rep", None),
        P(EP, None, "rep"),
        P(EP, "rep", None),
        P(EP, "rep", None),
    )
    return jax.shard_map(
        on_device, mesh=split, in_specs=placed, out_specs=P(EP, "rep", None), check_vma=False
    )
```

time: 435 us -> 330 us (0.76)
  the two profiles are of different devices: /device:TPU:8 before, /device:TPU:4 now
where the time goes in v2:
time: 330 us; the launch traced here: 329 us
  waiting for transfers between devices  135 us (41%)
  starting transfers between devices  99.9 us (30%)
  blocking collectives  39 us (12%)
  matrix products  29.8 us (9%)
  between operations  14.1 us (4%)
  other arithmetic  9.29 us (3%)
    reduce_scatter x1, waiting for transfers between devices, on_device(): expert_mix = lax.psum_scatter(mixed, 'z', scatter_dimension=0, tiled=True)  65.4 us
    ppermute x20, starting transfers between devices, shift(): lax.ppermute(value, axis, [(i, (i + by) % devices) for i in range(devices)])  64.9 us
    ppermute x20, waiting for transfers between devices, shift(): lax.ppermute(value, axis, [(i, (i + by) % devices) for i in range(devices)])  39.3 us
    all_gather x1, blocking collectives, on_device(): lax.all_gather(jnp.concatenate([out_weight, info], 1), 'z', axis=0, tiled...  39 us
    dot_general x5, matrix products, contract(): lax.dot_general(left, right, (dims, ((), ())), preferred_element_type=F32)  14.9 us
    all_to_all x1, waiting for transfers between devices, on_device(): lax.all_to_all(partial_value, 'rep', split_axis=0, concat_axis=0, tiled=T...  14.6 us
    all_to_all x2, waiting for transfers between devices, on_device(): lax.all_to_all(expert_out, XC, split_axis=0, concat_axis=0, tiled=True)  11.5 us
    all_to_all x2, starting transfers between devices, on_device(): lax.all_to_all(expert_out, XC, split_axis=0, concat_axis=0, tiled=True)  11.4 us
  transfers between devices with their start and end apart: 33, of which 16 were waited for; matrix products, arithmetic and copies ran while one was open for 11% of the time, Pallas kernels for 0%

profile of v2, /device:TPU:4, one launch (start us, length us, event | category | flops | bytes accessed | tf_op | source)
XLA Modules:
  0.0 329.0 jit_solution(10488322294574833191)
XLA Ops:
  10.3 39.0 %all_gather.12 = bf16[128,2176]{1,0:T(8,128)(2,1)S(1)} all-gather(bf16[8,2176]{1,0:T(8,128)(2,1)S(1)} %fusion.64), channel_id=1, replica_groups=mesh['rep'=4,'x'=4,'z'=16,'core'=2] {'z'}, dimensions={0}, use_global_device_ids=true | all-gather | bytes 591872 | tf_op jit(solution)/shard_map/all_gather | solution.py:121
  55.3 3.1 collective-permute-start.4
  58.4 2.7 collective-permute-start.5
  62.8 10.7 %collective-permute-done.4 = bf16[128,2048]{1,0:T(8,128)(2,1)S(1)} collective-permute-done((bf16[128,2048]{1,0:T(8,128)(2,1)S(1)}, bf16[128,2048]{1,0:T(8,128)(2,1)S(1)}, u32[]{:S(2)}, u32[]{:S(2)}) %collective-permute-start.4) | collective-permute-done | bytes 524320 | tf_op jit(solution)/shard_map/ppermute | solution.py:22
  73.5 3.1 collective-permute-start.6
  76.7 2.7 collective-permute-start.7
  79.5 4.4 %collective-permute-done.6 = bf16[64,2048]{1,0:T(8,128)(2,1)S(1)} collective-permute-done((bf16[64,2048]{1,0:T(8,128)(2,1)S(1)}, bf16[64,2048]{1,0:T(8,128)(2,1)S(1)}, u32[]{:S(2)}, u32[]{:S(2)}) %collective-permute-start.6) | collective-permute-done | bytes 262176 | tf_op jit(solution)/shard_map/ppermute | solution.py:22
  88.6 2.9 collective-permute-done.3
  96.2 4.6 %all-to-all-start = ((bf16[4,32,2048]{2,1,0:T(8,128)(2,1)}), bf16[4,32,2048]{2,1,0:T(8,128)(2,1)S(1)}, u32[]{:S(2)}, u32[]{:S(2)}) async-start(bf16[4,32,2048]{2,1,0:T(8,128)(2,1)} %bitcast.12), calls=%async_computation | async-start | bytes 1048576 | tf_op jit(solution)/shard_map/all_to_all | solution.py:144
  101.7 14.6 %all-to-all-done = bf16[4,32,2048]{2,1,0:T(8,128)(2,1)S(1)} async-done(((bf16[4,32,2048]{2,1,0:T(8,128)(2,1)}), bf16[4,32,2048]{2,1,0:T(8,128)(2,1)S(1)}, u32[]{:S(2)}, u32[]{:S(2)}) %all-to-all-start) | async-done | bytes 524320 | tf_op jit(solution)/shard_map/all_to_all | solution.py:144
  117.1 3.9 %collective-permute-start.9 = (bf16[32,2048]{1,0:T(8,128)(2,1)S(1)}, bf16[32,2048]{1,0:T(8,128)(2,1)S(1)}, u32[]{:S(2)}, u32[]{:S(2)}) collective-permute-start(bf16[32,2048]{1,0:T(8,128)(2,1)S(1)} %get-tuple-element.16), channel_id=1, source_target_pairs={{0,30},{2,0},{4,2},{6,4},{8,6},{10,8},{12,10},{14,12},{16,14},{18,... | collective-permute-start | bytes 393224 | tf_op jit(solution)/shard_map/ppermute | solution.py:22
  124.0 5.1 %collective-permute-start.10 = (bf16[32,2048]{1,0:T(8,128)(2,1)S(1)}, bf16[32,2048]{1,0:T(8,128)(2,1)S(1)}, u32[]{:S(2)}, u32[]{:S(2)}) collective-permute-start(bf16[32,2048]{1,0:T(8,128)(2,1)S(1)} %collective-permute-done.9), channel_id=1, source_target_pairs={{0,30},{2,0},{4,2},{6,4},{8,6},{10,8},{12,10},{14,12},{16,14},{18,... | collective-permute-start | bytes 393224 | tf_op jit(solution)/shard_map/ppermute | solution.py:22
  131.6 5.6 %collective-permute-start.11 = (bf16[32,2048]{1,0:T(8,128)(2,1)S(1)}, bf16[32,2048]{1,0:T(8,128)(2,1)S(1)}, u32[]{:S(2)}, u32[]{:S(2)}) collective-permute-start(bf16[32,2048]{1,0:T(8,128)(2,1)S(1)} %collective-permute-done.10), channel_id=1, source_target_pairs={{0,30},{2,0},{4,2},{6,4},{8,6},{10,8},{12,10},{14,12},{16,14},{18,... | collective-permute-start | bytes 393224 | tf_op jit(solution)/shard_map/ppermute | solution.py:22
  139.1 6.1 %collective-permute-done.14 = bf16[32,2048]{1,0:T(8,128)(2,1)S(1)} collective-permute-done((bf16[32,2048]{1,0:T(8,128)(2,1)S(1)}, bf16[32,2048]{1,0:T(8,128)(2,1)S(1)}, u32[]{:S(2)}, u32[]{:S(2)}) %collective-permute-start.14) | collective-permute-done | bytes 131104 | tf_op jit(solution)/shard_map/ppermute | solution.py:22
  147.2 5.1 %collective-permute-start.16 = (bf16[32,2048]{1,0:T(8,128)(2,1)S(1)}, bf16[32,2048]{1,0:T(8,128)(2,1)S(1)}, u32[]{:S(2)}, u32[]{:S(2)}) collective-permute-start(bf16[32,2048]{1,0:T(8,128)(2,1)S(1)} %collective-permute-done.11), channel_id=1, source_target_pairs={{0,30},{2,0},{4,2},{6,4},{8,6},{10,8},{12,10},{14,12},{16,14},{18,... | collective-permute-start | bytes 393224 | tf_op jit(solution)/shard_map/ppermute | solution.py:22
  154.6 6.3 %all-to-all-start.1 = ((bf16[8,24,2048]{2,1,0:T(8,128)(2,1)}), bf16[8,24,2048]{2,1,0:T(8,128)(2,1)S(1)}, u32[]{:S(2)}, u32[]{:S(2)}) async-start(bf16[8,24,2048]{2,1,0:T(8,128)(2,1)} %bitcast.34), calls=%async_computation.1 | async-start | bytes 1572864 | tf_op jit(solution)/shard_map/all_to_all | solution.py:175
  162.8 5.1 %collective-permute-start.17 = (bf16[32,2048]{1,0:T(8,128)(2,1)S(1)}, bf16[32,2048]{1,0:T(8,128)(2,1)S(1)}, u32[]{:S(2)}, u32[]{:S(2)}) collective-permute-start(bf16[32,2048]{1,0:T(8,128)(2,1)S(1)} %collective-permute-done.16), channel_id=1, source_target_pairs={{0,30},{2,0},{4,2},{6,4},{8,6},{10,8},{12,10},{14,12},{16,14},{18,... | collective-permute-start | bytes 393224 | tf_op jit(solution)/shard_map/ppermute | solution.py:22
  168.0 2.7 collective-permute-done.17
  170.8 5.6 %collective-permute-start.18 = (bf16[32,2048]{1,0:T(8,128)(2,1)S(1)}, bf16[32,2048]{1,0:T(8,128)(2,1)S(1)}, u32[]{:S(2)}, u32[]{:S(2)}) collective-permute-start(bf16[32,2048]{1,0:T(8,128)(2,1)S(1)} %collective-permute-done.17), channel_id=1, source_target_pairs={{0,30},{2,0},{4,2},{6,4},{8,6},{10,8},{12,10},{14,12},{16,14},{18,... | collective-permute-start | bytes 393224 | tf_op jit(solution)/shard_map/ppermute | solution.py:22
  178.9 5.6 %collective-permute-start.19 = (bf16[32,2048]{1,0:T(8,128)(2,1)S(1)}, bf16[32,2048]{1,0:T(8,128)(2,1)S(1)}, u32[]{:S(2)}, u32[]{:S(2)}) collective-permute-start(bf16[32,2048]{1,0:T(8,128)(2,1)S(1)} %collective-permute-done.18), channel_id=1, source_target_pairs={{0,30},{2,0},{4,2},{6,4},{8,6},{10,8},{12,10},{14,12},{16,14},{18,... | collective-permute-start | bytes 393224 | tf_op jit(solution)/shard_map/ppermute | solution.py:22
  186.4 6.1 %collective-permute-done.22 = bf16[32,2048]{1,0:T(8,128)(2,1)S(1)} collective-permute-done((bf16[32,2048]{1,0:T(8,128)(2,1)S(1)}, bf16[32,2048]{1,0:T(8,128)(2,1)S(1)}, u32[]{:S(2)}, u32[]{:S(2)}) %collective-permute-start.22) | collective-permute-done | bytes 131104 | tf_op jit(solution)/shard_map/ppermute | solution.py:22
  194.4 6.1 %collective-permute-done.23 = bf16[32,2048]{1,0:T(8,128)(2,1)S(1)} collective-permute-done((bf16[32,2048]{1,0:T(8,128)(2,1)S(1)}, bf16[32,2048]{1,0:T(8,128)(2,1)S(1)}, u32[]{:S(2)}, u32[]{:S(2)}) %collective-permute-start.23) | collective-permute-done | bytes 131104 | tf_op jit(solution)/shard_map/ppermute | solution.py:22
  201.9 4.8 %all-to-all-start.3 = ((bf16[8,24,2048]{2,1,0:T(8,128)(2,1)}), bf16[8,24,2048]{2,1,0:T(8,128)(2,1)}, u32[]{:S(2)}, u32[]{:S(2)}) async-start(bf16[8,24,2048]{2,1,0:T(8,128)(2,1)} %bitcast.44), calls=%async_computation.3 | async-start | bytes 1572864 | tf_op jit(solution)/shard_map/all_to_all | solution.py:175
  206.7 3.1 fusion.7
  209.8 3.1 fusion.32
  220.1 4.8 %all-to-all-start.2 = ((bf16[8,24,2048]{2,1,0:T(8,128)(2,1)}), bf16[8,24,2048]{2,1,0:T(8,128)(2,1)}, u32[]{:S(2)}, u32[]{:S(2)}) async-start(bf16[8,24,2048]{2,1,0:T(8,128)(2,1)} %bitcast.177), calls=%async_computation.2 | async-start | bytes 1572864 | tf_op jit(solution)/shard_map/all_to_all | solution.py:186
  227.4 2.5 fusion.29
  232.4 2.7 all-to-all-done.2
  235.0 6.6 %all-to-all-start.4 = ((bf16[8,24,2048]{2,1,0:T(8,128)(2,1)}), bf16[8,24,2048]{2,1,0:T(8,128)(2,1)S(1)}, u32[]{:S(2)}, u32[]{:S(2)}) async-start(bf16[8,24,2048]{2,1,0:T(8,128)(2,1)} %bitcast.46), calls=%async_computation.4 | async-start | bytes 1572864 | tf_op jit(solution)/shard_map/all_to_all | solution.py:186
  242.8 8.8 %all-to-all-done.4 = bf16[8,24,2048]{2,1,0:T(8,128)(2,1)S(1)} async-done(((bf16[8,24,2048]{2,1,0:T(8,128)(2,1)}), bf16[8,24,2048]{2,1,0:T(8,128)(2,1)S(1)}, u32[]{:S(2)}, u32[]{:S(2)}) %all-to-all-start.4) | async-done | bytes 786464 | tf_op jit(solution)/shard_map/all_to_all | solution.py:186
  251.6 3.8 %convolution_convert_fusion = bf16[512,2048]{1,0:T(8,128)(2,1)} fusion(bf16[192,2048]{1,0:T(8,128)(2,1)S(1)} %bitcast.180, bf16[192,2048]{1,0:T(8,128)(2,1)} %bitcast.43, bf16[192,512]{1,0:T(8,128)(2,1)S(1)} %convolution_convert_fusion.3, bf16[192,512]{1,0:T(8,128)(2,1)S(1)} %convolution_convert_fusion.4), kind=kOutput, calls=%fused_computation.10 | convolution fusion | flops 810287104 | bytes 4063232 | tf_op jit(solution)/shard_map/dot_general | solution.py:30
  255.5 65.4 %reduce-scatter.2.cloned.1.call-done = bf16[32,2048]{1,0:T(8,128)(2,1)} async-done(((bf16[512,2048]{1,0:T(8,128)(2,1)}), bf16[32,2048]{1,0:T(8,128)(2,1)}) %reduce-scatter.2.cloned.1.call-update) | async-done | bytes 131088 | tf_op jit(solution)/shard_map/reduce_scatter | solution.py:189
  (180 shorter events, 57.9 us)
Async XLA Ops:
  6.5 200.2 %all-gather.7.cloned.1.call-start = ((), (), s32[]{:S(2)}) async-start(), calls=%async_computation.7 | async-start | bytes 3932160 | tf_op jit(solution)/shard_map/all_gather | solution.py:113
  7.3 202.5 %all-gather.9.cloned.1.call-start = ((), (), s32[]{:S(2)}) async-start(), calls=%async_computation.8 | async-start | bytes 3932160 | tf_op jit(solution)/shard_map/all_gather | solution.py:114
  8.0 204.9 %all-gather.11.cloned.1.call-start = ((), (), s32[]{:S(2)}) async-start(), calls=%async_computation.9 | async-start | bytes 3932160 | tf_op jit(solution)/shard_map/all_gather | solution.py:115
  49.4 39.1 %collective-permute-start = (bf16[256,128]{1,0:T(8,128)(2,1)S(1)}, bf16[256,128]{1,0:T(8,128)(2,1)S(1)}, u32[]{:S(2)}, u32[]{:S(2)}) collective-permute-start(bf16[256,128]{1,0:T(8,128)(2,1)S(1)} %constant_dynamic-update-slice_fusion), channel_id=1, source_target_pairs={{0,4},{1,5},{2,6},{3,7},{4,8},{5,9},{6,10},{7,11},{8,12},{9,13},{1... | collective-permute-start | bytes 196616 | tf_op jit(solution)/shard_map/ppermute | solution.py:17
  51.4 37.2 %collective-permute-start.1 = (bf16[256,128]{1,0:T(8,128)(2,1)S(1)}, bf16[256,128]{1,0:T(8,128)(2,1)S(1)}, u32[]{:S(2)}, u32[]{:S(2)}) collective-permute-start(bf16[256,128]{1,0:T(8,128)(2,1)S(1)} %constant_dynamic-update-slice_fusion), channel_id=1, source_target_pairs={{0,3},{1,4},{2,5},{3,6},{4,7},{5,8},{6,9},{7,10},{8,11},{9,12},{10... | collective-permute-start | bytes 196616 | tf_op jit(solution)/shard_map/ppermute | solution.py:17
  53.3 35.3 %collective-permute-start.2 = (bf16[256,128]{1,0:T(8,128)(2,1)S(1)}, bf16[256,128]{1,0:T(8,128)(2,1)S(1)}, u32[]{:S(2)}, u32[]{:S(2)}) collective-permute-start(bf16[256,128]{1,0:T(8,128)(2,1)S(1)} %constant_dynamic-update-slice_fusion), channel_id=1, source_target_pairs={{0,2},{1,3},{2,4},{3,5},{4,6},{5,7},{6,8},{7,9},{8,10},{9,11},{10,... | collective-permute-start | bytes 196616 | tf_op jit(solution)/shard_map/ppermute | solution.py:17
  55.3 18.2 %collective-permute-start.4 = (bf16[128,2048]{1,0:T(8,128)(2,1)S(1)}, bf16[128,2048]{1,0:T(8,128)(2,1)S(1)}, u32[]{:S(2)}, u32[]{:S(2)}) collective-permute-start(bf16[128,2048]{1,0:T(8,128)(2,1)S(1)} %slice.164), channel_id=1, source_target_pairs={{0,32},{32,64},{64,96},{96,0},{1,33},{33,65},{65,97},{97,1},{2,34}... | collective-permute-start | bytes 1572872 | tf_op jit(solution)/shard_map/ppermute | solution.py:22
  58.4 18.3 %collective-permute-start.5 = (bf16[128,2048]{1,0:T(8,128)(2,1)S(1)}, bf16[128,2048]{1,0:T(8,128)(2,1)S(1)}, u32[]{:S(2)}, u32[]{:S(2)}) collective-permute-start(bf16[128,2048]{1,0:T(8,128)(2,1)S(1)} %slice.164), channel_id=1, source_target_pairs={{0,96},{32,0},{64,32},{96,64},{1,97},{33,1},{65,33},{97,65},{2,98}... | collective-permute-start | bytes 1572872 | tf_op jit(solution)/shard_map/ppermute | solution.py:22
  73.5 10.4 %collective-permute-start.6 = (bf16[64,2048]{1,0:T(8,128)(2,1)S(1)}, bf16[64,2048]{1,0:T(8,128)(2,1)S(1)}, u32[]{:S(2)}, u32[]{:S(2)}) collective-permute-start(bf16[64,2048]{1,0:T(8,128)(2,1)S(1)} %slice.174), channel_id=1, source_target_pairs={{0,32},{32,64},{64,96},{96,0},{1,33},{33,65},{65,97},{97,1},{2,34}... | collective-permute-start | bytes 786440 | tf_op jit(solution)/shard_map/ppermute | solution.py:22
  76.7 9.9 %collective-permute-start.7 = (bf16[64,2048]{1,0:T(8,128)(2,1)S(1)}, bf16[64,2048]{1,0:T(8,128)(2,1)S(1)}, u32[]{:S(2)}, u32[]{:S(2)}) collective-permute-start(bf16[64,2048]{1,0:T(8,128)(2,1)S(1)} %slice.175), channel_id=1, source_target_pairs={{0,96},{32,0},{64,32},{96,64},{1,97},{33,1},{65,33},{97,65},{2,98}... | collective-permute-start | bytes 786440 | tf_op jit(solution)/shard_map/ppermute | solution.py:22
  83.9 7.7 %collective-permute-start.3 = (bf16[256,128]{1,0:T(8,128)(2,1)S(1)}, bf16[256,128]{1,0:T(8,128)(2,1)S(1)}, u32[]{:S(2)}, u32[]{:S(2)}) collective-permute-start(bf16[256,128]{1,0:T(8,128)(2,1)S(1)} %constant_dynamic-update-slice_fusion), channel_id=1, source_target_pairs={{0,1},{1,2},{2,3},{3,4},{4,5},{5,6},{6,7},{7,8},{8,9},{9,10},{10,1... | collective-permute-start | bytes 196616 | tf_op jit(solution)/shard_map/ppermute | solution.py:17
  86.6 7.8 %collective-permute-start.8 = (bf16[512,2048]{1,0:T(8,128)(2,1)S(1)}, bf16[512,2048]{1,0:T(8,128)(2,1)S(1)}, u32[]{:S(2)}, u32[]{:S(2)}) collective-permute-start(bf16[512,2048]{1,0:T(8,128)(2,1)S(1)} %constant_dynamic-update-slice_fusion.12), channel_id=1, source_target_pairs={{0,1},{1,0},{2,3},{3,2},{4,5},{5,4},{6,7},{7,6},{8,9},{9,8},{10,11... | collective-permute-start | bytes 6291464 | tf_op jit(solution)/shard_map/ppermute | solution.py:22
  96.2 20.0 %all-to-all-start = ((bf16[4,32,2048]{2,1,0:T(8,128)(2,1)}), bf16[4,32,2048]{2,1,0:T(8,128)(2,1)S(1)}, u32[]{:S(2)}, u32[]{:S(2)}) async-start(bf16[4,32,2048]{2,1,0:T(8,128)(2,1)} %bitcast.12), calls=%async_computation | async-start | bytes 1048576 | tf_op jit(solution)/shard_map/all_to_all | solution.py:144
  121.0 8.1 %collective-permute-start.12 = (bf16[32,2048]{1,0:T(8,128)(2,1)S(1)}, bf16[32,2048]{1,0:T(8,128)(2,1)S(1)}, u32[]{:S(2)}, u32[]{:S(2)}) collective-permute-start(bf16[32,2048]{1,0:T(8,128)(2,1)S(1)} %get-tuple-element.16), channel_id=1, source_target_pairs={{0,2},{2,4},{4,6},{6,8},{8,10},{10,12},{12,14},{14,16},{16,18},{18... | collective-permute-start | bytes 393224 | tf_op jit(solution)/shard_map/ppermute | solution.py:22
  124.0 7.6 %collective-permute-start.10 = (bf16[32,2048]{1,0:T(8,128)(2,1)S(1)}, bf16[32,2048]{1,0:T(8,128)(2,1)S(1)}, u32[]{:S(2)}, u32[]{:S(2)}) collective-permute-start(bf16[32,2048]{1,0:T(8,128)(2,1)S(1)} %collective-permute-done.9), channel_id=1, source_target_pairs={{0,30},{2,0},{4,2},{6,4},{8,6},{10,8},{12,10},{14,12},{16,14},{18,... | collective-permute-start | bytes 393224 | tf_op jit(solution)/shard_map/ppermute | solution.py:22
  129.1 8.1 %collective-permute-start.13 = (bf16[32,2048]{1,0:T(8,128)(2,1)S(1)}, bf16[32,2048]{1,0:T(8,128)(2,1)S(1)}, u32[]{:S(2)}, u32[]{:S(2)}) collective-permute-start(bf16[32,2048]{1,0:T(8,128)(2,1)S(1)} %collective-permute-done.12), channel_id=1, source_target_pairs={{0,2},{2,4},{4,6},{6,8},{8,10},{10,12},{12,14},{14,16},{16,18},{18... | collective-permute-start | bytes 393224 | tf_op jit(solution)/shard_map/ppermute | solution.py:22
  131.6 15.6 %collective-permute-start.11 = (bf16[32,2048]{1,0:T(8,128)(2,1)S(1)}, bf16[32,2048]{1,0:T(8,128)(2,1)S(1)}, u32[]{:S(2)}, u32[]{:S(2)}) collective-permute-start(bf16[32,2048]{1,0:T(8,128)(2,1)S(1)} %collective-permute-done.10), channel_id=1, source_target_pairs={{0,30},{2,0},{4,2},{6,4},{8,6},{10,8},{12,10},{14,12},{16,14},{18,... | collective-permute-start | bytes 393224 | tf_op jit(solution)/shard_map/ppermute | solution.py:22
  137.2 8.1 %collective-permute-start.14 = (bf16[32,2048]{1,0:T(8,128)(2,1)S(1)}, bf16[32,2048]{1,0:T(8,128)(2,1)S(1)}, u32[]{:S(2)}, u32[]{:S(2)}) collective-permute-start(bf16[32,2048]{1,0:T(8,128)(2,1)S(1)} %collective-permute-done.13), channel_id=1, source_target_pairs={{0,2},{2,4},{4,6},{6,8},{8,10},{10,12},{12,14},{14,16},{16,18},{18... | collective-permute-start | bytes 393224 | tf_op jit(solution)/shard_map/ppermute | solution.py:22
  145.2 8.1 %collective-permute-start.15 = (bf16[32,2048]{1,0:T(8,128)(2,1)S(1)}, bf16[32,2048]{1,0:T(8,128)(2,1)S(1)}, u32[]{:S(2)}, u32[]{:S(2)}) collective-permute-start(bf16[32,2048]{1,0:T(8,128)(2,1)S(1)} %collective-permute-done.14), channel_id=1, source_target_pairs={{0,2},{2,4},{4,6},{6,8},{8,10},{10,12},{12,14},{14,16},{16,18},{18... | collective-permute-start | bytes 393224 | tf_op jit(solution)/shard_map/ppermute | solution.py:22
  147.2 15.6 %collective-permute-start.16 = (bf16[32,2048]{1,0:T(8,128)(2,1)S(1)}, bf16[32,2048]{1,0:T(8,128)(2,1)S(1)}, u32[]{:S(2)}, u32[]{:S(2)}) collective-permute-start(bf16[32,2048]{1,0:T(8,128)(2,1)S(1)} %collective-permute-done.11), channel_id=1, source_target_pairs={{0,30},{2,0},{4,2},{6,4},{8,6},{10,8},{12,10},{14,12},{16,14},{18,... | collective-permute-start | bytes 393224 | tf_op jit(solution)/shard_map/ppermute | solution.py:22
  154.6 47.3 %all-to-all-start.1 = ((bf16[8,24,2048]{2,1,0:T(8,128)(2,1)}), bf16[8,24,2048]{2,1,0:T(8,128)(2,1)S(1)}, u32[]{:S(2)}, u32[]{:S(2)}) async-start(bf16[8,24,2048]{2,1,0:T(8,128)(2,1)} %bitcast.34), calls=%async_computation.1 | async-start | bytes 1572864 | tf_op jit(solution)/shard_map/all_to_all | solution.py:175
  160.9 15.4 %collective-permute-start.20 = (bf16[32,2048]{1,0:T(8,128)(2,1)S(1)}, bf16[32,2048]{1,0:T(8,128)(2,1)S(1)}, u32[]{:S(2)}, u32[]{:S(2)}) collective-permute-start(bf16[32,2048]{1,0:T(8,128)(2,1)S(1)} %collective-permute-done.15), channel_id=1, source_target_pairs={{0,2},{2,4},{4,6},{6,8},{8,10},{10,12},{12,14},{14,16},{16,18},{18... | collective-permute-start | bytes 393224 | tf_op jit(solution)/shard_map/ppermute | solution.py:22
  162.8 7.9 %collective-permute-start.17 = (bf16[32,2048]{1,0:T(8,128)(2,1)S(1)}, bf16[32,2048]{1,0:T(8,128)(2,1)S(1)}, u32[]{:S(2)}, u32[]{:S(2)}) collective-permute-start(bf16[32,2048]{1,0:T(8,128)(2,1)S(1)} %collective-permute-done.16), channel_id=1, source_target_pairs={{0,30},{2,0},{4,2},{6,4},{8,6},{10,8},{12,10},{14,12},{16,14},{18,... | collective-permute-start | bytes 393224 | tf_op jit(solution)/shard_map/ppermute | solution.py:22
  170.8 8.1 %collective-permute-start.18 = (bf16[32,2048]{1,0:T(8,128)(2,1)S(1)}, bf16[32,2048]{1,0:T(8,128)(2,1)S(1)}, u32[]{:S(2)}, u32[]{:S(2)}) collective-permute-start(bf16[32,2048]{1,0:T(8,128)(2,1)S(1)} %collective-permute-done.17), channel_id=1, source_target_pairs={{0,30},{2,0},{4,2},{6,4},{8,6},{10,8},{12,10},{14,12},{16,14},{18,... | collective-permute-start | bytes 393224 | tf_op jit(solution)/shard_map/ppermute | solution.py:22
  176.4 8.1 %collective-permute-start.21 = (bf16[32,2048]{1,0:T(8,128)(2,1)S(1)}, bf16[32,2048]{1,0:T(8,128)(2,1)S(1)}, u32[]{:S(2)}, u32[]{:S(2)}) collective-permute-start(bf16[32,2048]{1,0:T(8,128)(2,1)S(1)} %collective-permute-done.20), channel_id=1, source_target_pairs={{0,2},{2,4},{4,6},{6,8},{8,10},{10,12},{12,14},{14,16},{16,18},{18... | collective-permute-start | bytes 393224 | tf_op jit(solution)/shard_map/ppermute | solution.py:22
  178.9 15.6 %collective-permute-start.19 = (bf16[32,2048]{1,0:T(8,128)(2,1)S(1)}, bf16[32,2048]{1,0:T(8,128)(2,1)S(1)}, u32[]{:S(2)}, u32[]{:S(2)}) collective-permute-start(bf16[32,2048]{1,0:T(8,128)(2,1)S(1)} %collective-permute-done.18), channel_id=1, source_target_pairs={{0,30},{2,0},{4,2},{6,4},{8,6},{10,8},{12,10},{14,12},{16,14},{18,... | collective-permute-start | bytes 393224 | tf_op jit(solution)/shard_map/ppermute | solution.py:22
  184.4 8.1 %collective-permute-start.22 = (bf16[32,2048]{1,0:T(8,128)(2,1)S(1)}, bf16[32,2048]{1,0:T(8,128)(2,1)S(1)}, u32[]{:S(2)}, u32[]{:S(2)}) collective-permute-start(bf16[32,2048]{1,0:T(8,128)(2,1)S(1)} %collective-permute-done.21), channel_id=1, source_target_pairs={{0,2},{2,4},{4,6},{6,8},{8,10},{10,12},{12,14},{14,16},{16,18},{18... | collective-permute-start | bytes 393224 | tf_op jit(solution)/shard_map/ppermute | solution.py:22
  192.5 8.1 %collective-permute-start.23 = (bf16[32,2048]{1,0:T(8,128)(2,1)S(1)}, bf16[32,2048]{1,0:T(8,128)(2,1)S(1)}, u32[]{:S(2)}, u32[]{:S(2)}) collective-permute-start(bf16[32,2048]{1,0:T(8,128)(2,1)S(1)} %collective-permute-done.22), channel_id=1, source_target_pairs={{0,2},{2,4},{4,6},{6,8},{8,10},{10,12},{12,14},{14,16},{16,18},{18... | collective-permute-start | bytes 393224 | tf_op jit(solution)/shard_map/ppermute | solution.py:22
  201.9 18.2 %all-to-all-start.3 = ((bf16[8,24,2048]{2,1,0:T(8,128)(2,1)}), bf16[8,24,2048]{2,1,0:T(8,128)(2,1)}, u32[]{:S(2)}, u32[]{:S(2)}) async-start(bf16[8,24,2048]{2,1,0:T(8,128)(2,1)} %bitcast.44), calls=%async_computation.3 | async-start | bytes 1572864 | tf_op jit(solution)/shard_map/all_to_all | solution.py:175
  220.1 14.9 %all-to-all-start.2 = ((bf16[8,24,2048]{2,1,0:T(8,128)(2,1)}), bf16[8,24,2048]{2,1,0:T(8,128)(2,1)}, u32[]{:S(2)}, u32[]{:S(2)}) async-start(bf16[8,24,2048]{2,1,0:T(8,128)(2,1)} %bitcast.177), calls=%async_computation.2 | async-start | bytes 1572864 | tf_op jit(solution)/shard_map/all_to_all | solution.py:186
  235.0 16.6 %all-to-all-start.4 = ((bf16[8,24,2048]{2,1,0:T(8,128)(2,1)}), bf16[8,24,2048]{2,1,0:T(8,128)(2,1)S(1)}, u32[]{:S(2)}, u32[]{:S(2)}) async-start(bf16[8,24,2048]{2,1,0:T(8,128)(2,1)} %bitcast.46), calls=%async_computation.4 | async-start | bytes 1572864 | tf_op jit(solution)/shard_map/all_to_all | solution.py:186
  241.7 79.2 %reduce-scatter.2.cloned.1.call-start = ((), (), s32[]{:S(2)}) async-start(), calls=%async_computation.6 | async-start | bytes 2228224 | tf_op jit(solution)/shard_map/reduce_scatter | solution.py:189
  (27 other events, 688.6 us)
Sparse Core Ops, SparseCore 0:
  9.5 51.6 all-gather.6
  63.3 52.9 all-gather.8
  118.4 47.6 all-gather.10
  255.6 65.2 reduce-scatter.1

commit v3 on v2

v3 whole, which is shorter than its diff:
```python
import functools

import jax
import jax.numpy as jnp
from jax import lax
from jax.experimental import pallas as pl
from jax.experimental.pallas import tpu as pltpu
from jax.sharding import Mesh, PartitionSpec as P

HS = 128
HOPS = 4
CAP = 3
BF = jnp.bfloat16
F16 = jnp.float16
F32 = jnp.float32
EP = ("x", "z", "core")
XC = ("x", "core")
XZ = ("x", "z")
ZC = ("z", "core")


def from_earlier(value, by):
    chips = lax.axis_size(XZ)
    return lax.ppermute(value, XZ, [(i, i + by) for i in range(chips - by)])


def shift(value, axis, by):
    devices = lax.axis_size(axis)
    return lax.ppermute(value, axis, [(i, (i + by) % devices) for i in range(devices)])


def other_core(value):
    return shift(value, "core", 1)


def contract(left, right, dims):
    return lax.dot_general(left, right, (dims, ((), ())), preferred_element_type=F32)


def gather_x(value):
    half = value.shape[0] // 2
    from_left, from_right = shift(value, "x", 1), shift(value, "x", -1)
    far_low, far_high = shift(from_left[:half], "x", 1), shift(from_right[half:], "x", -1)
    return jnp.concatenate([value, from_left, from_right, far_low, far_high], 0)


def attention(queries, keys, values, doc_start):
    tok_ep = queries.shape[0]
    group_size = queries.shape[1] // HS
    cores = lax.axis_size("core")
    chips = -(-HOPS // cores)
    own = lax.all_gather(jnp.concatenate([keys, values], 1), "core", axis=0, tiled=True)
    both = jnp.concatenate([from_earlier(own, by) for by in range(chips, 0, -1)] + [own], 0)
    key_all, value_all = both[:, :HS], both[:, HS:]
    first = (lax.axis_index(XZ) - chips) * cores * tok_ep
    key_pos = first + jnp.arange(both.shape[0], dtype=jnp.int32)
    query_pos = lax.axis_index(EP) * tok_ep + jnp.arange(tok_ep, dtype=jnp.int32)
    key_mask = (key_pos[None, :] <= query_pos[:, None]) & (key_pos[None, :] >= doc_start[:, None])
    query_heads = queries.reshape(tok_ep, group_size, HS)
    score_vals = jnp.einsum("igd,jd->gij", query_heads, key_all, preferred_element_type=F32) * (
        1.0 / HS**0.5
    )
    score_vals = jnp.where(key_mask[None], score_vals, -jnp.inf)
    row_peak = jnp.max(score_vals, axis=-1, keepdims=True)
    prob_vals = jnp.exp(score_vals - row_peak)
    row_total = jnp.sum(prob_vals, axis=-1, keepdims=True)
    weighted = jnp.einsum("gij,jd->igd", prob_vals.astype(BF), value_all, preferred_element_type=F32)
    return (
        (weighted / jnp.transpose(row_total, (1, 0, 2))).reshape(tok_ep, group_size * HS).astype(BF)
    )


def slot_ranks(ids, experts, core_of):
    match = ids[None] == experts[:, None, None]
    hit = jnp.any(match, axis=1)
    step = jnp.arange(ids.shape[1], dtype=jnp.int32)
    before = (step[:, None] < step[None, :]) & (core_of[:, None] == core_of[None, :])
    rank = jnp.dot(hit.astype(BF), before.astype(BF), preferred_element_type=F32).astype(jnp.int32)
    return match, jnp.where(hit, rank, -1)


def expert_kernel(parts, rows_ref, gate_up_ref, down_ref, out_ref, hidden_ref):
    step = pl.program_id(0)
    units = gate_up_ref.shape[0] // 2

    @pl.when(step < parts)
    def _():
        rows = rows_ref[...]
        gate = contract(rows, gate_up_ref[:units], ((1,), (1,)))
        up = contract(rows, gate_up_ref[units:], ((1,), (1,)))
        hidden_ref[step] = (gate / (1.0 + jnp.exp(-gate)) * up).astype(BF)

    @pl.when(step >= parts)
    def _():
        total = jnp.dot(hidden_ref[0], down_ref[:units], preferred_element_type=F32)
        for part in range(1, parts):
            rows_of = pl.ds(part * units, units)
            total += jnp.dot(hidden_ref[part], down_ref[rows_of], preferred_element_type=F32)
        out_ref[...] = total.astype(BF)


def expert(rows, gate_up, down, parts):
    count, width = rows.shape
    units, cols = gate_up.shape[0] // parts, down.shape[1]
    return pl.pallas_call(
        functools.partial(expert_kernel, parts),
        grid=(2 * parts,),
        in_specs=[
            pl.BlockSpec((count, width), lambda i: (0, 0)),
            pl.BlockSpec((units, width), lambda i: (jnp.minimum(i, parts - 1), 0)),
            pl.BlockSpec((down.shape[0] // parts, cols), lambda i: (jnp.maximum(i - parts, 0), 0)),
        ],
        out_specs=pl.BlockSpec((count, cols), lambda i: (0, jnp.maximum(i - parts, 0))),
        out_shape=jax.ShapeDtypeStruct((count, width), BF),
        scratch_shapes=[pltpu.VMEM((parts, count, units // 2), BF)],
        compiler_params=pltpu.CompilerParams(vmem_limit_bytes=40 * 2**20),
        cost_estimate=pl.CostEstimate(
            flops=2 * count * (gate_up.size + down.size),
            bytes_accessed=2 * (2 * rows.size + gate_up.size + down.size),
            transcendentals=count * gate_up.shape[0] // 2,
        ),
    )(rows, gate_up, down)


def on_device(
    queries,
    keys,
    values,
    doc_start,
    residual,
    out_weight,
    norm_gain,
    gate_weight,
    up_weight,
    down_weight,
    route_ids,
    route_weights,
):
    nx, nz, nc, nr = (lax.axis_size(a) for a in ("x", "z", "core", "rep"))
    width = out_weight.shape[1]
    rows8 = out_weight.shape[0]
    tok_sub, top = route_ids.shape[1], route_ids.shape[2]
    here = lax.axis_index("z")

    gate_up = jnp.concatenate([gate_weight[0], up_weight[0]], 0)
    gate_up = lax.all_gather(gate_up, "rep", axis=0, tiled=True)

    info = jnp.concatenate([route_ids[0].astype(F16), route_weights[0].astype(F16)], 1)
    info = info.reshape(rows8, -1)
    info_width = info.shape[1]
    info = jnp.pad(info, ((0, 0), (0, -info_width % 128)))
    z_all = lax.all_gather(
        jnp.concatenate([out_weight.astype(F16), info], 1), ZC, axis=0, tiled=True
    )
    z_rows = z_all[:, :width].reshape(nz, nc, rows8, width)
    z_rows = lax.dynamic_slice_in_dim(z_rows, lax.axis_index("core"), 1, 1)
    z_rows = z_rows.reshape(nz * rows8, width).astype(BF)
    z_rows, keys, values = lax.optimization_barrier((z_rows, keys, values))
    out_own = gather_x(z_rows)
    out_other = other_core(out_own)

    attended = attention(queries, keys, values, doc_start)
    feats = attended.shape[1]
    place = jnp.arange(feats, dtype=jnp.int32)
    block = nz * rows8
    hop = (place // block) % nx
    pc = place // (block * nx)
    pc = jnp.where(lax.axis_index("core") == 0, pc, nc - 1 - pc)
    px = (lax.axis_index("x") + nx + jnp.where(hop == 1, -1, jnp.where(hop == 2, 1, hop // 3 * 2))) % nx
    pz, pi = (place // rows8) % nz, place % rows8
    source = ((px * nz + pz) * nc + pc) * rows8 + pi
    permute = (place[:, None] == source[None, :]).astype(BF)
    attended = jnp.dot(attended, permute, preferred_element_type=F32).astype(BF)

    half = feats // 2
    partial_value = jnp.dot(attended[:, :half], out_own, preferred_element_type=F32)
    partial_value += jnp.dot(attended[:, half:], out_other, preferred_element_type=F32)
    partial_value = partial_value.astype(BF)
    parts = lax.all_to_all(partial_value, "rep", split_axis=0, concat_axis=0, tiled=True)
    parts, gate_up, down_weight = lax.optimization_barrier((parts, gate_up, down_weight))
    down_all = lax.all_gather(down_weight[0], "rep", axis=0, tiled=True)
    head_total = jnp.sum(parts.reshape(nr, tok_sub, width).astype(F32), axis=0)
    hidden_sum = residual[0].astype(F32) + head_total
    inverse_rms = lax.rsqrt(jnp.mean(hidden_sum * hidden_sum, axis=-1, keepdims=True) + 1e-06)
    normed = (hidden_sum * inverse_rms * norm_gain).astype(BF)
    column = lax.all_gather(normed.astype(F16), ZC, axis=0, tiled=True).astype(BF)

    table = z_all[:, width : width + info_width].astype(F32).reshape(-1, 2 * top)
    table = jnp.transpose(table)
    count = table.shape[1]
    core = lax.axis_index("core")
    core_of = jnp.arange(count, dtype=jnp.int32) // tok_sub % nc
    slot = jnp.arange(CAP * nz, dtype=jnp.int32)
    ids = table[:top].astype(jnp.int32)
    experts = (jnp.arange(nx, dtype=jnp.int32) * nz + here) * nc + core
    _, rank = slot_ranks(ids, experts, core_of)
    seat = core_of[None, :] * slot.size + rank
    seat = jnp.where(rank < 0, -1, seat)
    seats = jnp.arange(nc * slot.size, dtype=jnp.int32)
    send = (seat[:, None, :] == seats[None, :, None]).astype(BF).reshape(-1, count)

    table = table.reshape(2 * top, nz, nc, tok_sub)
    table = lax.dynamic_slice_in_dim(table, core, 1, 2).reshape(2 * top, -1)
    lane = jnp.arange(nx * nc, dtype=jnp.int32)
    experts = ((lane // nc) * nz + here) * nc + lane % nc
    own_count = table.shape[1]
    match, rank = slot_ranks(
        table[:top].astype(jnp.int32), experts, jnp.zeros((own_count,), jnp.int32)
    )
    gain = jnp.sum(jnp.where(match, table[None, top:], 0.0), axis=1)
    back = jnp.where(rank[:, None, :] == slot[None, :, None], gain[:, None, :], 0.0)
    back = back.astype(BF).reshape(-1, own_count)

    send_rows = jnp.dot(send, column, preferred_element_type=F32).astype(BF)
    rows = lax.all_to_all(send_rows, "x", split_axis=0, concat_axis=0, tiled=True)
    expert_out = expert(rows, gate_up, down_all, nr)
    returned = lax.all_to_all(expert_out, XC, split_axis=0, concat_axis=0, tiled=True)
    mixed = contract(back, returned, ((0,), (0,))).astype(BF)
    expert_mix = lax.psum_scatter(mixed, "z", scatter_dimension=0, tiled=True)
    return (hidden_sum + expert_mix.astype(F32)).astype(BF)[None]


def solution(mesh):
    devices = mesh.devices
    split = Mesh(devices.reshape(4, 4, devices.shape[1] // 8, 2), ("rep",) + EP)
    placed = (
        P(EP, "rep"),
        P(EP, "rep"),
        P(EP, "rep"),
        P(EP),
        P(EP, "rep", None),
        P(("rep",) + EP, None),
        P(),
        P(EP, "rep", None),
        P(EP, "rep", None),
        P(EP, None, "rep"),
        P(EP, "rep", None),
        P(EP, "rep", None),
    )
    return jax.shard_map(
        on_device, mesh=split, in_specs=placed, out_specs=P(EP, "rep", None), check_vma=False
    )
```

time: 330 us -> 296 us (0.90)
  the two profiles are of different devices: /device:TPU:4 before, /device:TPU:2 now
where the time goes in v3:
time: 296 us; the launch traced here: 295 us
  blocking collectives  109 us (37%)
  waiting for transfers between devices  102 us (34%)
  starting transfers between devices  27.1 us (9%)
  local copies, waits for them, and re-layouts  14.1 us (5%)
  between operations  13.6 us (5%)
  matrix products  11.9 us (4%)
  other arithmetic  8.76 us (3%)
  Pallas kernels  7.42 us (3%)
    reduce_scatter x1, waiting for transfers between devices, on_device(): expert_mix = lax.psum_scatter(mixed, 'z', scatter_dimension=0, tiled=True)  65.9 us
    all_gather x1, blocking collectives, on_device(): lax.all_gather(normed.astype(F16), ZC, axis=0, tiled=True).astype(BF)  41.7 us
    all_gather x1, blocking collectives, on_device(): lax.all_gather(jnp.concatenate([out_weight.astype(F16), info], 1), ZC, ax...  39.3 us
    all_to_all x1, blocking collectives, on_device(): lax.all_to_all(send_rows, 'x', split_axis=0, concat_axis=0, tiled=True)  26.4 us
    all_to_all x1, waiting for transfers between devices, on_device(): lax.all_to_all(expert_out, XC, split_axis=0, concat_axis=0, tiled=True)  18.9 us
    ppermute x5, starting transfers between devices, shift(): lax.ppermute(value, axis, [(i, (i + by) % devices) for i in range(devices)])  13.6 us
    unnamed x32, local copies, waits for them, and re-layouts  9.84 us
    all_to_all x1, waiting for transfers between devices, on_device(): lax.all_to_all(partial_value, 'rep', split_axis=0, concat_axis=0, tiled=T...  9.65 us
  transfers between devices with their start and end apart: 12, of which 5 were waited for; matrix products, arithmetic and copies ran while one was open for 8% of the time, Pallas kernels for 0%

profile of v3, /device:TPU:2, one launch (start us, length us, event | category | flops | bytes accessed | tf_op | source)
XLA Modules:
  0.0 294.6 jit_solution(10868268100528866833)
XLA Ops:
  6.6 2.8 pad_maximum_fusion
  9.7 39.3 %all-gather.9 = f16[256,2176]{1,0:T(8,128)(2,1)S(1)} all-gather(f16[8,2176]{1,0:T(8,128)(2,1)S(1)} %fusion.50), channel_id=1, replica_groups=mesh['rep'=4,'x'=4,'z'=16,'core'=2] {'z','core'}, dimensions={0}, use_global_device_ids=true | all-gather | bytes 1148928 | tf_op jit(solution)/shard_map/all_gather | solution.py:152
  50.1 3.4 %collective-permute-start.2 = (bf16[128,2048]{1,0:T(8,128)(2,1)}, bf16[128,2048]{1,0:T(8,128)(2,1)}, u32[]{:S(2)}, u32[]{:S(2)}) collective-permute-start(bf16[128,2048]{1,0:T(8,128)(2,1)} %convert_bitcast_fusion), channel_id=1, source_target_pairs={{0,32},{32,64},{64,96},{96,0},{1,33},{33,65},{65,97},{97,1},{2,34}... | collective-permute-start | bytes 1572872 | tf_op jit(solution)/shard_map/ppermute | solution.py:29
  53.4 2.4 collective-permute-start.3
  55.9 2.0 all_gather.16
  58.0 2.2 collective-permute-start
  60.1 1.9 collective-permute-start.1
  62.1 1.1 constant_dynamic-update-slice_fusion.7
  63.2 5.2 %collective-permute-done.2 = bf16[128,2048]{1,0:T(8,128)(2,1)} collective-permute-done((bf16[128,2048]{1,0:T(8,128)(2,1)}, bf16[128,2048]{1,0:T(8,128)(2,1)}, u32[]{:S(2)}, u32[]{:S(2)}) %collective-permute-start.2) | collective-permute-done | bytes 524320 | tf_op jit(solution)/shard_map/ppermute | solution.py:29
  69.3 2.2 collective-permute-start.4
  71.6 1.0 slice.51
  72.5 3.6 %collective-permute-start.5 = (bf16[64,2048]{1,0:T(8,128)(2,1)S(1)}, bf16[64,2048]{1,0:T(8,128)(2,1)S(1)}, u32[]{:S(2)}, u32[]{:S(2)}) collective-permute-start(bf16[64,2048]{1,0:T(8,128)(2,1)S(1)} %slice.51), channel_id=1, source_target_pairs={{0,96},{32,0},{64,32},{96,64},{1,97},{33,1},{65,33},{97,65},{2,98}... | collective-permute-start | bytes 786440 | tf_op jit(solution)/shard_map/ppermute | solution.py:29
  76.2 1.1 constant_dynamic-update-slice_fusion.6
  77.2 1.1 constant_dynamic-update-slice_fusion.5
  78.4 2.8 collective-permute-done.5
  81.2 1.9 collective-permute-start.6
  87.5 1.5 fusion.12
  91.4 2.0 fusion.45
  93.5 1.3 fusion.11
  94.7 4.5 %all-to-all-start = ((bf16[4,32,2048]{2,1,0:T(8,128)(2,1)}), bf16[4,32,2048]{2,1,0:T(8,128)(2,1)S(1)}, u32[]{:S(2)}, u32[]{:S(2)}) async-start(bf16[4,32,2048]{2,1,0:T(8,128)(2,1)} %bitcast.13), calls=%async_computation | async-start | bytes 1048576 | tf_op jit(solution)/shard_map/all_to_all | solution.py:179
  99.7 9.6 %all-to-all-done = bf16[4,32,2048]{2,1,0:T(8,128)(2,1)S(1)} async-done(((bf16[4,32,2048]{2,1,0:T(8,128)(2,1)}), bf16[4,32,2048]{2,1,0:T(8,128)(2,1)S(1)}, u32[]{:S(2)}, u32[]{:S(2)}) %all-to-all-start) | async-done | bytes 524320 | tf_op jit(solution)/shard_map/all_to_all | solution.py:179
  110.8 41.7 %all-gather.10 = f16[1024,2048]{1,0:T(8,128)(2,1)S(1)} all-gather(f16[32,2048]{1,0:T(8,128)(2,1)S(1)} %fusion.43), channel_id=1, replica_groups=mesh['rep'=4,'x'=4,'z'=16,'core'=2] {'z','core'}, dimensions={0}, use_global_device_ids=true | all-gather | bytes 4325376 | tf_op jit(solution)/shard_map/all_gather | solution.py:186
  152.5 1.8 fusion.6
  154.3 26.4 %all_to_all.32 = bf16[4,96,2048]{2,1,0:T(8,128)(2,1)S(1)} all-to-all(bf16[4,96,2048]{2,1,0:T(8,128)(2,1)S(1)} %bitcast.87), channel_id=1, replica_groups=mesh['rep'=4,'x'=4,'z'=16,'core'=2] {'x'}, dimensions={0} | all-to-all | bytes 3145728 | tf_op jit(solution)/shard_map/all_to_all | solution.py:215
  180.8 2.8 copy-done.1
  183.6 1.9 copy-done.2
  185.5 7.4 %shard_map.118 = bf16[384,2048]{1,0:T(8,128)(2,1)} custom-call(bf16[384,2048]{1,0:T(8,128)(2,1)S(1)} %bitcast.84, bf16[1536,2048]{1,0:T(8,128)(2,1)S(1)} %copy-done.1, bf16[3072,512]{1,0:T(8,128)(2,1)S(1)} %bitcast.85), custom_call_target="tpu_custom_call" | custom-call | flops 3623878656 | bytes 12582912 | tf_op jit(solution)/shard_map/pallas_call | solution.py:105
  192.9 5.0 %all-to-all-start.2 = ((bf16[8,48,2048]{2,1,0:T(8,128)(2,1)}), bf16[8,48,2048]{2,1,0:T(8,128)(2,1)S(1)}, u32[]{:S(2)}, u32[]{:S(2)}) async-start(bf16[8,48,2048]{2,1,0:T(8,128)(2,1)} %bitcast.23), calls=%async_computation.2 | async-start | bytes 3145728 | tf_op jit(solution)/shard_map/all_to_all | solution.py:217
  199.1 18.9 %all-to-all-done.2 = bf16[8,48,2048]{2,1,0:T(8,128)(2,1)S(1)} async-done(((bf16[8,48,2048]{2,1,0:T(8,128)(2,1)}), bf16[8,48,2048]{2,1,0:T(8,128)(2,1)S(1)}, u32[]{:S(2)}, u32[]{:S(2)}) %all-to-all-start.2) | async-done | bytes 1572896 | tf_op jit(solution)/shard_map/all_to_all | solution.py:217
  218.0 2.6 bitcast_convert_fusion
  220.6 65.9 %reduce-scatter.2.cloned.1.call-done = bf16[32,2048]{1,0:T(8,128)(2,1)} async-done(((bf16[512,2048]{1,0:T(8,128)(2,1)}), bf16[32,2048]{1,0:T(8,128)(2,1)}) %reduce-scatter.2.cloned.1.call-update) | async-done | bytes 131088 | tf_op jit(solution)/shard_map/reduce_scatter | solution.py:219
  286.5 1.6 fusion.44
  (84 shorter events, 12.3 us)
Async XLA Ops:
  6.5 80.9 %copy-start = (bf16[128,1024]{1,0:T(8,128)(2,1)S(1)}, bf16[128,1024]{1,0:T(8,128)(2,1)}, u32[]{:S(2)}) copy-start(bf16[128,1024]{1,0:T(8,128)(2,1)} %param.12) | copy-start | bytes 786436
  6.5 102.8 %all-gather.6.cloned.1.call-start = ((), (), s32[]{:S(2)}) async-start(), calls=%async_computation.4 | async-start | bytes 7864320 | tf_op jit(solution)/shard_map/all_gather | solution.py:146
  6.5 2.9 copy-start.6
  6.5 2.9 copy-start.11
  6.5 2.9 copy-start.10
  9.7 46.2 %copy-start.7 = (bf16[128,128]{1,0:T(8,128)(2,1)S(1)}, bf16[128,128]{1,0:T(8,128)(2,1)}, u32[]{:S(2)}) copy-start(bf16[128,128]{1,0:T(8,128)(2,1)} %param.14) | copy-start | bytes 98308
  9.7 46.2 %copy-start.8 = (bf16[128,128]{1,0:T(8,128)(2,1)S(1)}, bf16[128,128]{1,0:T(8,128)(2,1)}, u32[]{:S(2)}) copy-start(bf16[128,128]{1,0:T(8,128)(2,1)} %param.13) | copy-start | bytes 98308
  50.1 18.3 %collective-permute-start.2 = (bf16[128,2048]{1,0:T(8,128)(2,1)}, bf16[128,2048]{1,0:T(8,128)(2,1)}, u32[]{:S(2)}, u32[]{:S(2)}) collective-permute-start(bf16[128,2048]{1,0:T(8,128)(2,1)} %convert_bitcast_fusion), channel_id=1, source_target_pairs={{0,32},{32,64},{64,96},{96,0},{1,33},{33,65},{65,97},{97,1},{2,34}... | collective-permute-start | bytes 1572872 | tf_op jit(solution)/shard_map/ppermute | solution.py:29
  53.4 18.1 %collective-permute-start.3 = (bf16[128,2048]{1,0:T(8,128)(2,1)}, bf16[128,2048]{1,0:T(8,128)(2,1)}, u32[]{:S(2)}, u32[]{:S(2)}) collective-permute-start(bf16[128,2048]{1,0:T(8,128)(2,1)} %convert_bitcast_fusion), channel_id=1, source_target_pairs={{0,96},{32,0},{64,32},{96,64},{1,97},{33,1},{65,33},{97,65},{2,98}... | collective-permute-start | bytes 1572872 | tf_op jit(solution)/shard_map/ppermute | solution.py:29
  58.0 26.7 %collective-permute-start = (bf16[256,256]{1,0:T(8,128)(2,1)}, bf16[256,256]{1,0:T(8,128)(2,1)}, u32[]{:S(2)}, u32[]{:S(2)}) collective-permute-start(bf16[256,256]{1,0:T(8,128)(2,1)} %all_gather.16), channel_id=1, source_target_pairs={{0,4},{2,6},{4,8},{6,10},{8,12},{10,14},{12,16},{14,18},{16,20},{1... | collective-permute-start | bytes 393224 | tf_op jit(solution)/shard_map/ppermute | solution.py:24
  60.1 25.4 %collective-permute-start.1 = (bf16[256,256]{1,0:T(8,128)(2,1)}, bf16[256,256]{1,0:T(8,128)(2,1)}, u32[]{:S(2)}, u32[]{:S(2)}) collective-permute-start(bf16[256,256]{1,0:T(8,128)(2,1)} %all_gather.16), channel_id=1, source_target_pairs={{0,2},{2,4},{4,6},{6,8},{8,10},{10,12},{12,14},{14,16},{16,18},{18... | collective-permute-start | bytes 393224 | tf_op jit(solution)/shard_map/ppermute | solution.py:24
  63.2 19.9 %copy-start.12 = (s32[128]{0:T(128)S(1)}, s32[128]{0:T(128)}, u32[]{:S(2)}) copy-start(s32[128]{0:T(128)} %param.15) | copy-start | bytes 1540
  69.3 9.0 %collective-permute-start.4 = (bf16[64,2048]{1,0:T(8,128)(2,1)S(1)}, bf16[64,2048]{1,0:T(8,128)(2,1)S(1)}, u32[]{:S(2)}, u32[]{:S(2)}) collective-permute-start(bf16[64,2048]{1,0:T(8,128)(2,1)S(1)} %slice.50), channel_id=1, source_target_pairs={{0,32},{32,64},{64,96},{96,0},{1,33},{33,65},{65,97},{97,1},{2,34}... | collective-permute-start | bytes 786440 | tf_op jit(solution)/shard_map/ppermute | solution.py:29
  72.5 8.6 %collective-permute-start.5 = (bf16[64,2048]{1,0:T(8,128)(2,1)S(1)}, bf16[64,2048]{1,0:T(8,128)(2,1)S(1)}, u32[]{:S(2)}, u32[]{:S(2)}) collective-permute-start(bf16[64,2048]{1,0:T(8,128)(2,1)S(1)} %slice.51), channel_id=1, source_target_pairs={{0,96},{32,0},{64,32},{96,64},{1,97},{33,1},{65,33},{97,65},{2,98}... | collective-permute-start | bytes 786440 | tf_op jit(solution)/shard_map/ppermute | solution.py:29
  81.2 10.2 %collective-permute-start.6 = (bf16[512,2048]{1,0:T(8,128)(2,1)S(1)}, bf16[512,2048]{1,0:T(8,128)(2,1)}, u32[]{:S(2)}, u32[]{:S(2)}) collective-permute-start(bf16[512,2048]{1,0:T(8,128)(2,1)S(1)} %constant_dynamic-update-slice_fusion.3), channel_id=1, source_target_pairs={{0,1},{1,0},{2,3},{3,2},{4,5},{5,4},{6,7},{7,6},{8,9},{9,8},{10,11... | collective-permute-start | bytes 6291464 | tf_op jit(solution)/shard_map/ppermute | solution.py:29
  85.6 3.4 %copy-start.4 = (pred[128,768]{0,1:T(8,128)(4,1)S(1)}, pred[128,768]{0,1:T(8,128)(4,1)}, u32[]{:S(2)}) copy-start(pred[128,768]{0,1:T(8,128)(4,1)} %compare_and_fusion) | copy-start | bytes 294916
  93.4 5.7 %copy-start.5 = (f32[256,64]{1,0:T(8,128)S(1)}, f32[256,64]{1,0:T(8,128)}, u32[]{:S(2)}) copy-start(f32[256,64]{1,0:T(8,128)} %slice_convert_fusion) | copy-start | bytes 196612
  94.7 14.6 %all-to-all-start = ((bf16[4,32,2048]{2,1,0:T(8,128)(2,1)}), bf16[4,32,2048]{2,1,0:T(8,128)(2,1)S(1)}, u32[]{:S(2)}, u32[]{:S(2)}) async-start(bf16[4,32,2048]{2,1,0:T(8,128)(2,1)} %bitcast.13), calls=%async_computation | async-start | bytes 1048576 | tf_op jit(solution)/shard_map/all_to_all | solution.py:179
  99.2 81.6 %all-gather.8.cloned.1.call-start = ((), (), s32[]{:S(2)}) async-start(), calls=%async_computation.6 | async-start | bytes 3932160 | tf_op jit(solution)/shard_map/all_gather | solution.py:181
  109.4 1.2 copy-start.3
  109.4 1.3 copy-start.9
  180.8 2.8 copy-start.1
  183.6 1.9 copy-start.2
  192.9 25.1 %all-to-all-start.2 = ((bf16[8,48,2048]{2,1,0:T(8,128)(2,1)}), bf16[8,48,2048]{2,1,0:T(8,128)(2,1)S(1)}, u32[]{:S(2)}, u32[]{:S(2)}) async-start(bf16[8,48,2048]{2,1,0:T(8,128)(2,1)} %bitcast.23), calls=%async_computation.2 | async-start | bytes 3145728 | tf_op jit(solution)/shard_map/all_to_all | solution.py:217
  197.8 88.7 %reduce-scatter.2.cloned.1.call-start = ((), (), s32[]{:S(2)}) async-start(), calls=%async_computation.5 | async-start | bytes 2228224 | tf_op jit(solution)/shard_map/reduce_scatter | solution.py:219
Sparse Core Ops, SparseCore 0:
  9.5 77.8 all-gather.5
  109.5 42.3 all-gather.7
  220.8 65.7 reduce-scatter.1

commit v4 on v3

v4 whole, which is shorter than its diff:
```python
import functools

import jax
import jax.numpy as jnp
from jax import lax
from jax.experimental import pallas as pl
from jax.experimental.pallas import tpu as pltpu
from jax.sharding import Mesh, PartitionSpec as P

HS = 128
HOPS = 4
CAP = 3
VMEM_GRANT = 56 * 2**20
BF = jnp.bfloat16
F16 = jnp.float16
F32 = jnp.float32
X = ("xh", "xl")
EP = ("xh", "xl", "z", "core")
XC = ("xh", "xl", "core")
XZ = ("xh", "xl", "z")
ZC = ("z", "core")


def from_earlier(value, by):
    chips = lax.axis_size(XZ)
    return lax.ppermute(value, XZ, [(i, i + by) for i in range(chips - by)])


def shift(value, axis, by):
    devices = lax.axis_size(axis)
    return lax.ppermute(value, axis, [(i, (i + by) % devices) for i in range(devices)])


def contract(left, right, dims):
    return lax.dot_general(left, right, (dims, ((), ())), preferred_element_type=F32)


def attention(queries, keys, values, doc_start):
    tok_ep = queries.shape[0]
    group_size = queries.shape[1] // HS
    cores = lax.axis_size("core")
    chips = -(-HOPS // cores)
    own = lax.all_gather(jnp.concatenate([keys, values], 1), "core", axis=0, tiled=True)
    both = jnp.concatenate([from_earlier(own, by) for by in range(chips, 0, -1)] + [own], 0)
    key_all, value_all = both[:, :HS], both[:, HS:]
    first = (lax.axis_index(XZ) - chips) * cores * tok_ep
    key_pos = first + jnp.arange(both.shape[0], dtype=jnp.int32)
    query_pos = lax.axis_index(EP) * tok_ep + jnp.arange(tok_ep, dtype=jnp.int32)
    key_mask = (key_pos[None, :] <= query_pos[:, None]) & (key_pos[None, :] >= doc_start[:, None])
    query_heads = queries.reshape(tok_ep, group_size, HS)
    score_vals = jnp.einsum("igd,jd->gij", query_heads, key_all, preferred_element_type=F32) * (
        1.0 / HS**0.5
    )
    score_vals = jnp.where(key_mask[None], score_vals, -jnp.inf)
    row_peak = jnp.max(score_vals, axis=-1, keepdims=True)
    prob_vals = jnp.exp(score_vals - row_peak)
    row_total = jnp.sum(prob_vals, axis=-1, keepdims=True)
    weighted = jnp.einsum("gij,jd->igd", prob_vals.astype(BF), value_all, preferred_element_type=F32)
    return (
        (weighted / jnp.transpose(row_total, (1, 0, 2))).reshape(tok_ep, group_size * HS).astype(BF)
    )


def slot_ranks(ids, experts, core_of):
    match = ids[None] == experts[:, None, None]
    hit = jnp.any(match, axis=1)
    step = jnp.arange(ids.shape[1], dtype=jnp.int32)
    before = (step[:, None] < step[None, :]) & (core_of[:, None] == core_of[None, :])
    rank = jnp.dot(hit.astype(BF), before.astype(BF), preferred_element_type=F32).astype(jnp.int32)
    return match, jnp.where(hit, rank, -1)


def expert_kernel(parts, rows_ref, gate_up_ref, down_ref, out_ref, gu_ref, dn_ref, hidden_ref, sems):
    units, cols = gu_ref.shape[1] // 2, dn_ref.shape[2]
    copies = [
        pltpu.make_async_copy(gate_up_ref.at[part], gu_ref.at[part], sems.at[part])
        for part in range(parts)
    ] + [
        pltpu.make_async_copy(down_ref.at[part], dn_ref.at[part], sems.at[parts + part])
        for part in range(parts)
    ]
    for copy in copies:
        copy.start()
    rows = rows_ref[...]
    for part in range(0, parts, 2):
        copies[part].wait()
        copies[part + 1].wait()
        both = gu_ref[part : part + 2].reshape(4 * units, rows.shape[1])
        act = contract(rows, both, ((1,), (1,)))
        for k in range(2):
            gate = act[:, 2 * k * units : (2 * k + 1) * units]
            up = act[:, (2 * k + 1) * units : (2 * k + 2) * units]
            hidden = (gate / (1.0 + jnp.exp(-gate)) * up).astype(BF)
            hidden_ref[:, (part + k) * units : (part + k + 1) * units] = hidden
    hidden = hidden_ref[...]
    for part in range(parts):
        copies[parts + part].wait()
        total = jnp.dot(hidden, dn_ref[part], preferred_element_type=F32)
        out_ref[:, part * cols : (part + 1) * cols] = total.astype(BF)


def expert(rows, gate_up, down, parts):
    count, width = rows.shape
    gate_up = gate_up.reshape(parts, -1, width)
    down = down.reshape(parts, -1, down.shape[1])
    return pl.pallas_call(
        functools.partial(expert_kernel, parts),
        in_specs=[
            pl.BlockSpec(memory_space=pltpu.VMEM),
            pl.BlockSpec(memory_space=pltpu.HBM),
            pl.BlockSpec(memory_space=pltpu.HBM),
        ],
        out_specs=pl.BlockSpec(memory_space=pltpu.VMEM),
        out_shape=jax.ShapeDtypeStruct((count, width), BF),
        scratch_shapes=[
            pltpu.VMEM(gate_up.shape, BF),
            pltpu.VMEM(down.shape, BF),
            pltpu.VMEM((count, parts * gate_up.shape[1] // 2), BF),
            pltpu.SemaphoreType.DMA((2 * parts,)),
        ],
        compiler_params=pltpu.CompilerParams(vmem_limit_bytes=VMEM_GRANT),
        cost_estimate=pl.CostEstimate(
            flops=2 * count * (gate_up.size + down.size),
            bytes_accessed=2 * (2 * rows.size + gate_up.size + down.size),
            transcendentals=count * gate_up.shape[1] * parts // 2,
        ),
    )(rows, gate_up, down)


def add_low(left, right):
    return (left.astype(F32) + right.astype(F32)).astype(BF)


def ring_sums(chunks):
    places = len(chunks)

    def two(k):
        return jnp.concatenate([chunks[k % places], chunks[(k - 1) % places]], 0)

    def two_back(k):
        return jnp.concatenate([chunks[-k % places], chunks[(1 - k) % places]], 0)

    rows = chunks[0].shape[0]
    half = places // 2
    right, left = two(half), two_back(half - 1)
    for k in range(half - 2, 0, -2):
        right = add_low(shift(right, "z", 2), two(k))
        left = shift(left, "z", -2)
        if k > 2:
            left = add_low(left, two_back(k - 1))
    last = shift(add_low(left[:rows], chunks[-1]), "z", -1)
    pieces = [left[rows:], shift(right[:rows], "z", 2), shift(right[rows:], "z", 1), last]
    return sum((p.astype(F32) for p in pieces), chunks[0].astype(F32))


def on_device(
    queries,
    keys,
    values,
    doc_start,
    residual,
    out_weight,
    norm_gain,
    gate_weight,
    up_weight,
    down_weight,
    route_ids,
    route_weights,
):
    nx, nz, nc, nr = (lax.axis_size(a) for a in (X, "z", "core", "rep"))
    width = out_weight.shape[1]
    rows8 = out_weight.shape[0]
    tok_sub, top = route_ids.shape[1], route_ids.shape[2]
    here = lax.axis_index("z")

    gate_up = jnp.concatenate([gate_weight[0], up_weight[0]], 0)
    gate_up = lax.all_gather(gate_up, "rep", axis=0, tiled=True)

    info = jnp.concatenate([route_ids[0].astype(F16), route_weights[0].astype(F16)], 1)
    info = jnp.pad(info, ((0, 0), (0, 128 - 2 * top)))
    groups = tok_sub // rows8
    own_rows = jnp.concatenate(
        [out_weight.astype(F16)] + [info[g * rows8 : (g + 1) * rows8] for g in range(groups)], 1
    )
    pair_rows = jnp.concatenate([own_rows, shift(own_rows, "xl", 1)], 0)

    attended = attention(queries, keys, values, doc_start)
    half = attended.shape[1] // 2
    xh = lax.axis_index("xh")
    low, high = attended[:, :half], attended[:, half:]
    kept = jnp.where(xh == 0, low, high)
    given = jnp.where(xh == 0, high, low)
    got = shift(given, "xh", 1)
    pair_rows, _ = lax.optimization_barrier((pair_rows, given))
    z_all = lax.all_gather(pair_rows, ZC, axis=0, tiled=True)
    out_rows = z_all[:, :width].astype(BF)

    both = jnp.stack([jnp.where(xh == 0, kept, got), jnp.where(xh == 0, got, kept)], 0)
    both = both.reshape(2, nr, tok_sub, half).transpose(1, 0, 2, 3).reshape(-1, half)
    place = jnp.arange(half, dtype=jnp.int32)
    pi, px = place % rows8, place // rows8 % 2
    px = jnp.where(lax.axis_index("xl") == 0, px, 1 - px)
    pc, pz = place // (2 * rows8) % nc, place // (2 * rows8 * nc)
    source = ((px * nz + pz) * nc + pc) * rows8 + pi
    permute = (place[:, None] == source[None, :]).astype(BF)
    both = jnp.dot(both, permute, preferred_element_type=F32).astype(BF)
    partial_value = jnp.dot(both, out_rows, preferred_element_type=F32).astype(BF)
    parts = lax.all_to_all(partial_value, ("rep", "xh"), split_axis=0, concat_axis=0, tiled=True)
    parts, gate_up, down_weight = lax.optimization_barrier((parts, gate_up, down_weight))
    down_all = lax.all_gather(down_weight[0], "rep", axis=0, tiled=True)
    head_total = jnp.sum(parts.reshape(-1, tok_sub, width).astype(F32), axis=0)
    hidden_sum = residual[0].astype(F32) + head_total
    inverse_rms = lax.rsqrt(jnp.mean(hidden_sum * hidden_sum, axis=-1, keepdims=True) + 1e-06)
    normed = (hidden_sum * inverse_rms * norm_gain).astype(BF)
    column = lax.all_gather(normed.astype(F16), ZC, axis=0, tiled=True).astype(BF)

    table = z_all.reshape(nz * nc, 2, rows8, -1)[:, 0].reshape(nz * nc * rows8, -1)
    table = [table[:, width + 128 * g :][:, : 2 * top].astype(F32) for g in range(groups)]
    table = jnp.stack([jnp.transpose(t).reshape(2 * top, -1, rows8) for t in table], 2)
    table = table.reshape(2 * top, -1)
    count = table.shape[1]
    core = lax.axis_index("core")
    core_of = jnp.arange(count, dtype=jnp.int32) // tok_sub % nc
    slot = jnp.arange(CAP * nz, dtype=jnp.int32)
    ids = table[:top].astype(jnp.int32)
    experts = (jnp.arange(nx, dtype=jnp.int32) * nz + here) * nc + core
    _, rank = slot_ranks(ids, experts, core_of)
    seat = core_of[None, :] * slot.size + rank
    seat = jnp.where(rank < 0, -1, seat)
    seats = jnp.arange(nc * slot.size, dtype=jnp.int32)
    send = (seat[:, None, :] == seats[None, :, None]).astype(BF).reshape(-1, count)

    table = table.reshape(2 * top, nz, nc, tok_sub)
    table = lax.dynamic_slice_in_dim(table, core, 1, 2).reshape(2 * top, -1)
    lane = jnp.arange(nx * nc, dtype=jnp.int32)
    experts = ((lane // nc) * nz + here) * nc + lane % nc
    own_count = table.shape[1]
    match, rank = slot_ranks(
        table[:top].astype(jnp.int32), experts, jnp.zeros((own_count,), jnp.int32)
    )
    gain = jnp.sum(jnp.where(match, table[None, top:], 0.0), axis=1)

    def back_for(rank, gain):
        back = jnp.where(rank[:, None, :] == slot[None, :, None], gain[:, None, :], 0.0)
        return back.astype(BF).reshape(-1, own_count)

    def from_here(value):
        value = value.reshape(-1, nz, tok_sub)
        value = lax.dynamic_slice_in_dim(jnp.concatenate([value, value], 1), here, nz, 1)
        return value.reshape(-1, own_count)

    back = back_for(from_here(rank), from_here(gain))

    send_rows = jnp.dot(send, column, preferred_element_type=F32).astype(BF)
    rows = lax.all_to_all(send_rows, X, split_axis=0, concat_axis=0, tiled=True)
    expert_out = expert(rows, gate_up, down_all, nr)
    returned = lax.all_to_all(expert_out, XC, split_axis=0, concat_axis=0, tiled=True)
    mixed = contract(back, returned, ((0,), (0,))).astype(BF)
    expert_mix = ring_sums([mixed[k * tok_sub : (k + 1) * tok_sub] for k in range(nz)])
    return (hidden_sum + expert_mix).astype(BF)[None]


def solution(mesh):
    devices = mesh.devices
    split = Mesh(devices.reshape(4, 2, 2, devices.shape[1] // 8, 2), ("rep",) + EP)
    placed = (
        P(EP, "rep"),
        P(EP, "rep"),
        P(EP, "rep"),
        P(EP),
        P(EP, "rep", None),
        P(("rep",) + EP, None),
        P(),
        P(EP, "rep", None),
        P(EP, "rep", None),
        P(EP, None, "rep"),
        P(EP, "rep", None),
        P(EP, "rep", None),
    )
    return jax.shard_map(
        on_device, mesh=split, in_specs=placed, out_specs=P(EP, "rep", None), check_vma=False
    )
```

time: 296 us -> 282 us (0.953)
  the two profiles are of different devices: /device:TPU:2 before, /device:TPU:1 now
where the time goes in v4:
time: 282 us; the launch traced here: 278 us
  blocking collectives  115 us (41%)
  starting transfers between devices  60.8 us (22%)
  waiting for transfers between devices  59.3 us (21%)
  between operations  14.1 us (5%)
  Pallas kernels  10.5 us (4%)
  other arithmetic  8.04 us (3%)
  matrix products  7.44 us (3%)
  local copies, waits for them, and re-layouts  3.63 us (1%)
    ppermute x11, starting transfers between devices, shift(): lax.ppermute(value, axis, [(i, (i + by) % devices) for i in range(devices)])  48.3 us
    all_gather x1, blocking collectives, on_device(): lax.all_gather(normed.astype(F16), ZC, axis=0, tiled=True).astype(BF)  45.4 us
    all_gather x1, blocking collectives, on_device(): z_all = lax.all_gather(pair_rows, ZC, axis=0, tiled=True)  36.5 us
    ppermute x11, waiting for transfers between devices, shift(): lax.ppermute(value, axis, [(i, (i + by) % devices) for i in range(devices)])  25.1 us
    all_to_all x1, blocking collectives, on_device(): rows = lax.all_to_all(send_rows, X, split_axis=0, concat_axis=0, tiled=True)  24.3 us
    all_to_all x1, waiting for transfers between devices, on_device(): lax.all_to_all(expert_out, XC, split_axis=0, concat_axis=0, tiled=True)  19 us
    all_to_all x1, waiting for transfers between devices, on_device(): lax.all_to_all(partial_value, ('rep', 'xh'), split_axis=0, concat_axis=0,...  15.1 us
    pallas_call x1, Pallas kernels, expert(): pl.pallas_call(functools.partial(expert_kernel, parts), in_specs=[pl.Bloc...  10.5 us
  transfers between devices with their start and end apart: 17, of which 10 were waited for; matrix products, arithmetic and copies ran while one was open for 5% of the time, Pallas kernels for 0%

profile of v4, /device:TPU:1, one launch (start us, length us, event | category | flops | bytes accessed | tf_op | source)
XLA Modules:
  0.0 278.3 jit_solution(14183406933086060616)
XLA Ops:
  6.6 2.8 pad_maximum_fusion
  9.4 8.4 %all_gather.15 = bf16[256,256]{1,0:T(8,128)(2,1)S(1)} all-gather(bf16[128,256]{1,0:T(8,128)(2,1)S(1)} %pad_maximum_fusion.3), channel_id=1, replica_groups=mesh['rep'=4,'xh'=2,'xl'=2,'z'=16,'core'=2] {'core'}, dimensions={0}, use_global_device_ids=true | all-gather | bytes 196608 | tf_op jit(solution)/shard_map/all_gather | solution.py:43
  17.9 1.3 collective-permute-start
  19.1 1.8 collective-permute-start.1
  21.5 3.1 %collective-permute-start.3 = (f16[8,2560]{1,0:T(8,128)(2,1)S(1)}, f16[8,2560]{1,0:T(8,128)(2,1)S(1)}, u32[]{:S(2)}, u32[]{:S(2)}) collective-permute-start(f16[8,2560]{1,0:T(8,128)(2,1)S(1)} %constant_dynamic-update-slice_fusion.3), channel_id=1, source_target_pairs={{0,32},{32,0},{1,33},{33,1},{2,34},{34,2},{3,35},{35,3},{4,36},{36... | collective-permute-start | bytes 122888 | tf_op jit(solution)/shard_map/ppermute | solution.py:31
  29.0 10.9 %collective-permute-start.2 = (bf16[128,512]{1,0:T(8,128)(2,1)S(1)}, bf16[128,512]{1,0:T(8,128)(2,1)S(1)}, u32[]{:S(2)}, u32[]{:S(2)}) collective-permute-start(bf16[128,512]{1,0:T(8,128)(2,1)S(1)} %broadcast_select_fusion.2), channel_id=1, source_target_pairs={{0,64},{64,0},{1,65},{65,1},{2,66},{66,2},{3,67},{67,3},{4,68},{68... | collective-permute-start | bytes 393224 | tf_op jit(solution)/shard_map/ppermute | solution.py:31
  39.9 36.5 %all-gather.9 = f16[512,2560]{1,0:T(8,128)(2,1)S(1)} all-gather(f16[16,2560]{1,0:T(8,128)(2,1)S(1)} %pad_maximum_fusion.2), channel_id=1, replica_groups=mesh['rep'=4,'xh'=2,'xl'=2,'z'=16,'core'=2] {'z','core'}, dimensions={0}, use_global_device_ids=true | all-gather | bytes 2703360 | tf_op jit(solution)/shard_map/all_gather | solution.py:195
  76.5 2.0 convolution_convert_fusion
  78.5 4.6 %all-to-all-start = ((bf16[8,32,2048]{2,1,0:T(8,128)(2,1)}), bf16[8,32,2048]{2,1,0:T(8,128)(2,1)}, u32[]{:S(2)}, u32[]{:S(2)}) async-start(bf16[8,32,2048]{2,1,0:T(8,128)(2,1)} %bitcast.113), calls=%async_computation | async-start | bytes 2097152 | tf_op jit(solution)/shard_map/all_to_all | solution.py:208
  85.0 15.1 %all-to-all-done = bf16[8,32,2048]{2,1,0:T(8,128)(2,1)} async-done(((bf16[8,32,2048]{2,1,0:T(8,128)(2,1)}), bf16[8,32,2048]{2,1,0:T(8,128)(2,1)}, u32[]{:S(2)}, u32[]{:S(2)}) %all-to-all-start) | async-done | bytes 1048608 | tf_op jit(solution)/shard_map/all_to_all | solution.py:208
  101.1 1.4 convert_reduce_fusion
  102.8 45.4 %all-gather.10 = f16[1024,2048]{1,0:T(8,128)(2,1)S(1)} all-gather(f16[32,2048]{1,0:T(8,128)(2,1)S(1)} %fusion.41), channel_id=1, replica_groups=mesh['rep'=4,'xh'=2,'xl'=2,'z'=16,'core'=2] {'z','core'}, dimensions={0}, use_global_device_ids=true | all-gather | bytes 4325376 | tf_op jit(solution)/shard_map/all_gather | solution.py:215
  148.2 1.9 fusion.5
  150.1 24.3 %all_to_all.32 = bf16[4,96,2048]{2,1,0:T(8,128)(2,1)} all-to-all(bf16[4,96,2048]{2,1,0:T(8,128)(2,1)S(1)} %bitcast.110), channel_id=1, replica_groups=mesh['rep'=4,'xh'=2,'xl'=2,'z'=16,'core'=2] {'xh','xl'}, dimensions={0} | all-to-all | bytes 3145728 | tf_op jit(solution)/shard_map/all_to_all | solution.py:255
  174.3 10.5 %shard_map.118 = bf16[384,2048]{1,0:T(8,128)(2,1)} custom-call(bf16[384,2048]{1,0:T(8,128)(2,1)} %bitcast.109, bf16[4,384,2048]{2,1,0:T(8,128)(2,1)} %bitcast.121, bf16[4,768,512]{2,1,0:T(8,128)(2,1)} %bitcast.122), custom_call_target="tpu_custom_call" | custom-call | flops 3623878656 | bytes 12582912 | tf_op jit(solution)/shard_map/pallas_call | solution.py:106
  184.8 4.8 %all-to-all-start.2 = ((bf16[8,48,2048]{2,1,0:T(8,128)(2,1)}), bf16[8,48,2048]{2,1,0:T(8,128)(2,1)S(1)}, u32[]{:S(2)}, u32[]{:S(2)}) async-start(bf16[8,48,2048]{2,1,0:T(8,128)(2,1)} %bitcast.108), calls=%async_computation.2 | async-start | bytes 3145728 | tf_op jit(solution)/shard_map/all_to_all | solution.py:257
  191.3 19.0 %all-to-all-done.2 = bf16[8,48,2048]{2,1,0:T(8,128)(2,1)S(1)} async-done(((bf16[8,48,2048]{2,1,0:T(8,128)(2,1)}), bf16[8,48,2048]{2,1,0:T(8,128)(2,1)S(1)}, u32[]{:S(2)}, u32[]{:S(2)}) %all-to-all-start.2) | async-done | bytes 1572896 | tf_op jit(solution)/shard_map/all_to_all | solution.py:257
  211.7 1.9 collective-permute-start.7
  213.7 5.5 %collective-permute-start.4 = (bf16[64,2048]{1,0:T(8,128)(2,1)S(1)}, bf16[64,2048]{1,0:T(8,128)(2,1)S(1)}, u32[]{:S(2)}, u32[]{:S(2)}) collective-permute-start(bf16[64,2048]{1,0:T(8,128)(2,1)S(1)} %concatenate.61), channel_id=1, source_target_pairs={{0,28},{2,30},{4,0},{6,2},{8,4},{10,6},{12,8},{14,10},{16,12},{18,... | collective-permute-start | bytes 786440 | tf_op jit(solution)/shard_map/ppermute | solution.py:31
  219.1 6.9 %collective-permute-done.7 = bf16[64,2048]{1,0:T(8,128)(2,1)S(1)} collective-permute-done((bf16[64,2048]{1,0:T(8,128)(2,1)S(1)}, bf16[64,2048]{1,0:T(8,128)(2,1)S(1)}, u32[]{:S(2)}, u32[]{:S(2)}) %collective-permute-start.7) | collective-permute-done | bytes 262176 | tf_op jit(solution)/shard_map/ppermute | solution.py:31
  226.1 1.9 collective-permute-start.8
  228.1 2.3 collective-permute-done.4
  230.4 6.4 %collective-permute-start.5 = (bf16[64,2048]{1,0:T(8,128)(2,1)S(1)}, bf16[64,2048]{1,0:T(8,128)(2,1)S(1)}, u32[]{:S(2)}, u32[]{:S(2)}) collective-permute-start(bf16[64,2048]{1,0:T(8,128)(2,1)S(1)} %add_convert_fusion.4), channel_id=1, source_target_pairs={{0,28},{2,30},{4,0},{6,2},{8,4},{10,6},{12,8},{14,10},{16,12},{18,... | collective-permute-start | bytes 786440 | tf_op jit(solution)/shard_map/ppermute | solution.py:31
  236.8 6.1 %collective-permute-done.8 = bf16[64,2048]{1,0:T(8,128)(2,1)S(1)} collective-permute-done((bf16[64,2048]{1,0:T(8,128)(2,1)S(1)}, bf16[64,2048]{1,0:T(8,128)(2,1)S(1)}, u32[]{:S(2)}, u32[]{:S(2)}) %collective-permute-start.8) | collective-permute-done | bytes 262176 | tf_op jit(solution)/shard_map/ppermute | solution.py:31
  243.0 1.9 collective-permute-start.9
  244.9 1.9 collective-permute-done.5
  246.9 6.4 %collective-permute-start.6 = (bf16[64,2048]{1,0:T(8,128)(2,1)S(1)}, bf16[64,2048]{1,0:T(8,128)(2,1)S(1)}, u32[]{:S(2)}, u32[]{:S(2)}) collective-permute-start(bf16[64,2048]{1,0:T(8,128)(2,1)S(1)} %add_convert_fusion.3), channel_id=1, source_target_pairs={{0,28},{2,30},{4,0},{6,2},{8,4},{10,6},{12,8},{14,10},{16,12},{18,... | collective-permute-start | bytes 786440 | tf_op jit(solution)/shard_map/ppermute | solution.py:31
  253.3 4.1 %collective-permute-done.9 = bf16[64,2048]{1,0:T(8,128)(2,1)S(1)} collective-permute-done((bf16[64,2048]{1,0:T(8,128)(2,1)S(1)}, bf16[64,2048]{1,0:T(8,128)(2,1)S(1)}, u32[]{:S(2)}, u32[]{:S(2)}) %collective-permute-start.9) | collective-permute-done | bytes 262176 | tf_op jit(solution)/shard_map/ppermute | solution.py:31
  257.5 2.5 collective-permute-start.10
  260.0 1.9 collective-permute-start.11
  262.0 5.9 %collective-permute-start.12 = (bf16[32,2048]{1,0:T(8,128)(2,1)S(1)}, bf16[32,2048]{1,0:T(8,128)(2,1)S(1)}, u32[]{:S(2)}, u32[]{:S(2)}) collective-permute-start(bf16[32,2048]{1,0:T(8,128)(2,1)S(1)} %add_convert_fusion.6), channel_id=1, source_target_pairs={{0,30},{2,0},{4,2},{6,4},{8,6},{10,8},{12,10},{14,12},{16,14},{18,... | collective-permute-start | bytes 393224 | tf_op jit(solution)/shard_map/ppermute | solution.py:31
  268.9 1.8 collective-permute-done.11
  (111 shorter events, 13.2 us)
Async XLA Ops:
  6.5 20.1 %copy-start = (bf16[128,1024]{1,0:T(8,128)(2,1)S(1)}, bf16[128,1024]{1,0:T(8,128)(2,1)}, u32[]{:S(2)}) copy-start(bf16[128,1024]{1,0:T(8,128)(2,1)} %param.12) | copy-start | bytes 786436
  6.5 2.9 %copy-start.4 = (bf16[128,128]{1,0:T(8,128)(2,1)S(1)}, bf16[128,128]{1,0:T(8,128)(2,1)}, u32[]{:S(2)}) copy-start(bf16[128,128]{1,0:T(8,128)(2,1)} %param.13) | copy-start | bytes 98308
  6.5 2.9 %copy-start.3 = (bf16[128,128]{1,0:T(8,128)(2,1)S(1)}, bf16[128,128]{1,0:T(8,128)(2,1)}, u32[]{:S(2)}) copy-start(bf16[128,128]{1,0:T(8,128)(2,1)} %param.14) | copy-start | bytes 98308
  6.5 14.4 %copy-start.7 = (bf16[1,32,8]{1,2,0:T(8,128)(2,1)S(1)}, bf16[1,32,8]{1,2,0:T(8,128)(2,1)}, u32[]{:S(2)}) copy-start(bf16[1,32,8]{1,2,0:T(8,128)(2,1)} %param.23) | copy-start | bytes 1540
  6.5 14.4 %copy-start.6 = (s32[1,32,8]{1,2,0:T(8,128)S(1)}, s32[1,32,8]{1,2,0:T(8,128)}, u32[]{:S(2)}) copy-start(s32[1,32,8]{1,2,0:T(8,128)} %param.22) | copy-start | bytes 3076
  6.5 14.9 %copy-start.2 = (bf16[8,2048]{1,0:T(8,128)(2,1)S(1)}, bf16[8,2048]{1,0:T(8,128)(2,1)}, u32[]{:S(2)}) copy-start(bf16[8,2048]{1,0:T(8,128)(2,1)} %param.17) | copy-start | bytes 98308
  6.6 18.2 %copy-start.8 = (s32[128]{0:T(128)S(1)}, s32[128]{0:T(128)}, u32[]{:S(2)}) copy-start(s32[128]{0:T(128)} %param.15) | copy-start | bytes 1540
  6.6 93.5 %all-gather.6.cloned.1.call-start = ((), (), s32[]{:S(2)}) async-start(), calls=%async_computation.3 | async-start | bytes 7864320 | tf_op jit(solution)/shard_map/all_gather | solution.py:177
  17.9 8.7 %collective-permute-start = (bf16[256,256]{1,0:T(8,128)(2,1)S(1)}, bf16[256,256]{1,0:T(8,128)(2,1)S(1)}, u32[]{:S(2)}, u32[]{:S(2)}) collective-permute-start(bf16[256,256]{1,0:T(8,128)(2,1)S(1)} %all_gather.15), channel_id=1, source_target_pairs={{0,4},{2,6},{4,8},{6,10},{8,12},{10,14},{12,16},{14,18},{16,20},{1... | collective-permute-start | bytes 393224 | tf_op jit(solution)/shard_map/ppermute | solution.py:26
  19.1 7.4 %collective-permute-start.1 = (bf16[256,256]{1,0:T(8,128)(2,1)S(1)}, bf16[256,256]{1,0:T(8,128)(2,1)S(1)}, u32[]{:S(2)}, u32[]{:S(2)}) collective-permute-start(bf16[256,256]{1,0:T(8,128)(2,1)S(1)} %all_gather.15), channel_id=1, source_target_pairs={{0,2},{2,4},{4,6},{6,8},{8,10},{10,12},{12,14},{14,16},{16,18},{18... | collective-permute-start | bytes 393224 | tf_op jit(solution)/shard_map/ppermute | solution.py:26
  21.5 5.0 %collective-permute-start.3 = (f16[8,2560]{1,0:T(8,128)(2,1)S(1)}, f16[8,2560]{1,0:T(8,128)(2,1)S(1)}, u32[]{:S(2)}, u32[]{:S(2)}) collective-permute-start(f16[8,2560]{1,0:T(8,128)(2,1)S(1)} %constant_dynamic-update-slice_fusion.3), channel_id=1, source_target_pairs={{0,32},{32,0},{1,33},{33,1},{2,34},{34,2},{3,35},{35,3},{4,36},{36... | collective-permute-start | bytes 122888 | tf_op jit(solution)/shard_map/ppermute | solution.py:31
  29.0 47.4 %collective-permute-start.2 = (bf16[128,512]{1,0:T(8,128)(2,1)S(1)}, bf16[128,512]{1,0:T(8,128)(2,1)S(1)}, u32[]{:S(2)}, u32[]{:S(2)}) collective-permute-start(bf16[128,512]{1,0:T(8,128)(2,1)S(1)} %broadcast_select_fusion.2), channel_id=1, source_target_pairs={{0,64},{64,0},{1,65},{65,1},{2,66},{66,2},{3,67},{67,3},{4,68},{68... | collective-permute-start | bytes 393224 | tf_op jit(solution)/shard_map/ppermute | solution.py:31
  78.5 21.6 %all-to-all-start = ((bf16[8,32,2048]{2,1,0:T(8,128)(2,1)}), bf16[8,32,2048]{2,1,0:T(8,128)(2,1)}, u32[]{:S(2)}, u32[]{:S(2)}) async-start(bf16[8,32,2048]{2,1,0:T(8,128)(2,1)} %bitcast.113), calls=%async_computation | async-start | bytes 2097152 | tf_op jit(solution)/shard_map/all_to_all | solution.py:208
  83.1 1.7 copy-start.9
  83.1 91.2 %all-gather.8.cloned.1.call-start = ((), (), s32[]{:S(2)}) async-start(), calls=%async_computation.4 | async-start | bytes 3932160 | tf_op jit(solution)/shard_map/all_gather | solution.py:210
  84.3 18.2 %copy-start.1 = (bf16[1,32,2048]{2,1,0:T(8,128)(2,1)S(1)}, bf16[1,32,2048]{2,1,0:T(8,128)(2,1)}, u32[]{:S(2)}) copy-start(bf16[1,32,2048]{2,1,0:T(8,128)(2,1)} %param.16) | copy-start | bytes 393220
  84.9 17.8 %copy-start.5 = (f32[2048]{0:T(1024)S(1)}, f32[2048]{0:T(1024)}, u32[]{:S(2)}) copy-start(f32[2048]{0:T(1024)} %param.18) | copy-start | bytes 24580
  184.8 25.5 %all-to-all-start.2 = ((bf16[8,48,2048]{2,1,0:T(8,128)(2,1)}), bf16[8,48,2048]{2,1,0:T(8,128)(2,1)S(1)}, u32[]{:S(2)}, u32[]{:S(2)}) async-start(bf16[8,48,2048]{2,1,0:T(8,128)(2,1)} %bitcast.108), calls=%async_computation.2 | async-start | bytes 3145728 | tf_op jit(solution)/shard_map/all_to_all | solution.py:257
  211.7 14.4 %collective-permute-start.7 = (bf16[64,2048]{1,0:T(8,128)(2,1)S(1)}, bf16[64,2048]{1,0:T(8,128)(2,1)S(1)}, u32[]{:S(2)}, u32[]{:S(2)}) collective-permute-start(bf16[64,2048]{1,0:T(8,128)(2,1)S(1)} %pad_maximum_fusion.1), channel_id=1, source_target_pairs={{0,4},{2,6},{4,8},{6,10},{8,12},{10,14},{12,16},{14,18},{16,20},{1... | collective-permute-start | bytes 786440 | tf_op jit(solution)/shard_map/ppermute | solution.py:31
  213.7 16.7 %collective-permute-start.4 = (bf16[64,2048]{1,0:T(8,128)(2,1)S(1)}, bf16[64,2048]{1,0:T(8,128)(2,1)S(1)}, u32[]{:S(2)}, u32[]{:S(2)}) collective-permute-start(bf16[64,2048]{1,0:T(8,128)(2,1)S(1)} %concatenate.61), channel_id=1, source_target_pairs={{0,28},{2,30},{4,0},{6,2},{8,4},{10,6},{12,8},{14,10},{16,12},{18,... | collective-permute-start | bytes 786440 | tf_op jit(solution)/shard_map/ppermute | solution.py:31
  226.1 16.8 %collective-permute-start.8 = (bf16[64,2048]{1,0:T(8,128)(2,1)S(1)}, bf16[64,2048]{1,0:T(8,128)(2,1)S(1)}, u32[]{:S(2)}, u32[]{:S(2)}) collective-permute-start(bf16[64,2048]{1,0:T(8,128)(2,1)S(1)} %add_convert_fusion.2), channel_id=1, source_target_pairs={{0,4},{2,6},{4,8},{6,10},{8,12},{10,14},{12,16},{14,18},{16,20},{1... | collective-permute-start | bytes 786440 | tf_op jit(solution)/shard_map/ppermute | solution.py:31
  230.4 16.4 %collective-permute-start.5 = (bf16[64,2048]{1,0:T(8,128)(2,1)S(1)}, bf16[64,2048]{1,0:T(8,128)(2,1)S(1)}, u32[]{:S(2)}, u32[]{:S(2)}) collective-permute-start(bf16[64,2048]{1,0:T(8,128)(2,1)S(1)} %add_convert_fusion.4), channel_id=1, source_target_pairs={{0,28},{2,30},{4,0},{6,2},{8,4},{10,6},{12,8},{14,10},{16,12},{18,... | collective-permute-start | bytes 786440 | tf_op jit(solution)/shard_map/ppermute | solution.py:31
  243.0 14.4 %collective-permute-start.9 = (bf16[64,2048]{1,0:T(8,128)(2,1)S(1)}, bf16[64,2048]{1,0:T(8,128)(2,1)S(1)}, u32[]{:S(2)}, u32[]{:S(2)}) collective-permute-start(bf16[64,2048]{1,0:T(8,128)(2,1)S(1)} %add_convert_fusion.1), channel_id=1, source_target_pairs={{0,4},{2,6},{4,8},{6,10},{8,12},{10,14},{12,16},{14,18},{16,20},{1... | collective-permute-start | bytes 786440 | tf_op jit(solution)/shard_map/ppermute | solution.py:31
  246.9 15.0 %collective-permute-start.6 = (bf16[64,2048]{1,0:T(8,128)(2,1)S(1)}, bf16[64,2048]{1,0:T(8,128)(2,1)S(1)}, u32[]{:S(2)}, u32[]{:S(2)}) collective-permute-start(bf16[64,2048]{1,0:T(8,128)(2,1)S(1)} %add_convert_fusion.3), channel_id=1, source_target_pairs={{0,28},{2,30},{4,0},{6,2},{8,4},{10,6},{12,8},{14,10},{16,12},{18,... | collective-permute-start | bytes 786440 | tf_op jit(solution)/shard_map/ppermute | solution.py:31
  257.5 11.4 %collective-permute-start.10 = (bf16[32,2048]{1,0:T(8,128)(2,1)S(1)}, bf16[32,2048]{1,0:T(8,128)(2,1)S(1)}, u32[]{:S(2)}, u32[]{:S(2)}) collective-permute-start(bf16[32,2048]{1,0:T(8,128)(2,1)S(1)} %get-tuple-element.29), channel_id=1, source_target_pairs={{0,4},{2,6},{4,8},{6,10},{8,12},{10,14},{12,16},{14,18},{16,20},{1... | collective-permute-start | bytes 393224 | tf_op jit(solution)/shard_map/ppermute | solution.py:31
  260.0 10.7 %collective-permute-start.11 = (bf16[32,2048]{1,0:T(8,128)(2,1)S(1)}, bf16[32,2048]{1,0:T(8,128)(2,1)S(1)}, u32[]{:S(2)}, u32[]{:S(2)}) collective-permute-start(bf16[32,2048]{1,0:T(8,128)(2,1)S(1)} %get-tuple-element.30), channel_id=1, source_target_pairs={{0,2},{2,4},{4,6},{6,8},{8,10},{10,12},{12,14},{14,16},{16,18},{18... | collective-permute-start | bytes 393224 | tf_op jit(solution)/shard_map/ppermute | solution.py:31
  262.0 8.7 %collective-permute-start.12 = (bf16[32,2048]{1,0:T(8,128)(2,1)S(1)}, bf16[32,2048]{1,0:T(8,128)(2,1)S(1)}, u32[]{:S(2)}, u32[]{:S(2)}) collective-permute-start(bf16[32,2048]{1,0:T(8,128)(2,1)S(1)} %add_convert_fusion.6), channel_id=1, source_target_pairs={{0,30},{2,0},{4,2},{6,4},{8,6},{10,8},{12,10},{14,12},{16,14},{18,... | collective-permute-start | bytes 393224 | tf_op jit(solution)/shard_map/ppermute | solution.py:31
Sparse Core Ops, SparseCore 0:
  9.5 79.6 all-gather.5
  100.2 49.2 all-gather.7

commit v5 on v4

--- a/solution.py
+++ b/solution.py
@@ -70,61 +70,60 @@
     return match, jnp.where(hit, rank, -1)
 
 
-def expert_kernel(parts, rows_ref, gate_up_ref, down_ref, out_ref, gu_ref, dn_ref, hidden_ref, sems):
-    units, cols = gu_ref.shape[1] // 2, dn_ref.shape[2]
-    copies = [
-        pltpu.make_async_copy(gate_up_ref.at[part], gu_ref.at[part], sems.at[part])
-        for part in range(parts)
-    ] + [
-        pltpu.make_async_copy(down_ref.at[part], dn_ref.at[part], sems.at[parts + part])
-        for part in range(parts)
-    ]
+def expert_kernel(chunk, rows_ref, gate_ref, up_ref, down_ref, *refs):
+    out_ref, gate_vm, up_vm, down_vm, hidden_ref, sems = refs
+    units, parts = gate_ref.shape[0], down_ref.shape[0]
+    cols = down_ref.shape[2]
+    steps = units // chunk
+    copies = []
+    for step in range(steps):
+        at = pl.ds(step * chunk, chunk)
+        copies.append((gate_ref.at[at], gate_vm.at[at]))
+        copies.append((up_ref.at[at], up_vm.at[at]))
+    for part in range(parts):
+        copies.append((down_ref.at[part], down_vm.at[part]))
+    copies = [pltpu.make_async_copy(*pair, sems.at[i]) for i, pair in enumerate(copies)]
     for copy in copies:
         copy.start()
     rows = rows_ref[...]
-    for part in range(0, parts, 2):
-        copies[part].wait()
-        copies[part + 1].wait()
-        both = gu_ref[part : part + 2].reshape(4 * units, rows.shape[1])
-        act = contract(rows, both, ((1,), (1,)))
-        for k in range(2):
-            gate = act[:, 2 * k * units : (2 * k + 1) * units]
-            up = act[:, (2 * k + 1) * units : (2 * k + 2) * units]
-            hidden = (gate / (1.0 + jnp.exp(-gate)) * up).astype(BF)
-            hidden_ref[:, (part + k) * units : (part + k + 1) * units] = hidden
+    for step in range(steps):
+        copies[2 * step].wait()
+        copies[2 * step + 1].wait()
+        at = slice(step * chunk, (step + 1) * chunk)
+        gate = contract(rows, gate_vm[at], ((1,), (1,)))
+        up = contract(rows, up_vm[at], ((1,), (1,)))
+        hidden_ref[:, at] = (gate / (1.0 + jnp.exp(-gate)) * up).astype(BF)
     hidden = hidden_ref[...]
     for part in range(parts):
-        copies[parts + part].wait()
-        total = jnp.dot(hidden, dn_ref[part], preferred_element_type=F32)
+        copies[2 * steps + part].wait()
+        total = jnp.dot(hidden, down_vm[part], preferred_element_type=F32)
         out_ref[:, part * cols : (part + 1) * cols] = total.astype(BF)
 
 
-def expert(rows, gate_up, down, parts):
+def expert(rows, gate, up, down, parts):
     count, width = rows.shape
-    gate_up = gate_up.reshape(parts, -1, width)
     down = down.reshape(parts, -1, down.shape[1])
+    chunk = min(256, gate.shape[0])
+    vmem, hbm = pl.BlockSpec(memory_space=pltpu.VMEM), pl.BlockSpec(memory_space=pltpu.HBM)
     return pl.pallas_call(
-        functools.partial(expert_kernel, parts),
-        in_specs=[
-            pl.BlockSpec(memory_space=pltpu.VMEM),
-            pl.BlockSpec(memory_space=pltpu.HBM),
-            pl.BlockSpec(memory_space=pltpu.HBM),
-        ],
-        out_specs=pl.BlockSpec(memory_space=pltpu.VMEM),
+        functools.partial(expert_kernel, chunk),
+        in_specs=[vmem, hbm, hbm, hbm],
+        out_specs=vmem,
         out_shape=jax.ShapeDtypeStruct((count, width), BF),
         scratch_shapes=[
-            pltpu.VMEM(gate_up.shape, BF),
+            pltpu.VMEM(gate.shape, BF),
+            pltpu.VMEM(up.shape, BF),
             pltpu.VMEM(down.shape, BF),
-            pltpu.VMEM((count, parts * gate_up.shape[1] // 2), BF),
-            pltpu.SemaphoreType.DMA((2 * parts,)),
+            pltpu.VMEM((count, gate.shape[0]), BF),
+            pltpu.SemaphoreType.DMA((2 * (gate.shape[0] // chunk) + parts,)),
         ],
         compiler_params=pltpu.CompilerParams(vmem_limit_bytes=VMEM_GRANT),
         cost_estimate=pl.CostEstimate(
-            flops=2 * count * (gate_up.size + down.size),
-            bytes_accessed=2 * (2 * rows.size + gate_up.size + down.size),
-            transcendentals=count * gate_up.shape[1] * parts // 2,
+            flops=2 * count * (gate.size + up.size + down.size),
+            bytes_accessed=2 * (2 * rows.size + gate.size + up.size + down.size),
+            transcendentals=count * gate.shape[0],
         ),
-    )(rows, gate_up, down)
+    )(rows, gate, up, down)
 
 
 def add_low(left, right):
@@ -173,16 +172,17 @@
     tok_sub, top = route_ids.shape[1], route_ids.shape[2]
     here = lax.axis_index("z")
 
-    gate_up = jnp.concatenate([gate_weight[0], up_weight[0]], 0)
-    gate_up = lax.all_gather(gate_up, "rep", axis=0, tiled=True)
-
+    gate_all = lax.all_gather(gate_weight[0], "rep", axis=0, tiled=True)
+    up_all = lax.all_gather(up_weight[0], "rep", axis=0, tiled=True)
+    down_all = lax.all_gather(down_weight[0], "rep", axis=0, tiled=True)
+
+    own_rows = out_weight.astype(F16)
+    pair_rows = jnp.concatenate([own_rows, shift(own_rows, "xl", 1)], 0)
     info = jnp.concatenate([route_ids[0].astype(F16), route_weights[0].astype(F16)], 1)
     info = jnp.pad(info, ((0, 0), (0, 128 - 2 * top)))
-    groups = tok_sub // rows8
-    own_rows = jnp.concatenate(
-        [out_weight.astype(F16)] + [info[g * rows8 : (g + 1) * rows8] for g in range(groups)], 1
-    )
-    pair_rows = jnp.concatenate([own_rows, shift(own_rows, "xl", 1)], 0)
+    groups = tok_sub // (2 * rows8)
+    info = [info[g * 2 * rows8 : (g + 1) * 2 * rows8] for g in range(groups)]
+    pair_rows = jnp.concatenate([pair_rows] + info, 1)
 
     attended = attention(queries, keys, values, doc_start)
     half = attended.shape[1] // 2
@@ -206,17 +206,14 @@
     both = jnp.dot(both, permute, preferred_element_type=F32).astype(BF)
     partial_value = jnp.dot(both, out_rows, preferred_element_type=F32).astype(BF)
     parts = lax.all_to_all(partial_value, ("rep", "xh"), split_axis=0, concat_axis=0, tiled=True)
-    parts, gate_up, down_weight = lax.optimization_barrier((parts, gate_up, down_weight))
-    down_all = lax.all_gather(down_weight[0], "rep", axis=0, tiled=True)
     head_total = jnp.sum(parts.reshape(-1, tok_sub, width).astype(F32), axis=0)
     hidden_sum = residual[0].astype(F32) + head_total
     inverse_rms = lax.rsqrt(jnp.mean(hidden_sum * hidden_sum, axis=-1, keepdims=True) + 1e-06)
     normed = (hidden_sum * inverse_rms * norm_gain).astype(BF)
     column = lax.all_gather(normed.astype(F16), ZC, axis=0, tiled=True).astype(BF)
 
-    table = z_all.reshape(nz * nc, 2, rows8, -1)[:, 0].reshape(nz * nc * rows8, -1)
-    table = [table[:, width + 128 * g :][:, : 2 * top].astype(F32) for g in range(groups)]
-    table = jnp.stack([jnp.transpose(t).reshape(2 * top, -1, rows8) for t in table], 2)
+    table = [z_all[:, width + 128 * g :][:, : 2 * top].astype(F32) for g in range(groups)]
+    table = jnp.stack([jnp.transpose(t).reshape(2 * top, -1, 2 * rows8) for t in table], 2)
     table = table.reshape(2 * top, -1)
     count = table.shape[1]
     core = lax.axis_index("core")
@@ -253,7 +250,7 @@
 
     send_rows = jnp.dot(send, column, preferred_element_type=F32).astype(BF)
     rows = lax.all_to_all(send_rows, X, split_axis=0, concat_axis=0, tiled=True)
-    expert_out = expert(rows, gate_up, down_all, nr)
+    expert_out = expert(rows, gate_all, up_all, down_all, nr)
     returned = lax.all_to_all(expert_out, XC, split_axis=0, concat_axis=0, tiled=True)
     mixed = contract(back, returned, ((0,), (0,))).astype(BF)
     expert_mix = ring_sums([mixed[k * tok_sub : (k + 1) * tok_sub] for k in range(nz)])

time: 282 us -> 278 us (0.986)
  transfers between devices with their start and end apart: 17 -> 18, of which waited for: 10 -> 7; matrix products, arithmetic and copies ran while one was open for 5% -> 6% of each run, Pallas kernels for 0% -> 0%
where the time goes in v5:
time: 278 us; the launch traced here: 277 us
  blocking collectives  113 us (41%)
  starting transfers between devices  60.8 us (22%)
  waiting for transfers between devices  60.6 us (22%)
  between operations  13.7 us (5%)
  Pallas kernels  9.21 us (3%)
  other arithmetic  7.74 us (3%)
  matrix products  7.41 us (3%)
  local copies, waits for them, and re-layouts  4.49 us (2%)
    ppermute x11, starting transfers between devices, shift(): lax.ppermute(value, axis, [(i, (i + by) % devices) for i in range(devices)])  48.4 us
    all_gather x1, blocking collectives, on_device(): lax.all_gather(normed.astype(F16), ZC, axis=0, tiled=True).astype(BF)  43.3 us
    all_gather x1, blocking collectives, on_device(): z_all = lax.all_gather(pair_rows, ZC, axis=0, tiled=True)  35.6 us
    all_to_all x1, blocking collectives, on_device(): rows = lax.all_to_all(send_rows, X, split_axis=0, concat_axis=0, tiled=True)  25.5 us
    ppermute x11, waiting for transfers between devices, shift(): lax.ppermute(value, axis, [(i, (i + by) % devices) for i in range(devices)])  25.2 us
    all_to_all x1, waiting for transfers between devices, on_device(): lax.all_to_all(expert_out, XC, split_axis=0, concat_axis=0, tiled=True)  18.9 us
    all_to_all x1, waiting for transfers between devices, on_device(): lax.all_to_all(partial_value, ('rep', 'xh'), split_axis=0, concat_axis=0,...  15.1 us
    pallas_call x1, Pallas kernels, expert(): pl.pallas_call(functools.partial(expert_kernel, chunk), in_specs=[vmem, h...  9.21 us
  transfers between devices with their start and end apart: 18, of which 7 were waited for; matrix products, arithmetic and copies ran while one was open for 6% of the time, Pallas kernels for 0%

profile of v5, /device:TPU:1, one launch (start us, length us, event | category | flops | bytes accessed | tf_op | source)
XLA Modules:
  0.0 276.8 jit_solution(494920291037635882)
XLA Ops:
  8.8 8.4 %all_gather.18 = bf16[256,256]{1,0:T(8,128)(2,1)S(1)} all-gather(bf16[128,256]{1,0:T(8,128)(2,1)S(1)} %pad_maximum_fusion.2), channel_id=1, replica_groups=mesh['rep'=4,'xh'=2,'xl'=2,'z'=16,'core'=2] {'core'}, dimensions={0}, use_global_device_ids=true | all-gather | bytes 196608 | tf_op jit(solution)/shard_map/all_gather | solution.py:43
  17.3 1.3 collective-permute-start
  18.6 1.8 collective-permute-start.1
  21.1 3.1 %collective-permute-start.3 = (f16[8,2048]{1,0:T(8,128)(2,1)S(1)}, f16[8,2048]{1,0:T(8,128)(2,1)S(1)}, u32[]{:S(2)}, u32[]{:S(2)}) collective-permute-start(f16[8,2048]{1,0:T(8,128)(2,1)S(1)} %convert_element_type.174), channel_id=1, source_target_pairs={{0,32},{32,0},{1,33},{33,1},{2,34},{34,2},{3,35},{35,3},{4,36},{36... | collective-permute-start | bytes 98312 | tf_op jit(solution)/shard_map/ppermute | solution.py:31
  25.8 0.8 compare_and_fusion
  28.3 0.9 fusion.29
  29.5 9.8 %collective-permute-start.2 = (bf16[128,512]{1,0:T(8,128)(2,1)S(1)}, bf16[128,512]{1,0:T(8,128)(2,1)S(1)}, u32[]{:S(2)}, u32[]{:S(2)}) collective-permute-start(bf16[128,512]{1,0:T(8,128)(2,1)S(1)} %broadcast_select_fusion.2), channel_id=1, source_target_pairs={{0,64},{64,0},{1,65},{65,1},{2,66},{66,2},{3,67},{67,3},{4,68},{68... | collective-permute-start | bytes 393224 | tf_op jit(solution)/shard_map/ppermute | solution.py:31
  39.3 35.6 %all-gather.14 = f16[512,2304]{1,0:T(8,128)(2,1)S(1)} all-gather(f16[16,2304]{1,0:T(8,128)(2,1)S(1)} %pad_maximum_fusion.1), channel_id=1, replica_groups=mesh['rep'=4,'xh'=2,'xl'=2,'z'=16,'core'=2] {'z','core'}, dimensions={0}, use_global_device_ids=true | all-gather | bytes 2433024 | tf_op jit(solution)/shard_map/all_gather | solution.py:195
  75.0 2.0 convolution_convert_fusion
  77.0 4.5 %all-to-all-start = ((bf16[8,32,2048]{2,1,0:T(8,128)(2,1)}), bf16[8,32,2048]{2,1,0:T(8,128)(2,1)S(1)}, u32[]{:S(2)}, u32[]{:S(2)}) async-start(bf16[8,32,2048]{2,1,0:T(8,128)(2,1)} %bitcast.93), calls=%async_computation | async-start | bytes 2097152 | tf_op jit(solution)/shard_map/all_to_all | solution.py:208
  81.5 1.1 fusion.79
  85.9 15.1 %all-to-all-done = bf16[8,32,2048]{2,1,0:T(8,128)(2,1)S(1)} async-done(((bf16[8,32,2048]{2,1,0:T(8,128)(2,1)}), bf16[8,32,2048]{2,1,0:T(8,128)(2,1)S(1)}, u32[]{:S(2)}, u32[]{:S(2)}) %all-to-all-start) | async-done | bytes 1048608 | tf_op jit(solution)/shard_map/all_to_all | solution.py:208
  101.4 43.3 %all-gather.15 = f16[1024,2048]{1,0:T(8,128)(2,1)S(1)} all-gather(f16[32,2048]{1,0:T(8,128)(2,1)S(1)} %fusion.41), channel_id=1, replica_groups=mesh['rep'=4,'xh'=2,'xl'=2,'z'=16,'core'=2] {'z','core'}, dimensions={0}, use_global_device_ids=true | all-gather | bytes 4325376 | tf_op jit(solution)/shard_map/all_gather | solution.py:213
  144.8 1.9 fusion.5
  146.6 25.5 %all_to_all.29 = bf16[4,96,2048]{2,1,0:T(8,128)(2,1)} all-to-all(bf16[4,96,2048]{2,1,0:T(8,128)(2,1)S(1)} %bitcast.92), channel_id=1, replica_groups=mesh['rep'=4,'xh'=2,'xl'=2,'z'=16,'core'=2] {'xh','xl'}, dimensions={0} | all-to-all | bytes 3145728 | tf_op jit(solution)/shard_map/all_to_all | solution.py:252
  172.2 9.2 %shard_map.118 = bf16[384,2048]{1,0:T(8,128)(2,1)} custom-call(bf16[384,2048]{1,0:T(8,128)(2,1)} %bitcast.91, bf16[768,2048]{1,0:T(8,128)(2,1)} %bitcast.101, bf16[768,2048]{1,0:T(8,128)(2,1)} %bitcast.102, bf16[4,768,512]{2,1,0:T(8,128)(2,1)} %bitcast.103), custom_call_target="tpu_custom_call" | custom-call | flops 3623878656 | bytes 12582912 | tf_op jit(solution)/shard_map/pallas_call | solution.py:108
  181.4 4.7 %all-to-all-start.2 = ((bf16[8,48,2048]{2,1,0:T(8,128)(2,1)}), bf16[8,48,2048]{2,1,0:T(8,128)(2,1)S(1)}, u32[]{:S(2)}, u32[]{:S(2)}) async-start(bf16[8,48,2048]{2,1,0:T(8,128)(2,1)} %bitcast.90), calls=%async_computation.2 | async-start | bytes 3145728 | tf_op jit(solution)/shard_map/all_to_all | solution.py:254
  188.0 18.9 %all-to-all-done.2 = bf16[8,48,2048]{2,1,0:T(8,128)(2,1)S(1)} async-done(((bf16[8,48,2048]{2,1,0:T(8,128)(2,1)}), bf16[8,48,2048]{2,1,0:T(8,128)(2,1)S(1)}, u32[]{:S(2)}, u32[]{:S(2)}) %all-to-all-start.2) | async-done | bytes 1572896 | tf_op jit(solution)/shard_map/all_to_all | solution.py:254
  206.9 1.3 bitcast_convert_fusion
  208.3 2.3 collective-permute-start.7
  210.6 5.1 %collective-permute-start.4 = (bf16[64,2048]{1,0:T(8,128)(2,1)S(1)}, bf16[64,2048]{1,0:T(8,128)(2,1)S(1)}, u32[]{:S(2)}, u32[]{:S(2)}) collective-permute-start(bf16[64,2048]{1,0:T(8,128)(2,1)S(1)} %concatenate.57), channel_id=1, source_target_pairs={{0,28},{2,30},{4,0},{6,2},{8,4},{10,6},{12,8},{14,10},{16,12},{18,... | collective-permute-start | bytes 786440 | tf_op jit(solution)/shard_map/ppermute | solution.py:31
  215.7 4.6 %collective-permute-done.7 = bf16[64,2048]{1,0:T(8,128)(2,1)S(1)} collective-permute-done((bf16[64,2048]{1,0:T(8,128)(2,1)S(1)}, bf16[64,2048]{1,0:T(8,128)(2,1)S(1)}, u32[]{:S(2)}, u32[]{:S(2)}) %collective-permute-start.7) | collective-permute-done | bytes 262176 | tf_op jit(solution)/shard_map/ppermute | solution.py:31
  220.4 1.9 collective-permute-start.8
  222.4 4.3 %collective-permute-done.4 = bf16[64,2048]{1,0:T(8,128)(2,1)S(1)} collective-permute-done((bf16[64,2048]{1,0:T(8,128)(2,1)S(1)}, bf16[64,2048]{1,0:T(8,128)(2,1)S(1)}, u32[]{:S(2)}, u32[]{:S(2)}) %collective-permute-start.4) | collective-permute-done | bytes 262176 | tf_op jit(solution)/shard_map/ppermute | solution.py:31
  226.8 4.0 %collective-permute-start.5 = (bf16[64,2048]{1,0:T(8,128)(2,1)S(1)}, bf16[64,2048]{1,0:T(8,128)(2,1)S(1)}, u32[]{:S(2)}, u32[]{:S(2)}) collective-permute-start(bf16[64,2048]{1,0:T(8,128)(2,1)S(1)} %add_convert_fusion.4), channel_id=1, source_target_pairs={{0,28},{2,30},{4,0},{6,2},{8,4},{10,6},{12,8},{14,10},{16,12},{18,... | collective-permute-start | bytes 786440 | tf_op jit(solution)/shard_map/ppermute | solution.py:31
  230.8 4.5 %collective-permute-start.9 = (bf16[64,2048]{1,0:T(8,128)(2,1)S(1)}, bf16[64,2048]{1,0:T(8,128)(2,1)S(1)}, u32[]{:S(2)}, u32[]{:S(2)}) collective-permute-start(bf16[64,2048]{1,0:T(8,128)(2,1)S(1)} %add_convert_fusion.1), channel_id=1, source_target_pairs={{0,4},{2,6},{4,8},{6,10},{8,12},{10,14},{12,16},{14,18},{16,20},{1... | collective-permute-start | bytes 786440 | tf_op jit(solution)/shard_map/ppermute | solution.py:31
  235.3 10.1 %collective-permute-done.5 = bf16[64,2048]{1,0:T(8,128)(2,1)S(1)} collective-permute-done((bf16[64,2048]{1,0:T(8,128)(2,1)S(1)}, bf16[64,2048]{1,0:T(8,128)(2,1)S(1)}, u32[]{:S(2)}, u32[]{:S(2)}) %collective-permute-start.5) | collective-permute-done | bytes 262176 | tf_op jit(solution)/shard_map/ppermute | solution.py:31
  245.5 1.9 collective-permute-start.6
  247.5 9.3 %collective-permute-start.10 = (bf16[32,2048]{1,0:T(8,128)(2,1)S(1)}, bf16[32,2048]{1,0:T(8,128)(2,1)S(1)}, u32[]{:S(2)}, u32[]{:S(2)}) collective-permute-start(bf16[32,2048]{1,0:T(8,128)(2,1)S(1)} %get-tuple-element.19), channel_id=1, source_target_pairs={{0,4},{2,6},{4,8},{6,10},{8,12},{10,14},{12,16},{14,18},{16,20},{1... | collective-permute-start | bytes 393224 | tf_op jit(solution)/shard_map/ppermute | solution.py:31
  256.8 1.9 collective-permute-start.11
  258.8 4.6 %collective-permute-start.12 = (bf16[32,2048]{1,0:T(8,128)(2,1)S(1)}, bf16[32,2048]{1,0:T(8,128)(2,1)S(1)}, u32[]{:S(2)}, u32[]{:S(2)}) collective-permute-start(bf16[32,2048]{1,0:T(8,128)(2,1)S(1)} %add_convert_fusion.6), channel_id=1, source_target_pairs={{0,30},{2,0},{4,2},{6,4},{8,6},{10,8},{12,10},{14,12},{16,14},{18,... | collective-permute-start | bytes 393224 | tf_op jit(solution)/shard_map/ppermute | solution.py:31
  263.8 5.8 %collective-permute-done.12 = bf16[32,2048]{1,0:T(8,128)(2,1)S(1)} collective-permute-done((bf16[32,2048]{1,0:T(8,128)(2,1)S(1)}, bf16[32,2048]{1,0:T(8,128)(2,1)S(1)}, u32[]{:S(2)}, u32[]{:S(2)}) %collective-permute-start.12) | collective-permute-done | bytes 131104 | tf_op jit(solution)/shard_map/ppermute | solution.py:31
  (93 shorter events, 13.6 us)
Async XLA Ops:
  6.5 20.5 %copy-start = (bf16[128,1024]{1,0:T(8,128)(2,1)S(1)}, bf16[128,1024]{1,0:T(8,128)(2,1)}, u32[]{:S(2)}) copy-start(bf16[128,1024]{1,0:T(8,128)(2,1)} %param.12) | copy-start | bytes 786436
  6.5 165.6 %all-gather.9.cloned.1.call-start = ((), (), s32[]{:S(2)}) async-start(), calls=%async_computation.3 | async-start | bytes 3932160 | tf_op jit(solution)/shard_map/all_gather | solution.py:175
  7.3 164.9 %all-gather.11.cloned.1.call-start = ((), (), s32[]{:S(2)}) async-start(), calls=%async_computation.4 | async-start | bytes 3932160 | tf_op jit(solution)/shard_map/all_gather | solution.py:176
  8.0 164.2 %all-gather.13.cloned.1.call-start = ((), (), s32[]{:S(2)}) async-start(), calls=%async_computation.5 | async-start | bytes 3932160 | tf_op jit(solution)/shard_map/all_gather | solution.py:177
  17.3 9.7 %collective-permute-start = (bf16[256,256]{1,0:T(8,128)(2,1)S(1)}, bf16[256,256]{1,0:T(8,128)(2,1)S(1)}, u32[]{:S(2)}, u32[]{:S(2)}) collective-permute-start(bf16[256,256]{1,0:T(8,128)(2,1)S(1)} %all_gather.18), channel_id=1, source_target_pairs={{0,4},{2,6},{4,8},{6,10},{8,12},{10,14},{12,16},{14,18},{16,20},{1... | collective-permute-start | bytes 393224 | tf_op jit(solution)/shard_map/ppermute | solution.py:26
  18.6 8.4 %collective-permute-start.1 = (bf16[256,256]{1,0:T(8,128)(2,1)S(1)}, bf16[256,256]{1,0:T(8,128)(2,1)S(1)}, u32[]{:S(2)}, u32[]{:S(2)}) collective-permute-start(bf16[256,256]{1,0:T(8,128)(2,1)S(1)} %all_gather.18), channel_id=1, source_target_pairs={{0,2},{2,4},{4,6},{6,8},{8,10},{10,12},{12,14},{14,16},{16,18},{18... | collective-permute-start | bytes 393224 | tf_op jit(solution)/shard_map/ppermute | solution.py:26
  21.1 5.8 %collective-permute-start.3 = (f16[8,2048]{1,0:T(8,128)(2,1)S(1)}, f16[8,2048]{1,0:T(8,128)(2,1)S(1)}, u32[]{:S(2)}, u32[]{:S(2)}) collective-permute-start(f16[8,2048]{1,0:T(8,128)(2,1)S(1)} %convert_element_type.174), channel_id=1, source_target_pairs={{0,32},{32,0},{1,33},{33,1},{2,34},{34,2},{3,35},{35,3},{4,36},{36... | collective-permute-start | bytes 98312 | tf_op jit(solution)/shard_map/ppermute | solution.py:31
  29.5 45.4 %collective-permute-start.2 = (bf16[128,512]{1,0:T(8,128)(2,1)S(1)}, bf16[128,512]{1,0:T(8,128)(2,1)S(1)}, u32[]{:S(2)}, u32[]{:S(2)}) collective-permute-start(bf16[128,512]{1,0:T(8,128)(2,1)S(1)} %broadcast_select_fusion.2), channel_id=1, source_target_pairs={{0,64},{64,0},{1,65},{65,1},{2,66},{66,2},{3,67},{67,3},{4,68},{68... | collective-permute-start | bytes 393224 | tf_op jit(solution)/shard_map/ppermute | solution.py:31
  74.9 2.1 copy-start.1
  77.0 24.0 %all-to-all-start = ((bf16[8,32,2048]{2,1,0:T(8,128)(2,1)}), bf16[8,32,2048]{2,1,0:T(8,128)(2,1)S(1)}, u32[]{:S(2)}, u32[]{:S(2)}) async-start(bf16[8,32,2048]{2,1,0:T(8,128)(2,1)} %bitcast.93), calls=%async_computation | async-start | bytes 2097152 | tf_op jit(solution)/shard_map/all_to_all | solution.py:208
  83.6 17.6 %copy-start.2 = (bf16[1,32,2048]{2,1,0:T(8,128)(2,1)S(1)}, bf16[1,32,2048]{2,1,0:T(8,128)(2,1)}, u32[]{:S(2)}) copy-start(bf16[1,32,2048]{2,1,0:T(8,128)(2,1)} %param.16) | copy-start | bytes 393220
  84.4 17.0 %copy-start.3 = (f32[2048]{0:T(1024)S(1)}, f32[2048]{0:T(1024)}, u32[]{:S(2)}) copy-start(f32[2048]{0:T(1024)} %param.18) | copy-start | bytes 24580
  181.4 25.5 %all-to-all-start.2 = ((bf16[8,48,2048]{2,1,0:T(8,128)(2,1)}), bf16[8,48,2048]{2,1,0:T(8,128)(2,1)S(1)}, u32[]{:S(2)}, u32[]{:S(2)}) async-start(bf16[8,48,2048]{2,1,0:T(8,128)(2,1)} %bitcast.90), calls=%async_computation.2 | async-start | bytes 3145728 | tf_op jit(solution)/shard_map/all_to_all | solution.py:254
  208.3 12.1 %collective-permute-start.7 = (bf16[64,2048]{1,0:T(8,128)(2,1)S(1)}, bf16[64,2048]{1,0:T(8,128)(2,1)S(1)}, u32[]{:S(2)}, u32[]{:S(2)}) collective-permute-start(bf16[64,2048]{1,0:T(8,128)(2,1)S(1)} %pad_maximum_fusion), channel_id=1, source_target_pairs={{0,4},{2,6},{4,8},{6,10},{8,12},{10,14},{12,16},{14,18},{16,20},{1... | collective-permute-start | bytes 786440 | tf_op jit(solution)/shard_map/ppermute | solution.py:31
  210.6 16.1 %collective-permute-start.4 = (bf16[64,2048]{1,0:T(8,128)(2,1)S(1)}, bf16[64,2048]{1,0:T(8,128)(2,1)S(1)}, u32[]{:S(2)}, u32[]{:S(2)}) collective-permute-start(bf16[64,2048]{1,0:T(8,128)(2,1)S(1)} %concatenate.57), channel_id=1, source_target_pairs={{0,28},{2,30},{4,0},{6,2},{8,4},{10,6},{12,8},{14,10},{16,12},{18,... | collective-permute-start | bytes 786440 | tf_op jit(solution)/shard_map/ppermute | solution.py:31
  220.4 10.3 %collective-permute-start.8 = (bf16[64,2048]{1,0:T(8,128)(2,1)S(1)}, bf16[64,2048]{1,0:T(8,128)(2,1)S(1)}, u32[]{:S(2)}, u32[]{:S(2)}) collective-permute-start(bf16[64,2048]{1,0:T(8,128)(2,1)S(1)} %add_convert_fusion.2), channel_id=1, source_target_pairs={{0,4},{2,6},{4,8},{6,10},{8,12},{10,14},{12,16},{14,18},{16,20},{1... | collective-permute-start | bytes 786440 | tf_op jit(solution)/shard_map/ppermute | solution.py:31
  226.8 18.6 %collective-permute-start.5 = (bf16[64,2048]{1,0:T(8,128)(2,1)S(1)}, bf16[64,2048]{1,0:T(8,128)(2,1)S(1)}, u32[]{:S(2)}, u32[]{:S(2)}) collective-permute-start(bf16[64,2048]{1,0:T(8,128)(2,1)S(1)} %add_convert_fusion.4), channel_id=1, source_target_pairs={{0,28},{2,30},{4,0},{6,2},{8,4},{10,6},{12,8},{14,10},{16,12},{18,... | collective-permute-start | bytes 786440 | tf_op jit(solution)/shard_map/ppermute | solution.py:31
  230.8 16.6 %collective-permute-start.9 = (bf16[64,2048]{1,0:T(8,128)(2,1)S(1)}, bf16[64,2048]{1,0:T(8,128)(2,1)S(1)}, u32[]{:S(2)}, u32[]{:S(2)}) collective-permute-start(bf16[64,2048]{1,0:T(8,128)(2,1)S(1)} %add_convert_fusion.1), channel_id=1, source_target_pairs={{0,4},{2,6},{4,8},{6,10},{8,12},{10,14},{12,16},{14,18},{16,20},{1... | collective-permute-start | bytes 786440 | tf_op jit(solution)/shard_map/ppermute | solution.py:31
  245.5 13.3 %collective-permute-start.6 = (bf16[64,2048]{1,0:T(8,128)(2,1)S(1)}, bf16[64,2048]{1,0:T(8,128)(2,1)S(1)}, u32[]{:S(2)}, u32[]{:S(2)}) collective-permute-start(bf16[64,2048]{1,0:T(8,128)(2,1)S(1)} %add_convert_fusion.3), channel_id=1, source_target_pairs={{0,28},{2,30},{4,0},{6,2},{8,4},{10,6},{12,8},{14,10},{16,12},{18,... | collective-permute-start | bytes 786440 | tf_op jit(solution)/shard_map/ppermute | solution.py:31
  247.5 15.9 %collective-permute-start.10 = (bf16[32,2048]{1,0:T(8,128)(2,1)S(1)}, bf16[32,2048]{1,0:T(8,128)(2,1)S(1)}, u32[]{:S(2)}, u32[]{:S(2)}) collective-permute-start(bf16[32,2048]{1,0:T(8,128)(2,1)S(1)} %get-tuple-element.19), channel_id=1, source_target_pairs={{0,4},{2,6},{4,8},{6,10},{8,12},{10,14},{12,16},{14,18},{16,20},{1... | collective-permute-start | bytes 393224 | tf_op jit(solution)/shard_map/ppermute | solution.py:31
  256.8 6.9 %collective-permute-start.11 = (bf16[32,2048]{1,0:T(8,128)(2,1)S(1)}, bf16[32,2048]{1,0:T(8,128)(2,1)S(1)}, u32[]{:S(2)}, u32[]{:S(2)}) collective-permute-start(bf16[32,2048]{1,0:T(8,128)(2,1)S(1)} %get-tuple-element.20), channel_id=1, source_target_pairs={{0,2},{2,4},{4,6},{6,8},{8,10},{10,12},{12,14},{14,16},{16,18},{18... | collective-permute-start | bytes 393224 | tf_op jit(solution)/shard_map/ppermute | solution.py:31
  258.8 10.7 %collective-permute-start.12 = (bf16[32,2048]{1,0:T(8,128)(2,1)S(1)}, bf16[32,2048]{1,0:T(8,128)(2,1)S(1)}, u32[]{:S(2)}, u32[]{:S(2)}) collective-permute-start(bf16[32,2048]{1,0:T(8,128)(2,1)S(1)} %add_convert_fusion.6), channel_id=1, source_target_pairs={{0,30},{2,0},{4,2},{6,4},{8,6},{10,8},{12,10},{14,12},{16,14},{18,... | collective-permute-start | bytes 393224 | tf_op jit(solution)/shard_map/ppermute | solution.py:31
Sparse Core Ops, SparseCore 0:
  9.5 52.5 all-gather.8
  64.1 58.2 all-gather.10
  124.6 43.7 all-gather.12

commit v6 on v5

--- a/solution.py
+++ b/solution.py
@@ -61,17 +61,17 @@
     )
 
 
-def slot_ranks(ids, experts, core_of):
+def slot_ranks(ids, experts, class_of):
     match = ids[None] == experts[:, None, None]
     hit = jnp.any(match, axis=1)
     step = jnp.arange(ids.shape[1], dtype=jnp.int32)
-    before = (step[:, None] < step[None, :]) & (core_of[:, None] == core_of[None, :])
+    before = (step[:, None] < step[None, :]) & (class_of[:, None] == class_of[None, :])
     rank = jnp.dot(hit.astype(BF), before.astype(BF), preferred_element_type=F32).astype(jnp.int32)
     return match, jnp.where(hit, rank, -1)
 
 
-def expert_kernel(chunk, rows_ref, gate_ref, up_ref, down_ref, *refs):
-    out_ref, gate_vm, up_vm, down_vm, hidden_ref, sems = refs
+def expert_kernel(chunk, group, rows_ref, gate_ref, up_ref, down_ref, *refs):
+    far_ref, near_ref, gate_vm, up_vm, down_vm, hidden_ref, sems = refs
     units, parts = gate_ref.shape[0], down_ref.shape[0]
     cols = down_ref.shape[2]
     steps = units // chunk
@@ -83,33 +83,44 @@
     for part in range(parts):
         copies.append((down_ref.at[part], down_vm.at[part]))
     copies = [pltpu.make_async_copy(*pair, sems.at[i]) for i, pair in enumerate(copies)]
-    for copy in copies:
+    ahead = 4
+    for copy in copies[:ahead]:
         copy.start()
+
+    def arrived(i):
+        copies[i].wait()
+        if i + ahead < len(copies):
+            copies[i + ahead].start()
+
     rows = rows_ref[...]
     for step in range(steps):
-        copies[2 * step].wait()
-        copies[2 * step + 1].wait()
+        arrived(2 * step)
+        arrived(2 * step + 1)
         at = slice(step * chunk, (step + 1) * chunk)
         gate = contract(rows, gate_vm[at], ((1,), (1,)))
         up = contract(rows, up_vm[at], ((1,), (1,)))
         hidden_ref[:, at] = (gate / (1.0 + jnp.exp(-gate)) * up).astype(BF)
     hidden = hidden_ref[...]
     for part in range(parts):
-        copies[2 * steps + part].wait()
-        total = jnp.dot(hidden, down_vm[part], preferred_element_type=F32)
-        out_ref[:, part * cols : (part + 1) * cols] = total.astype(BF)
-
-
-def expert(rows, gate, up, down, parts):
+        arrived(2 * steps + part)
+        total = jnp.dot(hidden, down_vm[part], preferred_element_type=F32).astype(BF)
+        at = slice(part * cols, (part + 1) * cols)
+        for k in range(far_ref.shape[0] // group):
+            begin = 2 * k * group
+            far_ref[k * group : (k + 1) * group, at] = total[begin : begin + group]
+            near_ref[k * group : (k + 1) * group, at] = total[begin + group : begin + 2 * group]
+
+
+def expert(rows, gate, up, down, parts, group):
     count, width = rows.shape
     down = down.reshape(parts, -1, down.shape[1])
     chunk = min(256, gate.shape[0])
     vmem, hbm = pl.BlockSpec(memory_space=pltpu.VMEM), pl.BlockSpec(memory_space=pltpu.HBM)
     return pl.pallas_call(
-        functools.partial(expert_kernel, chunk),
+        functools.partial(expert_kernel, chunk, group),
         in_specs=[vmem, hbm, hbm, hbm],
-        out_specs=vmem,
-        out_shape=jax.ShapeDtypeStruct((count, width), BF),
+        out_specs=[vmem, vmem],
+        out_shape=[jax.ShapeDtypeStruct((count // 2, width), BF)] * 2,
         scratch_shapes=[
             pltpu.VMEM(gate.shape, BF),
             pltpu.VMEM(up.shape, BF),
@@ -130,23 +141,24 @@
     return (left.astype(F32) + right.astype(F32)).astype(BF)
 
 
-def ring_sums(chunks):
+def pair_up(chunks, k):
     places = len(chunks)
-
-    def two(k):
-        return jnp.concatenate([chunks[k % places], chunks[(k - 1) % places]], 0)
-
-    def two_back(k):
-        return jnp.concatenate([chunks[-k % places], chunks[(1 - k) % places]], 0)
-
+    return jnp.concatenate([chunks[k % places], chunks[(k - 1) % places]], 0)
+
+
+def pair_down(chunks, k):
+    places = len(chunks)
+    return jnp.concatenate([chunks[-k % places], chunks[(1 - k) % places]], 0)
+
+
+def ring_sums(chunks, right, left):
+    half = len(chunks) // 2
     rows = chunks[0].shape[0]
-    half = places // 2
-    right, left = two(half), two_back(half - 1)
     for k in range(half - 2, 0, -2):
-        right = add_low(shift(right, "z", 2), two(k))
+        right = add_low(shift(right, "z", 2), pair_up(chunks, k))
         left = shift(left, "z", -2)
         if k > 2:
-            left = add_low(left, two_back(k - 1))
+            left = add_low(left, pair_down(chunks, k - 1))
     last = shift(add_low(left[:rows], chunks[-1]), "z", -1)
     pieces = [left[rows:], shift(right[:rows], "z", 2), shift(right[rows:], "z", 1), last]
     return sum((p.astype(F32) for p in pieces), chunks[0].astype(F32))
@@ -217,14 +229,23 @@
     table = table.reshape(2 * top, -1)
     count = table.shape[1]
     core = lax.axis_index("core")
-    core_of = jnp.arange(count, dtype=jnp.int32) // tok_sub % nc
-    slot = jnp.arange(CAP * nz, dtype=jnp.int32)
+    lanes = jnp.arange(count, dtype=jnp.int32)
+    core_of = lanes // tok_sub % nc
+    near_places = list(range(nz - nz // 4 + 1, nz)) + list(range(nz // 4 + 1))
+    far_places = list(range(nz // 4 + 1, nz - nz // 4 + 1))
+    cap = CAP * nz // 2
+
+    def is_near(place):
+        offset = (place - here + nz) % nz
+        return ((offset <= nz // 4) | (offset > nz - nz // 4)).astype(jnp.int32)
+
+    near = is_near(lanes // (tok_sub * nc))
     ids = table[:top].astype(jnp.int32)
     experts = (jnp.arange(nx, dtype=jnp.int32) * nz + here) * nc + core
-    _, rank = slot_ranks(ids, experts, core_of)
-    seat = core_of[None, :] * slot.size + rank
+    _, rank = slot_ranks(ids, experts, near * nc + core_of)
+    seat = (near * nc + core_of)[None, :] * cap + rank
     seat = jnp.where(rank < 0, -1, seat)
-    seats = jnp.arange(nc * slot.size, dtype=jnp.int32)
+    seats = jnp.arange(2 * nc * cap, dtype=jnp.int32)
     send = (seat[:, None, :] == seats[None, :, None]).astype(BF).reshape(-1, count)
 
     table = table.reshape(2 * top, nz, nc, tok_sub)
@@ -233,27 +254,41 @@
     experts = ((lane // nc) * nz + here) * nc + lane % nc
     own_count = table.shape[1]
     match, rank = slot_ranks(
-        table[:top].astype(jnp.int32), experts, jnp.zeros((own_count,), jnp.int32)
+        table[:top].astype(jnp.int32),
+        experts,
+        is_near(jnp.arange(own_count, dtype=jnp.int32) // tok_sub),
     )
     gain = jnp.sum(jnp.where(match, table[None, top:], 0.0), axis=1)
 
-    def back_for(rank, gain):
-        back = jnp.where(rank[:, None, :] == slot[None, :, None], gain[:, None, :], 0.0)
-        return back.astype(BF).reshape(-1, own_count)
-
-    def from_here(value):
+    def blocks_of(value, places):
         value = value.reshape(-1, nz, tok_sub)
         value = lax.dynamic_slice_in_dim(jnp.concatenate([value, value], 1), here, nz, 1)
-        return value.reshape(-1, own_count)
-
-    back = back_for(from_here(rank), from_here(gain))
+        return jnp.concatenate([value[:, k] for k in places], 1)
+
+    def back_for(places):
+        slot = jnp.arange(cap, dtype=jnp.int32)
+        taken = blocks_of(rank, places)[:, None, :] == slot[None, :, None]
+        back = jnp.where(taken, blocks_of(gain, places)[:, None, :], 0.0)
+        return back.astype(BF).reshape(len(experts) * cap, -1)
+
+    backs = back_for(far_places), back_for(near_places)
 
     send_rows = jnp.dot(send, column, preferred_element_type=F32).astype(BF)
     rows = lax.all_to_all(send_rows, X, split_axis=0, concat_axis=0, tiled=True)
-    expert_out = expert(rows, gate_all, up_all, down_all, nr)
-    returned = lax.all_to_all(expert_out, XC, split_axis=0, concat_axis=0, tiled=True)
-    mixed = contract(back, returned, ((0,), (0,))).astype(BF)
-    expert_mix = ring_sums([mixed[k * tok_sub : (k + 1) * tok_sub] for k in range(nz)])
+    far, near = expert(rows, gate_all, up_all, down_all, nr, nc * cap)
+    chunks = [None] * nz
+
+    def spread_out(out, back, places):
+        returned = lax.all_to_all(out, XC, split_axis=0, concat_axis=0, tiled=True)
+        mixed = contract(back, returned, ((0,), (0,))).astype(BF)
+        for i, place in enumerate(places):
+            chunks[place] = mixed[i * tok_sub : (i + 1) * tok_sub]
+
+    spread_out(far, backs[0], far_places)
+    right, left = pair_up(chunks, nz // 2), pair_down(chunks, nz // 2 - 1)
+    right, left, near = lax.optimization_barrier((right, left, near))
+    spread_out(near, backs[1], near_places)
+    expert_mix = ring_sums(chunks, right, left)
     return (hidden_sum + expert_mix).astype(BF)[None]
 
 

time: 278 us -> 277 us (level)
  blocking collectives: 113 us -> 87.4 us
  waiting for transfers between devices: 60.6 us -> 75 us
  starting transfers between devices: 60.8 us -> 66 us
    all_to_all x1 -> x0, blocking collectives: 25.5 us -> none  [on_device(): rows = lax.all_to_all(send_rows, X, split_axis=0, concat_axis=0, tiled=True)]
    all_to_all x1 -> x3, waiting for transfers between devices: 18.9 us -> 30.6 us  [the longest x1 18.9 us: on_device(): rows = lax.all_to_all(send_rows, X, split_axis=0, concat_axis=0, tiled=True)]
    all_to_all x1 -> x3, starting transfers between devices: 4.75 us -> 14.6 us  [the longest x2 9.35 us: spread_out(): returned = lax.all_to_all(out, XC, split_axis=0, concat_axis=0, tiled=True)]
    ppermute x11, starting transfers between devices: 48.4 us -> 43.8 us  [shift(): lax.ppermute(value, axis, [(i, (i + by) % devices) for i in range(devices)])]
  transfers between devices with their start and end apart: 18 -> 20, of which waited for: 7 -> 8; matrix products, arithmetic and copies ran while one was open for 6% -> 7% of each run, Pallas kernels for 0% -> 0%
where the time goes in v6:
time: 277 us; the launch traced here: 274 us
  blocking collectives  87.4 us (32%)
  waiting for transfers between devices  75 us (27%)
  starting transfers between devices  66 us (24%)
  between operations  13.7 us (5%)
  Pallas kernels  9.2 us (3%)
  matrix products  8.36 us (3%)
  other arithmetic  7.73 us (3%)
  local copies, waits for them, and re-layouts  6.54 us (2%)
    ppermute x11, starting transfers between devices, shift(): lax.ppermute(value, axis, [(i, (i + by) % devices) for i in range(devices)])  43.8 us
    all_gather x1, blocking collectives, on_device(): lax.all_gather(normed.astype(F16), ZC, axis=0, tiled=True).astype(BF)  43.4 us
    all_gather x1, blocking collectives, on_device(): z_all = lax.all_gather(pair_rows, ZC, axis=0, tiled=True)  35.6 us
    ppermute x11, waiting for transfers between devices, shift(): lax.ppermute(value, axis, [(i, (i + by) % devices) for i in range(devices)])  27.9 us
    all_to_all x1, waiting for transfers between devices, on_device(): rows = lax.all_to_all(send_rows, X, split_axis=0, concat_axis=0, tiled=True)  18.9 us
    all_to_all x1, waiting for transfers between devices, on_device(): lax.all_to_all(partial_value, ('rep', 'xh'), split_axis=0, concat_axis=0,...  15.1 us
    all_to_all x2, waiting for transfers between devices, spread_out(): returned = lax.all_to_all(out, XC, split_axis=0, concat_axis=0, tiled=True)  11.7 us
    all_to_all x2, starting transfers between devices, spread_out(): returned = lax.all_to_all(out, XC, split_axis=0, concat_axis=0, tiled=True)  9.35 us
  transfers between devices with their start and end apart: 20, of which 8 were waited for; matrix products, arithmetic and copies ran while one was open for 7% of the time, Pallas kernels for 0%

profile of v6, /device:TPU:1, one launch (start us, length us, event | category | flops | bytes accessed | tf_op | source)
XLA Modules:
  0.0 274.0 jit_solution(563910352914654637)
XLA Ops:
  8.8 8.4 %all_gather.18 = bf16[256,256]{1,0:T(8,128)(2,1)S(1)} all-gather(bf16[128,256]{1,0:T(8,128)(2,1)S(1)} %pad_maximum_fusion.2), channel_id=1, replica_groups=mesh['rep'=4,'xh'=2,'xl'=2,'z'=16,'core'=2] {'core'}, dimensions={0}, use_global_device_ids=true | all-gather | bytes 196608 | tf_op jit(solution)/shard_map/all_gather | solution.py:43
  17.3 1.3 collective-permute-start
  18.6 1.8 collective-permute-start.1
  21.1 3.1 %collective-permute-start.3 = (f16[8,2048]{1,0:T(8,128)(2,1)S(1)}, f16[8,2048]{1,0:T(8,128)(2,1)S(1)}, u32[]{:S(2)}, u32[]{:S(2)}) collective-permute-start(f16[8,2048]{1,0:T(8,128)(2,1)S(1)} %convert_element_type.192), channel_id=1, source_target_pairs={{0,32},{32,0},{1,33},{33,1},{2,34},{34,2},{3,35},{35,3},{4,36},{36... | collective-permute-start | bytes 98312 | tf_op jit(solution)/shard_map/ppermute | solution.py:31
  29.5 9.8 %collective-permute-start.2 = (bf16[128,512]{1,0:T(8,128)(2,1)S(1)}, bf16[128,512]{1,0:T(8,128)(2,1)S(1)}, u32[]{:S(2)}, u32[]{:S(2)}) collective-permute-start(bf16[128,512]{1,0:T(8,128)(2,1)S(1)} %broadcast_select_fusion.2), channel_id=1, source_target_pairs={{0,64},{64,0},{1,65},{65,1},{2,66},{66,2},{3,67},{67,3},{4,68},{68... | collective-permute-start | bytes 393224 | tf_op jit(solution)/shard_map/ppermute | solution.py:31
  39.3 35.6 %all-gather.14 = f16[512,2304]{1,0:T(8,128)(2,1)S(1)} all-gather(f16[16,2304]{1,0:T(8,128)(2,1)S(1)} %pad_maximum_fusion.1), channel_id=1, replica_groups=mesh['rep'=4,'xh'=2,'xl'=2,'z'=16,'core'=2] {'z','core'}, dimensions={0}, use_global_device_ids=true | all-gather | bytes 2433024 | tf_op jit(solution)/shard_map/all_gather | solution.py:207
  75.0 2.0 convolution_convert_fusion
  77.0 4.5 %all-to-all-start = ((bf16[8,32,2048]{2,1,0:T(8,128)(2,1)}), bf16[8,32,2048]{2,1,0:T(8,128)(2,1)S(1)}, u32[]{:S(2)}, u32[]{:S(2)}) async-start(bf16[8,32,2048]{2,1,0:T(8,128)(2,1)} %bitcast.188), calls=%async_computation | async-start | bytes 2097152 | tf_op jit(solution)/shard_map/all_to_all | solution.py:220
  85.9 15.1 %all-to-all-done = bf16[8,32,2048]{2,1,0:T(8,128)(2,1)S(1)} async-done(((bf16[8,32,2048]{2,1,0:T(8,128)(2,1)}), bf16[8,32,2048]{2,1,0:T(8,128)(2,1)S(1)}, u32[]{:S(2)}, u32[]{:S(2)}) %all-to-all-start) | async-done | bytes 1048608 | tf_op jit(solution)/shard_map/all_to_all | solution.py:220
  101.4 43.4 %all-gather.15 = f16[1024,2048]{1,0:T(8,128)(2,1)S(1)} all-gather(f16[32,2048]{1,0:T(8,128)(2,1)S(1)} %fusion.45), channel_id=1, replica_groups=mesh['rep'=4,'xh'=2,'xl'=2,'z'=16,'core'=2] {'z','core'}, dimensions={0}, use_global_device_ids=true | all-gather | bytes 4325376 | tf_op jit(solution)/shard_map/all_gather | solution.py:225
  144.9 3.0 %fusion.5 = bf16[384,2048]{1,0:T(8,128)(2,1)} fusion(pred[384,1024]{1,0:T(32,128)(4,1)S(1)} %bitcast_compare_fusion, f16[1024,2048]{1,0:T(8,128)(2,1)S(1)} %all-gather.15), kind=kOutput, calls=%fused_computation.7 | convolution fusion | flops 1613496320 | bytes 6160384 | tf_op jit(solution)/shard_map/dot_general | solution.py:276
  147.9 5.2 %all-to-all-start.1 = ((bf16[4,96,2048]{2,1,0:T(8,128)(2,1)}), bf16[4,96,2048]{2,1,0:T(8,128)(2,1)S(1)}, u32[]{:S(2)}, u32[]{:S(2)}) async-start(bf16[4,96,2048]{2,1,0:T(8,128)(2,1)} %bitcast.187), calls=%async_computation.1 | async-start | bytes 3145728 | tf_op jit(solution)/shard_map/all_to_all | solution.py:277
  154.6 18.9 %all-to-all-done.1 = bf16[4,96,2048]{2,1,0:T(8,128)(2,1)S(1)} async-done(((bf16[4,96,2048]{2,1,0:T(8,128)(2,1)}), bf16[4,96,2048]{2,1,0:T(8,128)(2,1)S(1)}, u32[]{:S(2)}, u32[]{:S(2)}) %all-to-all-start.1) | async-done | bytes 1572896 | tf_op jit(solution)/shard_map/all_to_all | solution.py:277
  173.5 1.1 copy-done.2
  174.7 9.2 %shard_map.118 = (bf16[192,2048]{1,0:T(8,128)(2,1)}, bf16[192,2048]{1,0:T(8,128)(2,1)}) custom-call(bf16[384,2048]{1,0:T(8,128)(2,1)} %bitcast.186, bf16[768,2048]{1,0:T(8,128)(2,1)} %bitcast.229, bf16[768,2048]{1,0:T(8,128)(2,1)} %bitcast.230, bf16[4,768,512]{2,1,0:T(8,128)(2,1)} %bitcast.231), custom_call_target="tpu_custom_call" | custom-call | flops 3623878656 | bytes 12582912 | tf_op jit(solution)/shard_map/pallas_call | solution.py:119
  183.9 4.7 %all-to-all-start.2 = ((bf16[8,24,2048]{2,1,0:T(8,128)(2,1)}), bf16[8,24,2048]{2,1,0:T(8,128)(2,1)S(1)}, u32[]{:S(2)}, u32[]{:S(2)}) async-start(bf16[8,24,2048]{2,1,0:T(8,128)(2,1)} %bitcast.189), calls=%async_computation.2 | async-start | bytes 1572864 | tf_op jit(solution)/shard_map/all_to_all | solution.py:282
  189.2 11.7 %all-to-all-done.2 = bf16[8,24,2048]{2,1,0:T(8,128)(2,1)S(1)} async-done(((bf16[8,24,2048]{2,1,0:T(8,128)(2,1)}), bf16[8,24,2048]{2,1,0:T(8,128)(2,1)S(1)}, u32[]{:S(2)}, u32[]{:S(2)}) %all-to-all-start.2) | async-done | bytes 786464 | tf_op jit(solution)/shard_map/all_to_all | solution.py:282
  202.2 2.2 collective-permute-start.7
  204.6 4.6 %all-to-all-start.3 = ((bf16[8,24,2048]{2,1,0:T(8,128)(2,1)}), bf16[8,24,2048]{2,1,0:T(8,128)(2,1)S(1)}, u32[]{:S(2)}, u32[]{:S(2)}) async-start(bf16[8,24,2048]{2,1,0:T(8,128)(2,1)} %bitcast.60), calls=%async_computation.3 | async-start | bytes 1572864 | tf_op jit(solution)/shard_map/all_to_all | solution.py:282
  209.2 5.2 %collective-permute-start.4 = (bf16[64,2048]{1,0:T(8,128)(2,1)}, bf16[64,2048]{1,0:T(8,128)(2,1)S(1)}, u32[]{:S(2)}, u32[]{:S(2)}) collective-permute-start(bf16[64,2048]{1,0:T(8,128)(2,1)} %concatenate.75), channel_id=1, source_target_pairs={{0,28},{2,30},{4,0},{6,2},{8,4},{10,6},{12,8},{14,10},{16,12},{18,... | collective-permute-start | bytes 786440 | tf_op jit(solution)/shard_map/ppermute | solution.py:31
  214.4 2.0 collective-permute-start.8
  216.5 10.4 %collective-permute-done.4 = bf16[64,2048]{1,0:T(8,128)(2,1)S(1)} collective-permute-done((bf16[64,2048]{1,0:T(8,128)(2,1)}, bf16[64,2048]{1,0:T(8,128)(2,1)S(1)}, u32[]{:S(2)}, u32[]{:S(2)}) %collective-permute-start.4) | collective-permute-done | bytes 262176 | tf_op jit(solution)/shard_map/ppermute | solution.py:31
  226.9 3.0 %collective-permute-start.5 = (bf16[64,2048]{1,0:T(8,128)(2,1)S(1)}, bf16[64,2048]{1,0:T(8,128)(2,1)S(1)}, u32[]{:S(2)}, u32[]{:S(2)}) collective-permute-start(bf16[64,2048]{1,0:T(8,128)(2,1)S(1)} %add_convert_fusion.4), channel_id=1, source_target_pairs={{0,28},{2,30},{4,0},{6,2},{8,4},{10,6},{12,8},{14,10},{16,12},{18,... | collective-permute-start | bytes 786440 | tf_op jit(solution)/shard_map/ppermute | solution.py:31
  230.6 4.6 %collective-permute-start.9 = (bf16[64,2048]{1,0:T(8,128)(2,1)S(1)}, bf16[64,2048]{1,0:T(8,128)(2,1)S(1)}, u32[]{:S(2)}, u32[]{:S(2)}) collective-permute-start(bf16[64,2048]{1,0:T(8,128)(2,1)S(1)} %add_convert_fusion.1), channel_id=1, source_target_pairs={{0,4},{2,6},{4,8},{6,10},{8,12},{10,14},{12,16},{14,18},{16,20},{1... | collective-permute-start | bytes 786440 | tf_op jit(solution)/shard_map/ppermute | solution.py:31
  235.1 8.8 %collective-permute-done.5 = bf16[64,2048]{1,0:T(8,128)(2,1)S(1)} collective-permute-done((bf16[64,2048]{1,0:T(8,128)(2,1)S(1)}, bf16[64,2048]{1,0:T(8,128)(2,1)S(1)}, u32[]{:S(2)}, u32[]{:S(2)}) %collective-permute-start.5) | collective-permute-done | bytes 262176 | tf_op jit(solution)/shard_map/ppermute | solution.py:31
  243.9 1.9 collective-permute-start.6
  245.9 1.2 collective-permute-done.9
  247.2 5.2 %collective-permute-start.10 = (bf16[32,2048]{1,0:T(8,128)(2,1)S(1)}, bf16[32,2048]{1,0:T(8,128)(2,1)S(1)}, u32[]{:S(2)}, u32[]{:S(2)}) collective-permute-start(bf16[32,2048]{1,0:T(8,128)(2,1)S(1)} %get-tuple-element.29), channel_id=1, source_target_pairs={{0,4},{2,6},{4,8},{6,10},{8,12},{10,14},{12,16},{14,18},{16,20},{1... | collective-permute-start | bytes 393224 | tf_op jit(solution)/shard_map/ppermute | solution.py:31
  252.4 2.3 collective-permute-start.11
  254.7 5.5 %collective-permute-done.6 = bf16[64,2048]{1,0:T(8,128)(2,1)S(1)} collective-permute-done((bf16[64,2048]{1,0:T(8,128)(2,1)S(1)}, bf16[64,2048]{1,0:T(8,128)(2,1)S(1)}, u32[]{:S(2)}, u32[]{:S(2)}) %collective-permute-start.6) | collective-permute-done | bytes 262176 | tf_op jit(solution)/shard_map/ppermute | solution.py:31
  260.3 4.4 %collective-permute-start.12 = (bf16[32,2048]{1,0:T(8,128)(2,1)S(1)}, bf16[32,2048]{1,0:T(8,128)(2,1)S(1)}, u32[]{:S(2)}, u32[]{:S(2)}) collective-permute-start(bf16[32,2048]{1,0:T(8,128)(2,1)S(1)} %add_convert_fusion.6), channel_id=1, source_target_pairs={{0,30},{2,0},{4,2},{6,4},{8,6},{10,8},{12,10},{14,12},{16,14},{18,... | collective-permute-start | bytes 393224 | tf_op jit(solution)/shard_map/ppermute | solution.py:31
  264.8 2.0 collective-permute-done.12
  (105 shorter events, 18.0 us)
Async XLA Ops:
  6.5 20.5 %copy-start = (bf16[128,1024]{1,0:T(8,128)(2,1)S(1)}, bf16[128,1024]{1,0:T(8,128)(2,1)}, u32[]{:S(2)}) copy-start(bf16[128,1024]{1,0:T(8,128)(2,1)} %param.12) | copy-start | bytes 786436
  6.5 167.0 %all-gather.9.cloned.1.call-start = ((), (), s32[]{:S(2)}) async-start(), calls=%async_computation.4 | async-start | bytes 3932160 | tf_op jit(solution)/shard_map/all_gather | solution.py:187
  7.3 166.3 %all-gather.11.cloned.1.call-start = ((), (), s32[]{:S(2)}) async-start(), calls=%async_computation.5 | async-start | bytes 3932160 | tf_op jit(solution)/shard_map/all_gather | solution.py:188
  8.0 165.5 %all-gather.13.cloned.1.call-start = ((), (), s32[]{:S(2)}) async-start(), calls=%async_computation.6 | async-start | bytes 3932160 | tf_op jit(solution)/shard_map/all_gather | solution.py:189
  17.3 9.7 %collective-permute-start = (bf16[256,256]{1,0:T(8,128)(2,1)S(1)}, bf16[256,256]{1,0:T(8,128)(2,1)S(1)}, u32[]{:S(2)}, u32[]{:S(2)}) collective-permute-start(bf16[256,256]{1,0:T(8,128)(2,1)S(1)} %all_gather.18), channel_id=1, source_target_pairs={{0,4},{2,6},{4,8},{6,10},{8,12},{10,14},{12,16},{14,18},{16,20},{1... | collective-permute-start | bytes 393224 | tf_op jit(solution)/shard_map/ppermute | solution.py:26
  18.6 8.5 %collective-permute-start.1 = (bf16[256,256]{1,0:T(8,128)(2,1)S(1)}, bf16[256,256]{1,0:T(8,128)(2,1)S(1)}, u32[]{:S(2)}, u32[]{:S(2)}) collective-permute-start(bf16[256,256]{1,0:T(8,128)(2,1)S(1)} %all_gather.18), channel_id=1, source_target_pairs={{0,2},{2,4},{4,6},{6,8},{8,10},{10,12},{12,14},{14,16},{16,18},{18... | collective-permute-start | bytes 393224 | tf_op jit(solution)/shard_map/ppermute | solution.py:26
  21.1 5.8 %collective-permute-start.3 = (f16[8,2048]{1,0:T(8,128)(2,1)S(1)}, f16[8,2048]{1,0:T(8,128)(2,1)S(1)}, u32[]{:S(2)}, u32[]{:S(2)}) collective-permute-start(f16[8,2048]{1,0:T(8,128)(2,1)S(1)} %convert_element_type.192), channel_id=1, source_target_pairs={{0,32},{32,0},{1,33},{33,1},{2,34},{34,2},{3,35},{35,3},{4,36},{36... | collective-permute-start | bytes 98312 | tf_op jit(solution)/shard_map/ppermute | solution.py:31
  29.5 45.4 %collective-permute-start.2 = (bf16[128,512]{1,0:T(8,128)(2,1)S(1)}, bf16[128,512]{1,0:T(8,128)(2,1)S(1)}, u32[]{:S(2)}, u32[]{:S(2)}) collective-permute-start(bf16[128,512]{1,0:T(8,128)(2,1)S(1)} %broadcast_select_fusion.2), channel_id=1, source_target_pairs={{0,64},{64,0},{1,65},{65,1},{2,66},{66,2},{3,67},{67,3},{4,68},{68... | collective-permute-start | bytes 393224 | tf_op jit(solution)/shard_map/ppermute | solution.py:31
  74.9 2.1 copy-start.1
  77.0 24.0 %all-to-all-start = ((bf16[8,32,2048]{2,1,0:T(8,128)(2,1)}), bf16[8,32,2048]{2,1,0:T(8,128)(2,1)S(1)}, u32[]{:S(2)}, u32[]{:S(2)}) async-start(bf16[8,32,2048]{2,1,0:T(8,128)(2,1)} %bitcast.188), calls=%async_computation | async-start | bytes 2097152 | tf_op jit(solution)/shard_map/all_to_all | solution.py:220
  83.6 17.6 %copy-start.3 = (bf16[1,32,2048]{2,1,0:T(8,128)(2,1)S(1)}, bf16[1,32,2048]{2,1,0:T(8,128)(2,1)}, u32[]{:S(2)}) copy-start(bf16[1,32,2048]{2,1,0:T(8,128)(2,1)} %param.16) | copy-start | bytes 393220
  84.4 17.0 %copy-start.4 = (f32[2048]{0:T(1024)S(1)}, f32[2048]{0:T(1024)}, u32[]{:S(2)}) copy-start(f32[2048]{0:T(1024)} %param.18) | copy-start | bytes 24580
  147.9 25.6 %all-to-all-start.1 = ((bf16[4,96,2048]{2,1,0:T(8,128)(2,1)}), bf16[4,96,2048]{2,1,0:T(8,128)(2,1)S(1)}, u32[]{:S(2)}, u32[]{:S(2)}) async-start(bf16[4,96,2048]{2,1,0:T(8,128)(2,1)} %bitcast.187), calls=%async_computation.1 | async-start | bytes 3145728 | tf_op jit(solution)/shard_map/all_to_all | solution.py:277
  173.5 1.1 copy-start.2
  183.9 17.1 %all-to-all-start.2 = ((bf16[8,24,2048]{2,1,0:T(8,128)(2,1)}), bf16[8,24,2048]{2,1,0:T(8,128)(2,1)S(1)}, u32[]{:S(2)}, u32[]{:S(2)}) async-start(bf16[8,24,2048]{2,1,0:T(8,128)(2,1)} %bitcast.189), calls=%async_computation.2 | async-start | bytes 1572864 | tf_op jit(solution)/shard_map/all_to_all | solution.py:282
  202.2 12.2 %collective-permute-start.7 = (bf16[64,2048]{1,0:T(8,128)(2,1)S(1)}, bf16[64,2048]{1,0:T(8,128)(2,1)S(1)}, u32[]{:S(2)}, u32[]{:S(2)}) collective-permute-start(bf16[64,2048]{1,0:T(8,128)(2,1)S(1)} %pad_maximum_fusion), channel_id=1, source_target_pairs={{0,4},{2,6},{4,8},{6,10},{8,12},{10,14},{12,16},{14,18},{16,20},{1... | collective-permute-start | bytes 786440 | tf_op jit(solution)/shard_map/ppermute | solution.py:31
  204.6 25.4 %all-to-all-start.3 = ((bf16[8,24,2048]{2,1,0:T(8,128)(2,1)}), bf16[8,24,2048]{2,1,0:T(8,128)(2,1)S(1)}, u32[]{:S(2)}, u32[]{:S(2)}) async-start(bf16[8,24,2048]{2,1,0:T(8,128)(2,1)} %bitcast.60), calls=%async_computation.3 | async-start | bytes 1572864 | tf_op jit(solution)/shard_map/all_to_all | solution.py:282
  209.2 17.7 %collective-permute-start.4 = (bf16[64,2048]{1,0:T(8,128)(2,1)}, bf16[64,2048]{1,0:T(8,128)(2,1)S(1)}, u32[]{:S(2)}, u32[]{:S(2)}) collective-permute-start(bf16[64,2048]{1,0:T(8,128)(2,1)} %concatenate.75), channel_id=1, source_target_pairs={{0,28},{2,30},{4,0},{6,2},{8,4},{10,6},{12,8},{14,10},{16,12},{18,... | collective-permute-start | bytes 786440 | tf_op jit(solution)/shard_map/ppermute | solution.py:31
  214.4 16.0 %collective-permute-start.8 = (bf16[64,2048]{1,0:T(8,128)(2,1)S(1)}, bf16[64,2048]{1,0:T(8,128)(2,1)S(1)}, u32[]{:S(2)}, u32[]{:S(2)}) collective-permute-start(bf16[64,2048]{1,0:T(8,128)(2,1)S(1)} %add_convert_fusion.2), channel_id=1, source_target_pairs={{0,4},{2,6},{4,8},{6,10},{8,12},{10,14},{12,16},{14,18},{16,20},{1... | collective-permute-start | bytes 786440 | tf_op jit(solution)/shard_map/ppermute | solution.py:31
  226.9 16.9 %collective-permute-start.5 = (bf16[64,2048]{1,0:T(8,128)(2,1)S(1)}, bf16[64,2048]{1,0:T(8,128)(2,1)S(1)}, u32[]{:S(2)}, u32[]{:S(2)}) collective-permute-start(bf16[64,2048]{1,0:T(8,128)(2,1)S(1)} %add_convert_fusion.4), channel_id=1, source_target_pairs={{0,28},{2,30},{4,0},{6,2},{8,4},{10,6},{12,8},{14,10},{16,12},{18,... | collective-permute-start | bytes 786440 | tf_op jit(solution)/shard_map/ppermute | solution.py:31
  230.6 16.5 %collective-permute-start.9 = (bf16[64,2048]{1,0:T(8,128)(2,1)S(1)}, bf16[64,2048]{1,0:T(8,128)(2,1)S(1)}, u32[]{:S(2)}, u32[]{:S(2)}) collective-permute-start(bf16[64,2048]{1,0:T(8,128)(2,1)S(1)} %add_convert_fusion.1), channel_id=1, source_target_pairs={{0,4},{2,6},{4,8},{6,10},{8,12},{10,14},{12,16},{14,18},{16,20},{1... | collective-permute-start | bytes 786440 | tf_op jit(solution)/shard_map/ppermute | solution.py:31
  243.9 16.3 %collective-permute-start.6 = (bf16[64,2048]{1,0:T(8,128)(2,1)S(1)}, bf16[64,2048]{1,0:T(8,128)(2,1)S(1)}, u32[]{:S(2)}, u32[]{:S(2)}) collective-permute-start(bf16[64,2048]{1,0:T(8,128)(2,1)S(1)} %add_convert_fusion.3), channel_id=1, source_target_pairs={{0,28},{2,30},{4,0},{6,2},{8,4},{10,6},{12,8},{14,10},{16,12},{18,... | collective-permute-start | bytes 786440 | tf_op jit(solution)/shard_map/ppermute | solution.py:31
  247.2 17.6 %collective-permute-start.10 = (bf16[32,2048]{1,0:T(8,128)(2,1)S(1)}, bf16[32,2048]{1,0:T(8,128)(2,1)S(1)}, u32[]{:S(2)}, u32[]{:S(2)}) collective-permute-start(bf16[32,2048]{1,0:T(8,128)(2,1)S(1)} %get-tuple-element.29), channel_id=1, source_target_pairs={{0,4},{2,6},{4,8},{6,10},{8,12},{10,14},{12,16},{14,18},{16,20},{1... | collective-permute-start | bytes 393224 | tf_op jit(solution)/shard_map/ppermute | solution.py:31
  252.4 12.4 %collective-permute-start.11 = (bf16[32,2048]{1,0:T(8,128)(2,1)S(1)}, bf16[32,2048]{1,0:T(8,128)(2,1)S(1)}, u32[]{:S(2)}, u32[]{:S(2)}) collective-permute-start(bf16[32,2048]{1,0:T(8,128)(2,1)S(1)} %get-tuple-element.30), channel_id=1, source_target_pairs={{0,2},{2,4},{4,6},{6,8},{8,10},{10,12},{12,14},{14,16},{16,18},{18... | collective-permute-start | bytes 393224 | tf_op jit(solution)/shard_map/ppermute | solution.py:31
  260.3 6.4 %collective-permute-start.12 = (bf16[32,2048]{1,0:T(8,128)(2,1)S(1)}, bf16[32,2048]{1,0:T(8,128)(2,1)S(1)}, u32[]{:S(2)}, u32[]{:S(2)}) collective-permute-start(bf16[32,2048]{1,0:T(8,128)(2,1)S(1)} %add_convert_fusion.6), channel_id=1, source_target_pairs={{0,30},{2,0},{4,2},{6,4},{8,6},{10,8},{12,10},{14,12},{16,14},{18,... | collective-permute-start | bytes 393224 | tf_op jit(solution)/shard_map/ppermute | solution.py:31
Sparse Core Ops, SparseCore 0:
  9.5 52.5 all-gather.8
  64.1 58.2 all-gather.10
  124.6 43.7 all-gather.12

commit v7 on v6

--- a/solution.py
+++ b/solution.py
@@ -11,6 +11,8 @@
 HOPS = 4
 CAP = 3
 VMEM_GRANT = 56 * 2**20
+WEIGHT_SCALE = 2.0**19
+ROW_SCALE = 2.0**9
 BF = jnp.bfloat16
 F16 = jnp.float16
 F32 = jnp.float32
@@ -188,7 +190,7 @@
     up_all = lax.all_gather(up_weight[0], "rep", axis=0, tiled=True)
     down_all = lax.all_gather(down_weight[0], "rep", axis=0, tiled=True)
 
-    own_rows = out_weight.astype(F16)
+    own_rows = (out_weight * WEIGHT_SCALE).astype(F16)
     pair_rows = jnp.concatenate([own_rows, shift(own_rows, "xl", 1)], 0)
     info = jnp.concatenate([route_ids[0].astype(F16), route_weights[0].astype(F16)], 1)
     info = jnp.pad(info, ((0, 0), (0, 128 - 2 * top)))
@@ -216,13 +218,15 @@
     source = ((px * nz + pz) * nc + pc) * rows8 + pi
     permute = (place[:, None] == source[None, :]).astype(BF)
     both = jnp.dot(both, permute, preferred_element_type=F32).astype(BF)
-    partial_value = jnp.dot(both, out_rows, preferred_element_type=F32).astype(BF)
+    partial_value = jnp.dot(both, out_rows, preferred_element_type=F32)
+    partial_value = (partial_value * (1.0 / WEIGHT_SCALE)).astype(BF)
     parts = lax.all_to_all(partial_value, ("rep", "xh"), split_axis=0, concat_axis=0, tiled=True)
     head_total = jnp.sum(parts.reshape(-1, tok_sub, width).astype(F32), axis=0)
     hidden_sum = residual[0].astype(F32) + head_total
     inverse_rms = lax.rsqrt(jnp.mean(hidden_sum * hidden_sum, axis=-1, keepdims=True) + 1e-06)
     normed = (hidden_sum * inverse_rms * norm_gain).astype(BF)
-    column = lax.all_gather(normed.astype(F16), ZC, axis=0, tiled=True).astype(BF)
+    column = (normed * ROW_SCALE).astype(F16)
+    column = lax.all_gather(column, ZC, axis=0, tiled=True).astype(BF)
 
     table = [z_all[:, width + 128 * g :][:, : 2 * top].astype(F32) for g in range(groups)]
     table = jnp.stack([jnp.transpose(t).reshape(2 * top, -1, 2 * rows8) for t in table], 2)
@@ -273,7 +277,8 @@
 
     backs = back_for(far_places), back_for(near_places)
 
-    send_rows = jnp.dot(send, column, preferred_element_type=F32).astype(BF)
+    send_rows = jnp.dot(send, column, preferred_element_type=F32)
+    send_rows = (send_rows * (1.0 / ROW_SCALE)).astype(BF)
     rows = lax.all_to_all(send_rows, X, split_axis=0, concat_axis=0, tiled=True)
     far, near = expert(rows, gate_all, up_all, down_all, nr, nc * cap)
     chunks = [None] * nz

time: 277 us -> 277 us (level)
  no operation moved by 1% of the time
where the time goes in v7:
time: 277 us; the launch traced here: 274 us
  blocking collectives  87.4 us (32%)
  waiting for transfers between devices  75 us (27%)
  starting transfers between devices  66.1 us (24%)
  between operations  13.7 us (5%)
  Pallas kernels  9.23 us (3%)
  matrix products  8.35 us (3%)
  other arithmetic  7.74 us (3%)
  local copies, waits for them, and re-layouts  6.54 us (2%)
    ppermute x11, starting transfers between devices, shift(): lax.ppermute(value, axis, [(i, (i + by) % devices) for i in range(devices)])  43.9 us
    all_gather x1, blocking collectives, on_device(): column = lax.all_gather(column, ZC, axis=0, tiled=True).astype(BF)  43.4 us
    all_gather x1, blocking collectives, on_device(): z_all = lax.all_gather(pair_rows, ZC, axis=0, tiled=True)  35.6 us
    ppermute x11, waiting for transfers between devices, shift(): lax.ppermute(value, axis, [(i, (i + by) % devices) for i in range(devices)])  27.8 us
    all_to_all x1, waiting for transfers between devices, on_device(): rows = lax.all_to_all(send_rows, X, split_axis=0, concat_axis=0, tiled=True)  18.9 us
    all_to_all x1, waiting for transfers between devices, on_device(): lax.all_to_all(partial_value, ('rep', 'xh'), split_axis=0, concat_axis=0,...  15.1 us
    all_to_all x2, waiting for transfers between devices, spread_out(): returned = lax.all_to_all(out, XC, split_axis=0, concat_axis=0, tiled=True)  11.7 us
    all_to_all x2, starting transfers between devices, spread_out(): returned = lax.all_to_all(out, XC, split_axis=0, concat_axis=0, tiled=True)  9.34 us
  transfers between devices with their start and end apart: 20, of which 8 were waited for; matrix products, arithmetic and copies ran while one was open for 7% of the time, Pallas kernels for 0%

profile of v7, /device:TPU:1, one launch (start us, length us, event | category | flops | bytes accessed | tf_op | source)
XLA Modules:
  0.0 274.1 jit_solution(14127290146126539254)
XLA Ops:
  8.8 8.4 %all_gather.18 = bf16[256,256]{1,0:T(8,128)(2,1)S(1)} all-gather(bf16[128,256]{1,0:T(8,128)(2,1)S(1)} %pad_maximum_fusion.2), channel_id=1, replica_groups=mesh['rep'=4,'xh'=2,'xl'=2,'z'=16,'core'=2] {'core'}, dimensions={0}, use_global_device_ids=true | all-gather | bytes 196608 | tf_op jit(solution)/shard_map/all_gather | solution.py:45
  17.3 1.3 collective-permute-start
  18.6 1.8 collective-permute-start.1
  21.1 3.1 %collective-permute-start.3 = (f16[8,2048]{1,0:T(8,128)(2,1)S(1)}, f16[8,2048]{1,0:T(8,128)(2,1)S(1)}, u32[]{:S(2)}, u32[]{:S(2)}) collective-permute-start(f16[8,2048]{1,0:T(8,128)(2,1)S(1)} %multiply_convert_fusion.2), channel_id=1, source_target_pairs={{0,32},{32,0},{1,33},{33,1},{2,34},{34,2},{3,35},{35,3},{4,36},{36... | collective-permute-start | bytes 98312 | tf_op jit(solution)/shard_map/ppermute | solution.py:33
  29.5 9.8 %collective-permute-start.2 = (bf16[128,512]{1,0:T(8,128)(2,1)S(1)}, bf16[128,512]{1,0:T(8,128)(2,1)S(1)}, u32[]{:S(2)}, u32[]{:S(2)}) collective-permute-start(bf16[128,512]{1,0:T(8,128)(2,1)S(1)} %broadcast_select_fusion.2), channel_id=1, source_target_pairs={{0,64},{64,0},{1,65},{65,1},{2,66},{66,2},{3,67},{67,3},{4,68},{68... | collective-permute-start | bytes 393224 | tf_op jit(solution)/shard_map/ppermute | solution.py:33
  39.3 35.6 %all-gather.14 = f16[512,2304]{1,0:T(8,128)(2,1)S(1)} all-gather(f16[16,2304]{1,0:T(8,128)(2,1)S(1)} %pad_maximum_fusion.1), channel_id=1, replica_groups=mesh['rep'=4,'xh'=2,'xl'=2,'z'=16,'core'=2] {'z','core'}, dimensions={0}, use_global_device_ids=true | all-gather | bytes 2433024 | tf_op jit(solution)/shard_map/all_gather | solution.py:209
  75.0 2.0 fusion.9
  77.0 4.5 %all-to-all-start = ((bf16[8,32,2048]{2,1,0:T(8,128)(2,1)}), bf16[8,32,2048]{2,1,0:T(8,128)(2,1)S(1)}, u32[]{:S(2)}, u32[]{:S(2)}) async-start(bf16[8,32,2048]{2,1,0:T(8,128)(2,1)} %bitcast.188), calls=%async_computation | async-start | bytes 2097152 | tf_op jit(solution)/shard_map/all_to_all | solution.py:223
  85.9 15.1 %all-to-all-done = bf16[8,32,2048]{2,1,0:T(8,128)(2,1)S(1)} async-done(((bf16[8,32,2048]{2,1,0:T(8,128)(2,1)}), bf16[8,32,2048]{2,1,0:T(8,128)(2,1)S(1)}, u32[]{:S(2)}, u32[]{:S(2)}) %all-to-all-start) | async-done | bytes 1048608 | tf_op jit(solution)/shard_map/all_to_all | solution.py:223
  101.5 43.4 %all-gather.15 = f16[1024,2048]{1,0:T(8,128)(2,1)S(1)} all-gather(f16[32,2048]{1,0:T(8,128)(2,1)S(1)} %fusion.46), channel_id=1, replica_groups=mesh['rep'=4,'xh'=2,'xl'=2,'z'=16,'core'=2] {'z','core'}, dimensions={0}, use_global_device_ids=true | all-gather | bytes 4325376 | tf_op jit(solution)/shard_map/all_gather | solution.py:229
  144.9 3.0 %multiply_convert_fusion = bf16[384,2048]{1,0:T(8,128)(2,1)} fusion(pred[384,1024]{1,0:T(32,128)(4,1)S(1)} %bitcast_compare_fusion, f16[1024,2048]{1,0:T(8,128)(2,1)S(1)} %all-gather.15), kind=kOutput, calls=%fused_computation.6 | convolution fusion | flops 1614282752 | bytes 6160384 | tf_op jit(solution)/shard_map/dot_general | solution.py:280
  147.9 5.2 %all-to-all-start.1 = ((bf16[4,96,2048]{2,1,0:T(8,128)(2,1)}), bf16[4,96,2048]{2,1,0:T(8,128)(2,1)S(1)}, u32[]{:S(2)}, u32[]{:S(2)}) async-start(bf16[4,96,2048]{2,1,0:T(8,128)(2,1)} %bitcast.187), calls=%async_computation.1 | async-start | bytes 3145728 | tf_op jit(solution)/shard_map/all_to_all | solution.py:282
  154.6 18.9 %all-to-all-done.1 = bf16[4,96,2048]{2,1,0:T(8,128)(2,1)S(1)} async-done(((bf16[4,96,2048]{2,1,0:T(8,128)(2,1)}), bf16[4,96,2048]{2,1,0:T(8,128)(2,1)S(1)}, u32[]{:S(2)}, u32[]{:S(2)}) %all-to-all-start.1) | async-done | bytes 1572896 | tf_op jit(solution)/shard_map/all_to_all | solution.py:282
  173.5 1.1 copy-done.2
  174.7 9.2 %shard_map.118 = (bf16[192,2048]{1,0:T(8,128)(2,1)}, bf16[192,2048]{1,0:T(8,128)(2,1)}) custom-call(bf16[384,2048]{1,0:T(8,128)(2,1)} %bitcast.186, bf16[768,2048]{1,0:T(8,128)(2,1)} %bitcast.229, bf16[768,2048]{1,0:T(8,128)(2,1)} %bitcast.230, bf16[4,768,512]{2,1,0:T(8,128)(2,1)} %bitcast.231), custom_call_target="tpu_custom_call" | custom-call | flops 3623878656 | bytes 12582912 | tf_op jit(solution)/shard_map/pallas_call | solution.py:121
  183.9 4.7 %all-to-all-start.2 = ((bf16[8,24,2048]{2,1,0:T(8,128)(2,1)}), bf16[8,24,2048]{2,1,0:T(8,128)(2,1)S(1)}, u32[]{:S(2)}, u32[]{:S(2)}) async-start(bf16[8,24,2048]{2,1,0:T(8,128)(2,1)} %bitcast.189), calls=%async_computation.2 | async-start | bytes 1572864 | tf_op jit(solution)/shard_map/all_to_all | solution.py:287
  189.3 11.7 %all-to-all-done.2 = bf16[8,24,2048]{2,1,0:T(8,128)(2,1)S(1)} async-done(((bf16[8,24,2048]{2,1,0:T(8,128)(2,1)}), bf16[8,24,2048]{2,1,0:T(8,128)(2,1)S(1)}, u32[]{:S(2)}, u32[]{:S(2)}) %all-to-all-start.2) | async-done | bytes 786464 | tf_op jit(solution)/shard_map/all_to_all | solution.py:287
  202.2 2.2 collective-permute-start.7
  204.6 4.6 %all-to-all-start.3 = ((bf16[8,24,2048]{2,1,0:T(8,128)(2,1)}), bf16[8,24,2048]{2,1,0:T(8,128)(2,1)S(1)}, u32[]{:S(2)}, u32[]{:S(2)}) async-start(bf16[8,24,2048]{2,1,0:T(8,128)(2,1)} %bitcast.60), calls=%async_computation.3 | async-start | bytes 1572864 | tf_op jit(solution)/shard_map/all_to_all | solution.py:287
  209.2 5.2 %collective-permute-start.4 = (bf16[64,2048]{1,0:T(8,128)(2,1)}, bf16[64,2048]{1,0:T(8,128)(2,1)S(1)}, u32[]{:S(2)}, u32[]{:S(2)}) collective-permute-start(bf16[64,2048]{1,0:T(8,128)(2,1)} %concatenate.75), channel_id=1, source_target_pairs={{0,28},{2,30},{4,0},{6,2},{8,4},{10,6},{12,8},{14,10},{16,12},{18,... | collective-permute-start | bytes 786440 | tf_op jit(solution)/shard_map/ppermute | solution.py:33
  214.5 2.2 collective-permute-start.8
  216.6 10.4 %collective-permute-done.4 = bf16[64,2048]{1,0:T(8,128)(2,1)S(1)} collective-permute-done((bf16[64,2048]{1,0:T(8,128)(2,1)}, bf16[64,2048]{1,0:T(8,128)(2,1)S(1)}, u32[]{:S(2)}, u32[]{:S(2)}) %collective-permute-start.4) | collective-permute-done | bytes 262176 | tf_op jit(solution)/shard_map/ppermute | solution.py:33
  227.1 3.0 %collective-permute-start.5 = (bf16[64,2048]{1,0:T(8,128)(2,1)S(1)}, bf16[64,2048]{1,0:T(8,128)(2,1)S(1)}, u32[]{:S(2)}, u32[]{:S(2)}) collective-permute-start(bf16[64,2048]{1,0:T(8,128)(2,1)S(1)} %add_convert_fusion.4), channel_id=1, source_target_pairs={{0,28},{2,30},{4,0},{6,2},{8,4},{10,6},{12,8},{14,10},{16,12},{18,... | collective-permute-start | bytes 786440 | tf_op jit(solution)/shard_map/ppermute | solution.py:33
  230.7 4.5 %collective-permute-start.9 = (bf16[64,2048]{1,0:T(8,128)(2,1)S(1)}, bf16[64,2048]{1,0:T(8,128)(2,1)S(1)}, u32[]{:S(2)}, u32[]{:S(2)}) collective-permute-start(bf16[64,2048]{1,0:T(8,128)(2,1)S(1)} %add_convert_fusion.1), channel_id=1, source_target_pairs={{0,4},{2,6},{4,8},{6,10},{8,12},{10,14},{12,16},{14,18},{16,20},{1... | collective-permute-start | bytes 786440 | tf_op jit(solution)/shard_map/ppermute | solution.py:33
  235.2 8.9 %collective-permute-done.5 = bf16[64,2048]{1,0:T(8,128)(2,1)S(1)} collective-permute-done((bf16[64,2048]{1,0:T(8,128)(2,1)S(1)}, bf16[64,2048]{1,0:T(8,128)(2,1)S(1)}, u32[]{:S(2)}, u32[]{:S(2)}) %collective-permute-start.5) | collective-permute-done | bytes 262176 | tf_op jit(solution)/shard_map/ppermute | solution.py:33
  244.2 1.9 collective-permute-start.6
  246.1 1.1 collective-permute-done.9
  247.3 5.2 %collective-permute-start.10 = (bf16[32,2048]{1,0:T(8,128)(2,1)S(1)}, bf16[32,2048]{1,0:T(8,128)(2,1)S(1)}, u32[]{:S(2)}, u32[]{:S(2)}) collective-permute-start(bf16[32,2048]{1,0:T(8,128)(2,1)S(1)} %get-tuple-element.29), channel_id=1, source_target_pairs={{0,4},{2,6},{4,8},{6,10},{8,12},{10,14},{12,16},{14,18},{16,20},{1... | collective-permute-start | bytes 393224 | tf_op jit(solution)/shard_map/ppermute | solution.py:33
  252.4 2.5 collective-permute-start.11
  254.9 5.4 %collective-permute-done.6 = bf16[64,2048]{1,0:T(8,128)(2,1)S(1)} collective-permute-done((bf16[64,2048]{1,0:T(8,128)(2,1)S(1)}, bf16[64,2048]{1,0:T(8,128)(2,1)S(1)}, u32[]{:S(2)}, u32[]{:S(2)}) %collective-permute-start.6) | collective-permute-done | bytes 262176 | tf_op jit(solution)/shard_map/ppermute | solution.py:33
  260.4 4.5 %collective-permute-start.12 = (bf16[32,2048]{1,0:T(8,128)(2,1)S(1)}, bf16[32,2048]{1,0:T(8,128)(2,1)S(1)}, u32[]{:S(2)}, u32[]{:S(2)}) collective-permute-start(bf16[32,2048]{1,0:T(8,128)(2,1)S(1)} %add_convert_fusion.6), channel_id=1, source_target_pairs={{0,30},{2,0},{4,2},{6,4},{8,6},{10,8},{12,10},{14,12},{16,14},{18,... | collective-permute-start | bytes 393224 | tf_op jit(solution)/shard_map/ppermute | solution.py:33
  264.9 1.9 collective-permute-done.12
  (105 shorter events, 18.0 us)
Async XLA Ops:
  6.5 20.5 %copy-start = (bf16[128,1024]{1,0:T(8,128)(2,1)S(1)}, bf16[128,1024]{1,0:T(8,128)(2,1)}, u32[]{:S(2)}) copy-start(bf16[128,1024]{1,0:T(8,128)(2,1)} %param.12) | copy-start | bytes 786436
  6.5 167.0 %all-gather.9.cloned.1.call-start = ((), (), s32[]{:S(2)}) async-start(), calls=%async_computation.4 | async-start | bytes 3932160 | tf_op jit(solution)/shard_map/all_gather | solution.py:189
  7.3 166.3 %all-gather.11.cloned.1.call-start = ((), (), s32[]{:S(2)}) async-start(), calls=%async_computation.5 | async-start | bytes 3932160 | tf_op jit(solution)/shard_map/all_gather | solution.py:190
  8.0 165.5 %all-gather.13.cloned.1.call-start = ((), (), s32[]{:S(2)}) async-start(), calls=%async_computation.6 | async-start | bytes 3932160 | tf_op jit(solution)/shard_map/all_gather | solution.py:191
  17.3 9.7 %collective-permute-start = (bf16[256,256]{1,0:T(8,128)(2,1)S(1)}, bf16[256,256]{1,0:T(8,128)(2,1)S(1)}, u32[]{:S(2)}, u32[]{:S(2)}) collective-permute-start(bf16[256,256]{1,0:T(8,128)(2,1)S(1)} %all_gather.18), channel_id=1, source_target_pairs={{0,4},{2,6},{4,8},{6,10},{8,12},{10,14},{12,16},{14,18},{16,20},{1... | collective-permute-start | bytes 393224 | tf_op jit(solution)/shard_map/ppermute | solution.py:28
  18.6 8.5 %collective-permute-start.1 = (bf16[256,256]{1,0:T(8,128)(2,1)S(1)}, bf16[256,256]{1,0:T(8,128)(2,1)S(1)}, u32[]{:S(2)}, u32[]{:S(2)}) collective-permute-start(bf16[256,256]{1,0:T(8,128)(2,1)S(1)} %all_gather.18), channel_id=1, source_target_pairs={{0,2},{2,4},{4,6},{6,8},{8,10},{10,12},{12,14},{14,16},{16,18},{18... | collective-permute-start | bytes 393224 | tf_op jit(solution)/shard_map/ppermute | solution.py:28
  21.1 5.8 %collective-permute-start.3 = (f16[8,2048]{1,0:T(8,128)(2,1)S(1)}, f16[8,2048]{1,0:T(8,128)(2,1)S(1)}, u32[]{:S(2)}, u32[]{:S(2)}) collective-permute-start(f16[8,2048]{1,0:T(8,128)(2,1)S(1)} %multiply_convert_fusion.2), channel_id=1, source_target_pairs={{0,32},{32,0},{1,33},{33,1},{2,34},{34,2},{3,35},{35,3},{4,36},{36... | collective-permute-start | bytes 98312 | tf_op jit(solution)/shard_map/ppermute | solution.py:33
  29.5 45.4 %collective-permute-start.2 = (bf16[128,512]{1,0:T(8,128)(2,1)S(1)}, bf16[128,512]{1,0:T(8,128)(2,1)S(1)}, u32[]{:S(2)}, u32[]{:S(2)}) collective-permute-start(bf16[128,512]{1,0:T(8,128)(2,1)S(1)} %broadcast_select_fusion.2), channel_id=1, source_target_pairs={{0,64},{64,0},{1,65},{65,1},{2,66},{66,2},{3,67},{67,3},{4,68},{68... | collective-permute-start | bytes 393224 | tf_op jit(solution)/shard_map/ppermute | solution.py:33
  74.9 2.1 copy-start.1
  77.0 24.0 %all-to-all-start = ((bf16[8,32,2048]{2,1,0:T(8,128)(2,1)}), bf16[8,32,2048]{2,1,0:T(8,128)(2,1)S(1)}, u32[]{:S(2)}, u32[]{:S(2)}) async-start(bf16[8,32,2048]{2,1,0:T(8,128)(2,1)} %bitcast.188), calls=%async_computation | async-start | bytes 2097152 | tf_op jit(solution)/shard_map/all_to_all | solution.py:223
  83.6 17.6 %copy-start.3 = (bf16[1,32,2048]{2,1,0:T(8,128)(2,1)S(1)}, bf16[1,32,2048]{2,1,0:T(8,128)(2,1)}, u32[]{:S(2)}) copy-start(bf16[1,32,2048]{2,1,0:T(8,128)(2,1)} %param.16) | copy-start | bytes 393220
  84.4 17.0 %copy-start.4 = (f32[2048]{0:T(1024)S(1)}, f32[2048]{0:T(1024)}, u32[]{:S(2)}) copy-start(f32[2048]{0:T(1024)} %param.18) | copy-start | bytes 24580
  147.9 25.6 %all-to-all-start.1 = ((bf16[4,96,2048]{2,1,0:T(8,128)(2,1)}), bf16[4,96,2048]{2,1,0:T(8,128)(2,1)S(1)}, u32[]{:S(2)}, u32[]{:S(2)}) async-start(bf16[4,96,2048]{2,1,0:T(8,128)(2,1)} %bitcast.187), calls=%async_computation.1 | async-start | bytes 3145728 | tf_op jit(solution)/shard_map/all_to_all | solution.py:282
  173.5 1.1 copy-start.2
  183.9 17.0 %all-to-all-start.2 = ((bf16[8,24,2048]{2,1,0:T(8,128)(2,1)}), bf16[8,24,2048]{2,1,0:T(8,128)(2,1)S(1)}, u32[]{:S(2)}, u32[]{:S(2)}) async-start(bf16[8,24,2048]{2,1,0:T(8,128)(2,1)} %bitcast.189), calls=%async_computation.2 | async-start | bytes 1572864 | tf_op jit(solution)/shard_map/all_to_all | solution.py:287
  202.2 12.2 %collective-permute-start.7 = (bf16[64,2048]{1,0:T(8,128)(2,1)S(1)}, bf16[64,2048]{1,0:T(8,128)(2,1)S(1)}, u32[]{:S(2)}, u32[]{:S(2)}) collective-permute-start(bf16[64,2048]{1,0:T(8,128)(2,1)S(1)} %pad_maximum_fusion), channel_id=1, source_target_pairs={{0,4},{2,6},{4,8},{6,10},{8,12},{10,14},{12,16},{14,18},{16,20},{1... | collective-permute-start | bytes 786440 | tf_op jit(solution)/shard_map/ppermute | solution.py:33
  204.6 25.5 %all-to-all-start.3 = ((bf16[8,24,2048]{2,1,0:T(8,128)(2,1)}), bf16[8,24,2048]{2,1,0:T(8,128)(2,1)S(1)}, u32[]{:S(2)}, u32[]{:S(2)}) async-start(bf16[8,24,2048]{2,1,0:T(8,128)(2,1)} %bitcast.60), calls=%async_computation.3 | async-start | bytes 1572864 | tf_op jit(solution)/shard_map/all_to_all | solution.py:287
  209.2 17.8 %collective-permute-start.4 = (bf16[64,2048]{1,0:T(8,128)(2,1)}, bf16[64,2048]{1,0:T(8,128)(2,1)S(1)}, u32[]{:S(2)}, u32[]{:S(2)}) collective-permute-start(bf16[64,2048]{1,0:T(8,128)(2,1)} %concatenate.75), channel_id=1, source_target_pairs={{0,28},{2,30},{4,0},{6,2},{8,4},{10,6},{12,8},{14,10},{16,12},{18,... | collective-permute-start | bytes 786440 | tf_op jit(solution)/shard_map/ppermute | solution.py:33
  214.5 16.2 %collective-permute-start.8 = (bf16[64,2048]{1,0:T(8,128)(2,1)S(1)}, bf16[64,2048]{1,0:T(8,128)(2,1)S(1)}, u32[]{:S(2)}, u32[]{:S(2)}) collective-permute-start(bf16[64,2048]{1,0:T(8,128)(2,1)S(1)} %add_convert_fusion.2), channel_id=1, source_target_pairs={{0,4},{2,6},{4,8},{6,10},{8,12},{10,14},{12,16},{14,18},{16,20},{1... | collective-permute-start | bytes 786440 | tf_op jit(solution)/shard_map/ppermute | solution.py:33
  227.1 17.0 %collective-permute-start.5 = (bf16[64,2048]{1,0:T(8,128)(2,1)S(1)}, bf16[64,2048]{1,0:T(8,128)(2,1)S(1)}, u32[]{:S(2)}, u32[]{:S(2)}) collective-permute-start(bf16[64,2048]{1,0:T(8,128)(2,1)S(1)} %add_convert_fusion.4), channel_id=1, source_target_pairs={{0,28},{2,30},{4,0},{6,2},{8,4},{10,6},{12,8},{14,10},{16,12},{18,... | collective-permute-start | bytes 786440 | tf_op jit(solution)/shard_map/ppermute | solution.py:33
  230.7 16.5 %collective-permute-start.9 = (bf16[64,2048]{1,0:T(8,128)(2,1)S(1)}, bf16[64,2048]{1,0:T(8,128)(2,1)S(1)}, u32[]{:S(2)}, u32[]{:S(2)}) collective-permute-start(bf16[64,2048]{1,0:T(8,128)(2,1)S(1)} %add_convert_fusion.1), channel_id=1, source_target_pairs={{0,4},{2,6},{4,8},{6,10},{8,12},{10,14},{12,16},{14,18},{16,20},{1... | collective-permute-start | bytes 786440 | tf_op jit(solution)/shard_map/ppermute | solution.py:33
  244.2 16.2 %collective-permute-start.6 = (bf16[64,2048]{1,0:T(8,128)(2,1)S(1)}, bf16[64,2048]{1,0:T(8,128)(2,1)S(1)}, u32[]{:S(2)}, u32[]{:S(2)}) collective-permute-start(bf16[64,2048]{1,0:T(8,128)(2,1)S(1)} %add_convert_fusion.3), channel_id=1, source_target_pairs={{0,28},{2,30},{4,0},{6,2},{8,4},{10,6},{12,8},{14,10},{16,12},{18,... | collective-permute-start | bytes 786440 | tf_op jit(solution)/shard_map/ppermute | solution.py:33
  247.3 17.6 %collective-permute-start.10 = (bf16[32,2048]{1,0:T(8,128)(2,1)S(1)}, bf16[32,2048]{1,0:T(8,128)(2,1)S(1)}, u32[]{:S(2)}, u32[]{:S(2)}) collective-permute-start(bf16[32,2048]{1,0:T(8,128)(2,1)S(1)} %get-tuple-element.29), channel_id=1, source_target_pairs={{0,4},{2,6},{4,8},{6,10},{8,12},{10,14},{12,16},{14,18},{16,20},{1... | collective-permute-start | bytes 393224 | tf_op jit(solution)/shard_map/ppermute | solution.py:33
  252.4 12.4 %collective-permute-start.11 = (bf16[32,2048]{1,0:T(8,128)(2,1)S(1)}, bf16[32,2048]{1,0:T(8,128)(2,1)S(1)}, u32[]{:S(2)}, u32[]{:S(2)}) collective-permute-start(bf16[32,2048]{1,0:T(8,128)(2,1)S(1)} %get-tuple-element.30), channel_id=1, source_target_pairs={{0,2},{2,4},{4,6},{6,8},{8,10},{10,12},{12,14},{14,16},{16,18},{18... | collective-permute-start | bytes 393224 | tf_op jit(solution)/shard_map/ppermute | solution.py:33
  260.4 6.4 %collective-permute-start.12 = (bf16[32,2048]{1,0:T(8,128)(2,1)S(1)}, bf16[32,2048]{1,0:T(8,128)(2,1)S(1)}, u32[]{:S(2)}, u32[]{:S(2)}) collective-permute-start(bf16[32,2048]{1,0:T(8,128)(2,1)S(1)} %add_convert_fusion.6), channel_id=1, source_target_pairs={{0,30},{2,0},{4,2},{6,4},{8,6},{10,8},{12,10},{14,12},{16,14},{18,... | collective-permute-start | bytes 393224 | tf_op jit(solution)/shard_map/ppermute | solution.py:33
Sparse Core Ops, SparseCore 0:
  9.5 52.5 all-gather.8
  64.1 58.2 all-gather.10
  124.6 43.7 all-gather.12

commit v8 on v7

--- a/solution.py
+++ b/solution.py
@@ -264,6 +264,11 @@
     )
     gain = jnp.sum(jnp.where(match, table[None, top:], 0.0), axis=1)
 
+    send_rows = jnp.dot(send, column, preferred_element_type=F32)
+    send_rows = (send_rows * (1.0 / ROW_SCALE)).astype(BF)
+    rows = lax.all_to_all(send_rows, X, split_axis=0, concat_axis=0, tiled=True)
+    rows, rank, gain = lax.optimization_barrier((rows, rank, gain))
+
     def blocks_of(value, places):
         value = value.reshape(-1, nz, tok_sub)
         value = lax.dynamic_slice_in_dim(jnp.concatenate([value, value], 1), here, nz, 1)
@@ -277,9 +282,6 @@
 
     backs = back_for(far_places), back_for(near_places)
 
-    send_rows = jnp.dot(send, column, preferred_element_type=F32)
-    send_rows = (send_rows * (1.0 / ROW_SCALE)).astype(BF)
-    rows = lax.all_to_all(send_rows, X, split_axis=0, concat_axis=0, tiled=True)
     far, near = expert(rows, gate_all, up_all, down_all, nr, nc * cap)
     chunks = [None] * nz
 

time: 277 us -> 276 us (level)
  waiting for transfers between devices: 75 us -> 62.4 us
  starting transfers between devices: 66.1 us -> 78.4 us
    ppermute x11, waiting for transfers between devices: 27.8 us -> 15.5 us  [shift(): lax.ppermute(value, axis, [(i, (i + by) % devices) for i in range(devices)])]
    ppermute x11, starting transfers between devices: 43.9 us -> 56.2 us  [shift(): lax.ppermute(value, axis, [(i, (i + by) % devices) for i in range(devices)])]
  transfers between devices with their start and end apart: 20 -> 20, of which waited for: 8 -> 7; matrix products, arithmetic and copies ran while one was open for 7% -> 8% of each run, Pallas kernels for 0% -> 0%
where the time goes in v8:
time: 276 us; the launch traced here: 275 us
  blocking collectives  87.4 us (32%)
  starting transfers between devices  78.4 us (28%)
  waiting for transfers between devices  62.4 us (23%)
  between operations  13.8 us (5%)
  Pallas kernels  9.21 us (3%)
  local copies, waits for them, and re-layouts  8.88 us (3%)
  matrix products  8.35 us (3%)
  other arithmetic  6.97 us (3%)
    ppermute x11, starting transfers between devices, shift(): lax.ppermute(value, axis, [(i, (i + by) % devices) for i in range(devices)])  56.2 us
    all_gather x1, blocking collectives, on_device(): column = lax.all_gather(column, ZC, axis=0, tiled=True).astype(BF)  43.4 us
    all_gather x1, blocking collectives, on_device(): z_all = lax.all_gather(pair_rows, ZC, axis=0, tiled=True)  35.6 us
    all_to_all x1, waiting for transfers between devices, on_device(): rows = lax.all_to_all(send_rows, X, split_axis=0, concat_axis=0, tiled=True)  18.5 us
    all_to_all x1, waiting for transfers between devices, on_device(): lax.all_to_all(partial_value, ('rep', 'xh'), split_axis=0, concat_axis=0,...  16.4 us
    ppermute x11, waiting for transfers between devices, shift(): lax.ppermute(value, axis, [(i, (i + by) % devices) for i in range(devices)])  15.5 us
    all_to_all x2, waiting for transfers between devices, spread_out(): returned = lax.all_to_all(out, XC, split_axis=0, concat_axis=0, tiled=True)  10.6 us
    all_to_all x2, starting transfers between devices, spread_out(): returned = lax.all_to_all(out, XC, split_axis=0, concat_axis=0, tiled=True)  9.35 us
  transfers between devices with their start and end apart: 20, of which 7 were waited for; matrix products, arithmetic and copies ran while one was open for 8% of the time, Pallas kernels for 0%

profile of v8, /device:TPU:1, one launch (start us, length us, event | category | flops | bytes accessed | tf_op | source)
XLA Modules:
  0.0 275.4 jit_solution(14451249931910382948)
XLA Ops:
  8.8 8.4 %all_gather.18 = bf16[256,256]{1,0:T(8,128)(2,1)S(1)} all-gather(bf16[128,256]{1,0:T(8,128)(2,1)S(1)} %pad_maximum_fusion.2), channel_id=1, replica_groups=mesh['rep'=4,'xh'=2,'xl'=2,'z'=16,'core'=2] {'core'}, dimensions={0}, use_global_device_ids=true | all-gather | bytes 196608 | tf_op jit(solution)/shard_map/all_gather | solution.py:45
  17.3 1.3 collective-permute-start
  18.6 1.8 collective-permute-start.1
  21.1 3.1 %collective-permute-start.3 = (f16[8,2048]{1,0:T(8,128)(2,1)S(1)}, f16[8,2048]{1,0:T(8,128)(2,1)S(1)}, u32[]{:S(2)}, u32[]{:S(2)}) collective-permute-start(f16[8,2048]{1,0:T(8,128)(2,1)S(1)} %multiply_convert_fusion.2), channel_id=1, source_target_pairs={{0,32},{32,0},{1,33},{33,1},{2,34},{34,2},{3,35},{35,3},{4,36},{36... | collective-permute-start | bytes 98312 | tf_op jit(solution)/shard_map/ppermute | solution.py:33
  29.5 9.8 %collective-permute-start.2 = (bf16[128,512]{1,0:T(8,128)(2,1)S(1)}, bf16[128,512]{1,0:T(8,128)(2,1)S(1)}, u32[]{:S(2)}, u32[]{:S(2)}) collective-permute-start(bf16[128,512]{1,0:T(8,128)(2,1)S(1)} %broadcast_select_fusion.2), channel_id=1, source_target_pairs={{0,64},{64,0},{1,65},{65,1},{2,66},{66,2},{3,67},{67,3},{4,68},{68... | collective-permute-start | bytes 393224 | tf_op jit(solution)/shard_map/ppermute | solution.py:33
  39.3 35.6 %all-gather.14 = f16[512,2304]{1,0:T(8,128)(2,1)S(1)} all-gather(f16[16,2304]{1,0:T(8,128)(2,1)S(1)} %pad_maximum_fusion.1), channel_id=1, replica_groups=mesh['rep'=4,'xh'=2,'xl'=2,'z'=16,'core'=2] {'z','core'}, dimensions={0}, use_global_device_ids=true | all-gather | bytes 2433024 | tf_op jit(solution)/shard_map/all_gather | solution.py:209
  75.0 2.0 fusion.9
  77.0 4.5 %all-to-all-start = ((bf16[8,32,2048]{2,1,0:T(8,128)(2,1)}), bf16[8,32,2048]{2,1,0:T(8,128)(2,1)S(1)}, u32[]{:S(2)}, u32[]{:S(2)}) async-start(bf16[8,32,2048]{2,1,0:T(8,128)(2,1)} %bitcast.194), calls=%async_computation | async-start | bytes 2097152 | tf_op jit(solution)/shard_map/all_to_all | solution.py:223
  84.7 16.4 %all-to-all-done = bf16[8,32,2048]{2,1,0:T(8,128)(2,1)S(1)} async-done(((bf16[8,32,2048]{2,1,0:T(8,128)(2,1)}), bf16[8,32,2048]{2,1,0:T(8,128)(2,1)S(1)}, u32[]{:S(2)}, u32[]{:S(2)}) %all-to-all-start) | async-done | bytes 1048608 | tf_op jit(solution)/shard_map/all_to_all | solution.py:223
  101.5 43.4 %all-gather.15 = f16[1024,2048]{1,0:T(8,128)(2,1)S(1)} all-gather(f16[32,2048]{1,0:T(8,128)(2,1)S(1)} %fusion.46), channel_id=1, replica_groups=mesh['rep'=4,'xh'=2,'xl'=2,'z'=16,'core'=2] {'z','core'}, dimensions={0}, use_global_device_ids=true | all-gather | bytes 4325376 | tf_op jit(solution)/shard_map/all_gather | solution.py:229
  144.9 3.0 %multiply_convert_fusion = bf16[384,2048]{1,0:T(8,128)(2,1)} fusion(pred[384,1024]{1,0:T(32,128)(4,1)S(1)} %bitcast_compare_fusion, f16[1024,2048]{1,0:T(8,128)(2,1)S(1)} %all-gather.15), kind=kOutput, calls=%fused_computation.6 | convolution fusion | flops 1614282752 | bytes 6160384 | tf_op jit(solution)/shard_map/dot_general | solution.py:267
  147.9 5.2 %all-to-all-start.1 = ((bf16[4,96,2048]{2,1,0:T(8,128)(2,1)}), bf16[4,96,2048]{2,1,0:T(8,128)(2,1)S(1)}, u32[]{:S(2)}, u32[]{:S(2)}) async-start(bf16[4,96,2048]{2,1,0:T(8,128)(2,1)} %bitcast.193), calls=%async_computation.1 | async-start | bytes 3145728 | tf_op jit(solution)/shard_map/all_to_all | solution.py:269
  155.0 18.5 %all-to-all-done.1 = bf16[4,96,2048]{2,1,0:T(8,128)(2,1)S(1)} async-done(((bf16[4,96,2048]{2,1,0:T(8,128)(2,1)}), bf16[4,96,2048]{2,1,0:T(8,128)(2,1)S(1)}, u32[]{:S(2)}, u32[]{:S(2)}) %all-to-all-start.1) | async-done | bytes 1572896 | tf_op jit(solution)/shard_map/all_to_all | solution.py:269
  173.5 1.1 copy-done.2
  174.7 9.2 %shard_map.118 = (bf16[192,2048]{1,0:T(8,128)(2,1)}, bf16[192,2048]{1,0:T(8,128)(2,1)}) custom-call(bf16[384,2048]{1,0:T(8,128)(2,1)} %bitcast.192, bf16[768,2048]{1,0:T(8,128)(2,1)} %bitcast.235, bf16[768,2048]{1,0:T(8,128)(2,1)} %bitcast.236, bf16[4,768,512]{2,1,0:T(8,128)(2,1)} %bitcast.237), custom_call_target="tpu_custom_call" | custom-call | flops 3623878656 | bytes 12582912 | tf_op jit(solution)/shard_map/pallas_call | solution.py:121
  183.9 4.7 %all-to-all-start.2 = ((bf16[8,24,2048]{2,1,0:T(8,128)(2,1)}), bf16[8,24,2048]{2,1,0:T(8,128)(2,1)S(1)}, u32[]{:S(2)}, u32[]{:S(2)}) async-start(bf16[8,24,2048]{2,1,0:T(8,128)(2,1)} %bitcast.195), calls=%async_computation.2 | async-start | bytes 1572864 | tf_op jit(solution)/shard_map/all_to_all | solution.py:289
  190.3 10.6 %all-to-all-done.2 = bf16[8,24,2048]{2,1,0:T(8,128)(2,1)S(1)} async-done(((bf16[8,24,2048]{2,1,0:T(8,128)(2,1)}), bf16[8,24,2048]{2,1,0:T(8,128)(2,1)S(1)}, u32[]{:S(2)}, u32[]{:S(2)}) %all-to-all-start.2) | async-done | bytes 786464 | tf_op jit(solution)/shard_map/all_to_all | solution.py:289
  201.5 2.6 collective-permute-start.4
  204.1 1.4 concatenate.65
  206.2 4.6 %all-to-all-start.3 = ((bf16[8,24,2048]{2,1,0:T(8,128)(2,1)}), bf16[8,24,2048]{2,1,0:T(8,128)(2,1)S(1)}, u32[]{:S(2)}, u32[]{:S(2)}) async-start(bf16[8,24,2048]{2,1,0:T(8,128)(2,1)} %bitcast.60), calls=%async_computation.3 | async-start | bytes 1572864 | tf_op jit(solution)/shard_map/all_to_all | solution.py:289
  210.9 3.6 %collective-permute-start.7 = (bf16[64,2048]{1,0:T(8,128)(2,1)S(1)}, bf16[64,2048]{1,0:T(8,128)(2,1)S(1)}, u32[]{:S(2)}, u32[]{:S(2)}) collective-permute-start(bf16[64,2048]{1,0:T(8,128)(2,1)S(1)} %pad_maximum_fusion), channel_id=1, source_target_pairs={{0,4},{2,6},{4,8},{6,10},{8,12},{10,14},{12,16},{14,18},{16,20},{1... | collective-permute-start | bytes 786440 | tf_op jit(solution)/shard_map/ppermute | solution.py:33
  214.5 3.8 %collective-permute-start.5 = (bf16[64,2048]{1,0:T(8,128)(2,1)S(1)}, bf16[64,2048]{1,0:T(8,128)(2,1)S(1)}, u32[]{:S(2)}, u32[]{:S(2)}) collective-permute-start(bf16[64,2048]{1,0:T(8,128)(2,1)S(1)} %add_convert_fusion.4), channel_id=1, source_target_pairs={{0,28},{2,30},{4,0},{6,2},{8,4},{10,6},{12,8},{14,10},{16,12},{18,... | collective-permute-start | bytes 786440 | tf_op jit(solution)/shard_map/ppermute | solution.py:33
  218.3 4.4 %collective-permute-done.7 = bf16[64,2048]{1,0:T(8,128)(2,1)S(1)} collective-permute-done((bf16[64,2048]{1,0:T(8,128)(2,1)S(1)}, bf16[64,2048]{1,0:T(8,128)(2,1)S(1)}, u32[]{:S(2)}, u32[]{:S(2)}) %collective-permute-start.7) | collective-permute-done | bytes 262176 | tf_op jit(solution)/shard_map/ppermute | solution.py:33
  222.8 2.4 collective-permute-start.8
  225.8 5.0 %collective-permute-start.6 = (bf16[64,2048]{1,0:T(8,128)(2,1)S(1)}, bf16[64,2048]{1,0:T(8,128)(2,1)S(1)}, u32[]{:S(2)}, u32[]{:S(2)}) collective-permute-start(bf16[64,2048]{1,0:T(8,128)(2,1)S(1)} %add_convert_fusion.3), channel_id=1, source_target_pairs={{0,28},{2,30},{4,0},{6,2},{8,4},{10,6},{12,8},{14,10},{16,12},{18,... | collective-permute-start | bytes 786440 | tf_op jit(solution)/shard_map/ppermute | solution.py:33
  230.8 2.5 collective-permute-done.8
  233.4 5.0 %collective-permute-start.9 = (bf16[64,2048]{1,0:T(8,128)(2,1)S(1)}, bf16[64,2048]{1,0:T(8,128)(2,1)S(1)}, u32[]{:S(2)}, u32[]{:S(2)}) collective-permute-start(bf16[64,2048]{1,0:T(8,128)(2,1)S(1)} %add_convert_fusion.1), channel_id=1, source_target_pairs={{0,4},{2,6},{4,8},{6,10},{8,12},{10,14},{12,16},{14,18},{16,20},{1... | collective-permute-start | bytes 786440 | tf_op jit(solution)/shard_map/ppermute | solution.py:33
  238.4 12.8 %collective-permute-start.12 = (bf16[32,2048]{1,0:T(8,128)(2,1)S(1)}, bf16[32,2048]{1,0:T(8,128)(2,1)S(1)}, u32[]{:S(2)}, u32[]{:S(2)}) collective-permute-start(bf16[32,2048]{1,0:T(8,128)(2,1)S(1)} %add_convert_fusion.6), channel_id=1, source_target_pairs={{0,30},{2,0},{4,2},{6,4},{8,6},{10,8},{12,10},{14,12},{16,14},{18,... | collective-permute-start | bytes 393224 | tf_op jit(solution)/shard_map/ppermute | solution.py:33
  251.4 4.4 %collective-permute-start.11 = (bf16[32,2048]{1,0:T(8,128)(2,1)S(1)}, bf16[32,2048]{1,0:T(8,128)(2,1)S(1)}, u32[]{:S(2)}, u32[]{:S(2)}) collective-permute-start(bf16[32,2048]{1,0:T(8,128)(2,1)S(1)} %get-tuple-element.36), channel_id=1, source_target_pairs={{0,2},{2,4},{4,6},{6,8},{8,10},{10,12},{12,14},{14,16},{16,18},{18... | collective-permute-start | bytes 393224 | tf_op jit(solution)/shard_map/ppermute | solution.py:33
  255.8 3.8 %collective-permute-start.10 = (bf16[32,2048]{1,0:T(8,128)(2,1)S(1)}, bf16[32,2048]{1,0:T(8,128)(2,1)S(1)}, u32[]{:S(2)}, u32[]{:S(2)}) collective-permute-start(bf16[32,2048]{1,0:T(8,128)(2,1)S(1)} %get-tuple-element.35), channel_id=1, source_target_pairs={{0,4},{2,6},{4,8},{6,10},{8,12},{10,14},{12,16},{14,18},{16,20},{1... | collective-permute-start | bytes 393224 | tf_op jit(solution)/shard_map/ppermute | solution.py:33
  259.5 1.9 collective-permute-done.11
  261.4 6.7 %collective-permute-done.10 = bf16[32,2048]{1,0:T(8,128)(2,1)S(1)} collective-permute-done((bf16[32,2048]{1,0:T(8,128)(2,1)S(1)}, bf16[32,2048]{1,0:T(8,128)(2,1)S(1)}, u32[]{:S(2)}, u32[]{:S(2)}) %collective-permute-start.10) | collective-permute-done | bytes 131104 | tf_op jit(solution)/shard_map/ppermute | solution.py:33
  (109 shorter events, 18.2 us)
Async XLA Ops:
  6.5 20.5 %copy-start = (bf16[128,1024]{1,0:T(8,128)(2,1)S(1)}, bf16[128,1024]{1,0:T(8,128)(2,1)}, u32[]{:S(2)}) copy-start(bf16[128,1024]{1,0:T(8,128)(2,1)} %param.12) | copy-start | bytes 786436
  6.5 167.0 %all-gather.9.cloned.1.call-start = ((), (), s32[]{:S(2)}) async-start(), calls=%async_computation.4 | async-start | bytes 3932160 | tf_op jit(solution)/shard_map/all_gather | solution.py:189
  7.3 166.3 %all-gather.11.cloned.1.call-start = ((), (), s32[]{:S(2)}) async-start(), calls=%async_computation.5 | async-start | bytes 3932160 | tf_op jit(solution)/shard_map/all_gather | solution.py:190
  8.0 165.5 %all-gather.13.cloned.1.call-start = ((), (), s32[]{:S(2)}) async-start(), calls=%async_computation.6 | async-start | bytes 3932160 | tf_op jit(solution)/shard_map/all_gather | solution.py:191
  17.3 9.7 %collective-permute-start = (bf16[256,256]{1,0:T(8,128)(2,1)S(1)}, bf16[256,256]{1,0:T(8,128)(2,1)S(1)}, u32[]{:S(2)}, u32[]{:S(2)}) collective-permute-start(bf16[256,256]{1,0:T(8,128)(2,1)S(1)} %all_gather.18), channel_id=1, source_target_pairs={{0,4},{2,6},{4,8},{6,10},{8,12},{10,14},{12,16},{14,18},{16,20},{1... | collective-permute-start | bytes 393224 | tf_op jit(solution)/shard_map/ppermute | solution.py:28
  18.6 8.5 %collective-permute-start.1 = (bf16[256,256]{1,0:T(8,128)(2,1)S(1)}, bf16[256,256]{1,0:T(8,128)(2,1)S(1)}, u32[]{:S(2)}, u32[]{:S(2)}) collective-permute-start(bf16[256,256]{1,0:T(8,128)(2,1)S(1)} %all_gather.18), channel_id=1, source_target_pairs={{0,2},{2,4},{4,6},{6,8},{8,10},{10,12},{12,14},{14,16},{16,18},{18... | collective-permute-start | bytes 393224 | tf_op jit(solution)/shard_map/ppermute | solution.py:28
  21.1 5.8 %collective-permute-start.3 = (f16[8,2048]{1,0:T(8,128)(2,1)S(1)}, f16[8,2048]{1,0:T(8,128)(2,1)S(1)}, u32[]{:S(2)}, u32[]{:S(2)}) collective-permute-start(f16[8,2048]{1,0:T(8,128)(2,1)S(1)} %multiply_convert_fusion.2), channel_id=1, source_target_pairs={{0,32},{32,0},{1,33},{33,1},{2,34},{34,2},{3,35},{35,3},{4,36},{36... | collective-permute-start | bytes 98312 | tf_op jit(solution)/shard_map/ppermute | solution.py:33
  29.5 45.4 %collective-permute-start.2 = (bf16[128,512]{1,0:T(8,128)(2,1)S(1)}, bf16[128,512]{1,0:T(8,128)(2,1)S(1)}, u32[]{:S(2)}, u32[]{:S(2)}) collective-permute-start(bf16[128,512]{1,0:T(8,128)(2,1)S(1)} %broadcast_select_fusion.2), channel_id=1, source_target_pairs={{0,64},{64,0},{1,65},{65,1},{2,66},{66,2},{3,67},{67,3},{4,68},{68... | collective-permute-start | bytes 393224 | tf_op jit(solution)/shard_map/ppermute | solution.py:33
  74.9 2.1 copy-start.1
  77.0 24.0 %all-to-all-start = ((bf16[8,32,2048]{2,1,0:T(8,128)(2,1)}), bf16[8,32,2048]{2,1,0:T(8,128)(2,1)S(1)}, u32[]{:S(2)}, u32[]{:S(2)}) async-start(bf16[8,32,2048]{2,1,0:T(8,128)(2,1)} %bitcast.194), calls=%async_computation | async-start | bytes 2097152 | tf_op jit(solution)/shard_map/all_to_all | solution.py:223
  83.0 18.2 %copy-start.3 = (bf16[1,32,2048]{2,1,0:T(8,128)(2,1)S(1)}, bf16[1,32,2048]{2,1,0:T(8,128)(2,1)}, u32[]{:S(2)}) copy-start(bf16[1,32,2048]{2,1,0:T(8,128)(2,1)} %param.16) | copy-start | bytes 393220
  83.0 18.3 %copy-start.4 = (f32[2048]{0:T(1024)S(1)}, f32[2048]{0:T(1024)}, u32[]{:S(2)}) copy-start(f32[2048]{0:T(1024)} %param.18) | copy-start | bytes 24580
  147.9 25.6 %all-to-all-start.1 = ((bf16[4,96,2048]{2,1,0:T(8,128)(2,1)}), bf16[4,96,2048]{2,1,0:T(8,128)(2,1)S(1)}, u32[]{:S(2)}, u32[]{:S(2)}) async-start(bf16[4,96,2048]{2,1,0:T(8,128)(2,1)} %bitcast.193), calls=%async_computation.1 | async-start | bytes 3145728 | tf_op jit(solution)/shard_map/all_to_all | solution.py:269
  173.5 1.1 copy-start.2
  183.9 17.0 %all-to-all-start.2 = ((bf16[8,24,2048]{2,1,0:T(8,128)(2,1)}), bf16[8,24,2048]{2,1,0:T(8,128)(2,1)S(1)}, u32[]{:S(2)}, u32[]{:S(2)}) async-start(bf16[8,24,2048]{2,1,0:T(8,128)(2,1)} %bitcast.195), calls=%async_computation.2 | async-start | bytes 1572864 | tf_op jit(solution)/shard_map/all_to_all | solution.py:289
  201.5 13.0 %collective-permute-start.4 = (bf16[64,2048]{1,0:T(8,128)(2,1)S(1)}, bf16[64,2048]{1,0:T(8,128)(2,1)S(1)}, u32[]{:S(2)}, u32[]{:S(2)}) collective-permute-start(bf16[64,2048]{1,0:T(8,128)(2,1)S(1)} %concatenate.75), channel_id=1, source_target_pairs={{0,28},{2,30},{4,0},{6,2},{8,4},{10,6},{12,8},{14,10},{16,12},{18,... | collective-permute-start | bytes 786440 | tf_op jit(solution)/shard_map/ppermute | solution.py:33
  205.5 19.8 %copy-start.5 = (bf16[8,256]{1,0:T(8,128)(2,1)S(1)}, bf16[8,256]{1,0:T(8,128)(2,1)}, u32[]{:S(2)}) copy-start(bf16[8,256]{1,0:T(8,128)(2,1)} %concatenate.65) | copy-start | bytes 12292
  206.2 19.0 %all-to-all-start.3 = ((bf16[8,24,2048]{2,1,0:T(8,128)(2,1)}), bf16[8,24,2048]{2,1,0:T(8,128)(2,1)S(1)}, u32[]{:S(2)}, u32[]{:S(2)}) async-start(bf16[8,24,2048]{2,1,0:T(8,128)(2,1)} %bitcast.60), calls=%async_computation.3 | async-start | bytes 1572864 | tf_op jit(solution)/shard_map/all_to_all | solution.py:289
  210.9 11.9 %collective-permute-start.7 = (bf16[64,2048]{1,0:T(8,128)(2,1)S(1)}, bf16[64,2048]{1,0:T(8,128)(2,1)S(1)}, u32[]{:S(2)}, u32[]{:S(2)}) collective-permute-start(bf16[64,2048]{1,0:T(8,128)(2,1)S(1)} %pad_maximum_fusion), channel_id=1, source_target_pairs={{0,4},{2,6},{4,8},{6,10},{8,12},{10,14},{12,16},{14,18},{16,20},{1... | collective-permute-start | bytes 786440 | tf_op jit(solution)/shard_map/ppermute | solution.py:33
  214.5 11.2 %collective-permute-start.5 = (bf16[64,2048]{1,0:T(8,128)(2,1)S(1)}, bf16[64,2048]{1,0:T(8,128)(2,1)S(1)}, u32[]{:S(2)}, u32[]{:S(2)}) collective-permute-start(bf16[64,2048]{1,0:T(8,128)(2,1)S(1)} %add_convert_fusion.4), channel_id=1, source_target_pairs={{0,28},{2,30},{4,0},{6,2},{8,4},{10,6},{12,8},{14,10},{16,12},{18,... | collective-permute-start | bytes 786440 | tf_op jit(solution)/shard_map/ppermute | solution.py:33
  222.8 10.5 %collective-permute-start.8 = (bf16[64,2048]{1,0:T(8,128)(2,1)S(1)}, bf16[64,2048]{1,0:T(8,128)(2,1)S(1)}, u32[]{:S(2)}, u32[]{:S(2)}) collective-permute-start(bf16[64,2048]{1,0:T(8,128)(2,1)S(1)} %add_convert_fusion.2), channel_id=1, source_target_pairs={{0,4},{2,6},{4,8},{6,10},{8,12},{10,14},{12,16},{14,18},{16,20},{1... | collective-permute-start | bytes 786440 | tf_op jit(solution)/shard_map/ppermute | solution.py:33
  225.8 12.6 %collective-permute-start.6 = (bf16[64,2048]{1,0:T(8,128)(2,1)S(1)}, bf16[64,2048]{1,0:T(8,128)(2,1)S(1)}, u32[]{:S(2)}, u32[]{:S(2)}) collective-permute-start(bf16[64,2048]{1,0:T(8,128)(2,1)S(1)} %add_convert_fusion.3), channel_id=1, source_target_pairs={{0,28},{2,30},{4,0},{6,2},{8,4},{10,6},{12,8},{14,10},{16,12},{18,... | collective-permute-start | bytes 786440 | tf_op jit(solution)/shard_map/ppermute | solution.py:33
  233.4 17.9 %collective-permute-start.9 = (bf16[64,2048]{1,0:T(8,128)(2,1)S(1)}, bf16[64,2048]{1,0:T(8,128)(2,1)S(1)}, u32[]{:S(2)}, u32[]{:S(2)}) collective-permute-start(bf16[64,2048]{1,0:T(8,128)(2,1)S(1)} %add_convert_fusion.1), channel_id=1, source_target_pairs={{0,4},{2,6},{4,8},{6,10},{8,12},{10,14},{12,16},{14,18},{16,20},{1... | collective-permute-start | bytes 786440 | tf_op jit(solution)/shard_map/ppermute | solution.py:33
  238.4 21.1 %collective-permute-start.12 = (bf16[32,2048]{1,0:T(8,128)(2,1)S(1)}, bf16[32,2048]{1,0:T(8,128)(2,1)S(1)}, u32[]{:S(2)}, u32[]{:S(2)}) collective-permute-start(bf16[32,2048]{1,0:T(8,128)(2,1)S(1)} %add_convert_fusion.6), channel_id=1, source_target_pairs={{0,30},{2,0},{4,2},{6,4},{8,6},{10,8},{12,10},{14,12},{16,14},{18,... | collective-permute-start | bytes 393224 | tf_op jit(solution)/shard_map/ppermute | solution.py:33
  251.4 10.0 %collective-permute-start.11 = (bf16[32,2048]{1,0:T(8,128)(2,1)S(1)}, bf16[32,2048]{1,0:T(8,128)(2,1)S(1)}, u32[]{:S(2)}, u32[]{:S(2)}) collective-permute-start(bf16[32,2048]{1,0:T(8,128)(2,1)S(1)} %get-tuple-element.36), channel_id=1, source_target_pairs={{0,2},{2,4},{4,6},{6,8},{8,10},{10,12},{12,14},{14,16},{16,18},{18... | collective-permute-start | bytes 393224 | tf_op jit(solution)/shard_map/ppermute | solution.py:33
  255.8 12.3 %collective-permute-start.10 = (bf16[32,2048]{1,0:T(8,128)(2,1)S(1)}, bf16[32,2048]{1,0:T(8,128)(2,1)S(1)}, u32[]{:S(2)}, u32[]{:S(2)}) collective-permute-start(bf16[32,2048]{1,0:T(8,128)(2,1)S(1)} %get-tuple-element.35), channel_id=1, source_target_pairs={{0,4},{2,6},{4,8},{6,10},{8,12},{10,14},{12,16},{14,18},{16,20},{1... | collective-permute-start | bytes 393224 | tf_op jit(solution)/shard_map/ppermute | solution.py:33
Sparse Core Ops, SparseCore 0:
  9.5 52.5 all-gather.8
  64.1 58.2 all-gather.10
  124.6 43.7 all-gather.12

commit v9 on v7

--- a/solution.py
+++ b/solution.py
@@ -252,6 +252,11 @@
     seats = jnp.arange(2 * nc * cap, dtype=jnp.int32)
     send = (seat[:, None, :] == seats[None, :, None]).astype(BF).reshape(-1, count)
 
+    send_rows = jnp.dot(send, column, preferred_element_type=F32)
+    send_rows = (send_rows * (1.0 / ROW_SCALE)).astype(BF)
+    rows = lax.all_to_all(send_rows, X, split_axis=0, concat_axis=0, tiled=True)
+    rows, table = lax.optimization_barrier((rows, table))
+
     table = table.reshape(2 * top, nz, nc, tok_sub)
     table = lax.dynamic_slice_in_dim(table, core, 1, 2).reshape(2 * top, -1)
     lane = jnp.arange(nx * nc, dtype=jnp.int32)
@@ -277,9 +282,6 @@
 
     backs = back_for(far_places), back_for(near_places)
 
-    send_rows = jnp.dot(send, column, preferred_element_type=F32)
-    send_rows = (send_rows * (1.0 / ROW_SCALE)).astype(BF)
-    rows = lax.all_to_all(send_rows, X, split_axis=0, concat_axis=0, tiled=True)
     far, near = expert(rows, gate_all, up_all, down_all, nr, nc * cap)
     chunks = [None] * nz
 

time: 277 us -> 277 us (level)
  waiting for transfers between devices: 75 us -> 62.1 us
  starting transfers between devices: 66.1 us -> 78.4 us
    ppermute x11, waiting for transfers between devices: 27.8 us -> 15.5 us  [shift(): lax.ppermute(value, axis, [(i, (i + by) % devices) for i in range(devices)])]
    ppermute x11, starting transfers between devices: 43.9 us -> 56.2 us  [shift(): lax.ppermute(value, axis, [(i, (i + by) % devices) for i in range(devices)])]
  transfers between devices with their start and end apart: 20 -> 20, of which waited for: 8 -> 7; matrix products, arithmetic and copies ran while one was open for 7% -> 8% of each run, Pallas kernels for 0% -> 0%
where the time goes in v9:
time: 277 us; the launch traced here: 276 us
  blocking collectives  87.4 us (32%)
  starting transfers between devices  78.4 us (28%)
  waiting for transfers between devices  62.1 us (22%)
  between operations  13.8 us (5%)
  Pallas kernels  9.21 us (3%)
  local copies, waits for them, and re-layouts  8.35 us (3%)
  matrix products  8.35 us (3%)
  other arithmetic  7.97 us (3%)
    ppermute x11, starting transfers between devices, shift(): lax.ppermute(value, axis, [(i, (i + by) % devices) for i in range(devices)])  56.2 us
    all_gather x1, blocking collectives, on_device(): column = lax.all_gather(column, ZC, axis=0, tiled=True).astype(BF)  43.4 us
    all_gather x1, blocking collectives, on_device(): z_all = lax.all_gather(pair_rows, ZC, axis=0, tiled=True)  35.6 us
    all_to_all x1, waiting for transfers between devices, on_device(): rows = lax.all_to_all(send_rows, X, split_axis=0, concat_axis=0, tiled=True)  19.6 us
    ppermute x11, waiting for transfers between devices, shift(): lax.ppermute(value, axis, [(i, (i + by) % devices) for i in range(devices)])  15.5 us
    all_to_all x1, waiting for transfers between devices, on_device(): lax.all_to_all(partial_value, ('rep', 'xh'), split_axis=0, concat_axis=0,...  15.1 us
    all_to_all x2, waiting for transfers between devices, spread_out(): returned = lax.all_to_all(out, XC, split_axis=0, concat_axis=0, tiled=True)  10.5 us
    all_to_all x2, starting transfers between devices, spread_out(): returned = lax.all_to_all(out, XC, split_axis=0, concat_axis=0, tiled=True)  9.33 us
  transfers between devices with their start and end apart: 20, of which 7 were waited for; matrix products, arithmetic and copies ran while one was open for 8% of the time, Pallas kernels for 0%

profile of v9, /device:TPU:1, one launch (start us, length us, event | category | flops | bytes accessed | tf_op | source)
XLA Modules:
  0.0 275.6 jit_solution(1306470646664684879)
XLA Ops:
  8.8 8.4 %all_gather.18 = bf16[256,256]{1,0:T(8,128)(2,1)S(1)} all-gather(bf16[128,256]{1,0:T(8,128)(2,1)S(1)} %pad_maximum_fusion.2), channel_id=1, replica_groups=mesh['rep'=4,'xh'=2,'xl'=2,'z'=16,'core'=2] {'core'}, dimensions={0}, use_global_device_ids=true | all-gather | bytes 196608 | tf_op jit(solution)/shard_map/all_gather | solution.py:45
  17.3 1.3 collective-permute-start
  18.6 1.8 collective-permute-start.1
  21.1 3.1 %collective-permute-start.3 = (f16[8,2048]{1,0:T(8,128)(2,1)S(1)}, f16[8,2048]{1,0:T(8,128)(2,1)S(1)}, u32[]{:S(2)}, u32[]{:S(2)}) collective-permute-start(f16[8,2048]{1,0:T(8,128)(2,1)S(1)} %multiply_convert_fusion.2), channel_id=1, source_target_pairs={{0,32},{32,0},{1,33},{33,1},{2,34},{34,2},{3,35},{35,3},{4,36},{36... | collective-permute-start | bytes 98312 | tf_op jit(solution)/shard_map/ppermute | solution.py:33
  29.5 9.8 %collective-permute-start.2 = (bf16[128,512]{1,0:T(8,128)(2,1)S(1)}, bf16[128,512]{1,0:T(8,128)(2,1)S(1)}, u32[]{:S(2)}, u32[]{:S(2)}) collective-permute-start(bf16[128,512]{1,0:T(8,128)(2,1)S(1)} %broadcast_select_fusion.2), channel_id=1, source_target_pairs={{0,64},{64,0},{1,65},{65,1},{2,66},{66,2},{3,67},{67,3},{4,68},{68... | collective-permute-start | bytes 393224 | tf_op jit(solution)/shard_map/ppermute | solution.py:33
  39.3 35.6 %all-gather.14 = f16[512,2304]{1,0:T(8,128)(2,1)S(1)} all-gather(f16[16,2304]{1,0:T(8,128)(2,1)S(1)} %pad_maximum_fusion.1), channel_id=1, replica_groups=mesh['rep'=4,'xh'=2,'xl'=2,'z'=16,'core'=2] {'z','core'}, dimensions={0}, use_global_device_ids=true | all-gather | bytes 2433024 | tf_op jit(solution)/shard_map/all_gather | solution.py:209
  75.0 2.0 fusion.9
  77.0 4.5 %all-to-all-start = ((bf16[8,32,2048]{2,1,0:T(8,128)(2,1)}), bf16[8,32,2048]{2,1,0:T(8,128)(2,1)S(1)}, u32[]{:S(2)}, u32[]{:S(2)}) async-start(bf16[8,32,2048]{2,1,0:T(8,128)(2,1)} %bitcast.184), calls=%async_computation | async-start | bytes 2097152 | tf_op jit(solution)/shard_map/all_to_all | solution.py:223
  81.5 1.1 fusion.101
  85.9 15.1 %all-to-all-done = bf16[8,32,2048]{2,1,0:T(8,128)(2,1)S(1)} async-done(((bf16[8,32,2048]{2,1,0:T(8,128)(2,1)}), bf16[8,32,2048]{2,1,0:T(8,128)(2,1)S(1)}, u32[]{:S(2)}, u32[]{:S(2)}) %all-to-all-start) | async-done | bytes 1048608 | tf_op jit(solution)/shard_map/all_to_all | solution.py:223
  101.4 43.4 %all-gather.15 = f16[1024,2048]{1,0:T(8,128)(2,1)S(1)} all-gather(f16[32,2048]{1,0:T(8,128)(2,1)S(1)} %fusion.46), channel_id=1, replica_groups=mesh['rep'=4,'xh'=2,'xl'=2,'z'=16,'core'=2] {'z','core'}, dimensions={0}, use_global_device_ids=true | all-gather | bytes 4325376 | tf_op jit(solution)/shard_map/all_gather | solution.py:229
  144.9 3.0 %multiply_convert_fusion = bf16[384,2048]{1,0:T(8,128)(2,1)} fusion(pred[384,1024]{1,0:T(32,128)(4,1)S(1)} %bitcast_compare_fusion, f16[1024,2048]{1,0:T(8,128)(2,1)S(1)} %all-gather.15), kind=kOutput, calls=%fused_computation.6 | convolution fusion | flops 1614282752 | bytes 6160384 | tf_op jit(solution)/shard_map/dot_general | solution.py:255
  147.9 5.3 %all-to-all-start.1 = ((bf16[4,96,2048]{2,1,0:T(8,128)(2,1)}), bf16[4,96,2048]{2,1,0:T(8,128)(2,1)S(1)}, u32[]{:S(2)}, u32[]{:S(2)}) async-start(bf16[4,96,2048]{2,1,0:T(8,128)(2,1)} %bitcast.183), calls=%async_computation.1 | async-start | bytes 3145728 | tf_op jit(solution)/shard_map/all_to_all | solution.py:257
  153.9 19.6 %all-to-all-done.1 = bf16[4,96,2048]{2,1,0:T(8,128)(2,1)S(1)} async-done(((bf16[4,96,2048]{2,1,0:T(8,128)(2,1)}), bf16[4,96,2048]{2,1,0:T(8,128)(2,1)S(1)}, u32[]{:S(2)}, u32[]{:S(2)}) %all-to-all-start.1) | async-done | bytes 1572896 | tf_op jit(solution)/shard_map/all_to_all | solution.py:257
  174.9 9.2 %shard_map.118 = (bf16[192,2048]{1,0:T(8,128)(2,1)}, bf16[192,2048]{1,0:T(8,128)(2,1)}) custom-call(bf16[384,2048]{1,0:T(8,128)(2,1)} %bitcast.182, bf16[768,2048]{1,0:T(8,128)(2,1)} %bitcast.225, bf16[768,2048]{1,0:T(8,128)(2,1)} %bitcast.226, bf16[4,768,512]{2,1,0:T(8,128)(2,1)} %bitcast.227), custom_call_target="tpu_custom_call" | custom-call | flops 3623878656 | bytes 12582912 | tf_op jit(solution)/shard_map/pallas_call | solution.py:121
  184.1 4.7 %all-to-all-start.2 = ((bf16[8,24,2048]{2,1,0:T(8,128)(2,1)}), bf16[8,24,2048]{2,1,0:T(8,128)(2,1)S(1)}, u32[]{:S(2)}, u32[]{:S(2)}) async-start(bf16[8,24,2048]{2,1,0:T(8,128)(2,1)} %bitcast.185), calls=%async_computation.2 | async-start | bytes 1572864 | tf_op jit(solution)/shard_map/all_to_all | solution.py:289
  190.6 10.5 %all-to-all-done.2 = bf16[8,24,2048]{2,1,0:T(8,128)(2,1)S(1)} async-done(((bf16[8,24,2048]{2,1,0:T(8,128)(2,1)}), bf16[8,24,2048]{2,1,0:T(8,128)(2,1)S(1)}, u32[]{:S(2)}, u32[]{:S(2)}) %all-to-all-start.2) | async-done | bytes 786464 | tf_op jit(solution)/shard_map/all_to_all | solution.py:289
  201.7 2.5 collective-permute-start.4
  204.3 1.4 concatenate.65
  206.4 4.6 %all-to-all-start.3 = ((bf16[8,24,2048]{2,1,0:T(8,128)(2,1)}), bf16[8,24,2048]{2,1,0:T(8,128)(2,1)S(1)}, u32[]{:S(2)}, u32[]{:S(2)}) async-start(bf16[8,24,2048]{2,1,0:T(8,128)(2,1)} %bitcast.60), calls=%async_computation.3 | async-start | bytes 1572864 | tf_op jit(solution)/shard_map/all_to_all | solution.py:289
  211.0 3.6 %collective-permute-start.7 = (bf16[64,2048]{1,0:T(8,128)(2,1)S(1)}, bf16[64,2048]{1,0:T(8,128)(2,1)S(1)}, u32[]{:S(2)}, u32[]{:S(2)}) collective-permute-start(bf16[64,2048]{1,0:T(8,128)(2,1)S(1)} %pad_maximum_fusion), channel_id=1, source_target_pairs={{0,4},{2,6},{4,8},{6,10},{8,12},{10,14},{12,16},{14,18},{16,20},{1... | collective-permute-start | bytes 786440 | tf_op jit(solution)/shard_map/ppermute | solution.py:33
  214.8 3.8 %collective-permute-start.5 = (bf16[64,2048]{1,0:T(8,128)(2,1)S(1)}, bf16[64,2048]{1,0:T(8,128)(2,1)S(1)}, u32[]{:S(2)}, u32[]{:S(2)}) collective-permute-start(bf16[64,2048]{1,0:T(8,128)(2,1)S(1)} %add_convert_fusion.4), channel_id=1, source_target_pairs={{0,28},{2,30},{4,0},{6,2},{8,4},{10,6},{12,8},{14,10},{16,12},{18,... | collective-permute-start | bytes 786440 | tf_op jit(solution)/shard_map/ppermute | solution.py:33
  218.5 4.4 %collective-permute-done.7 = bf16[64,2048]{1,0:T(8,128)(2,1)S(1)} collective-permute-done((bf16[64,2048]{1,0:T(8,128)(2,1)S(1)}, bf16[64,2048]{1,0:T(8,128)(2,1)S(1)}, u32[]{:S(2)}, u32[]{:S(2)}) %collective-permute-start.7) | collective-permute-done | bytes 262176 | tf_op jit(solution)/shard_map/ppermute | solution.py:33
  223.0 2.4 collective-permute-start.8
  226.0 5.0 %collective-permute-start.6 = (bf16[64,2048]{1,0:T(8,128)(2,1)S(1)}, bf16[64,2048]{1,0:T(8,128)(2,1)S(1)}, u32[]{:S(2)}, u32[]{:S(2)}) collective-permute-start(bf16[64,2048]{1,0:T(8,128)(2,1)S(1)} %add_convert_fusion.3), channel_id=1, source_target_pairs={{0,28},{2,30},{4,0},{6,2},{8,4},{10,6},{12,8},{14,10},{16,12},{18,... | collective-permute-start | bytes 786440 | tf_op jit(solution)/shard_map/ppermute | solution.py:33
  231.0 2.5 collective-permute-done.8
  233.5 5.0 %collective-permute-start.9 = (bf16[64,2048]{1,0:T(8,128)(2,1)S(1)}, bf16[64,2048]{1,0:T(8,128)(2,1)S(1)}, u32[]{:S(2)}, u32[]{:S(2)}) collective-permute-start(bf16[64,2048]{1,0:T(8,128)(2,1)S(1)} %add_convert_fusion.1), channel_id=1, source_target_pairs={{0,4},{2,6},{4,8},{6,10},{8,12},{10,14},{12,16},{14,18},{16,20},{1... | collective-permute-start | bytes 786440 | tf_op jit(solution)/shard_map/ppermute | solution.py:33
  238.6 12.8 %collective-permute-start.12 = (bf16[32,2048]{1,0:T(8,128)(2,1)S(1)}, bf16[32,2048]{1,0:T(8,128)(2,1)S(1)}, u32[]{:S(2)}, u32[]{:S(2)}) collective-permute-start(bf16[32,2048]{1,0:T(8,128)(2,1)S(1)} %add_convert_fusion.6), channel_id=1, source_target_pairs={{0,30},{2,0},{4,2},{6,4},{8,6},{10,8},{12,10},{14,12},{16,14},{18,... | collective-permute-start | bytes 393224 | tf_op jit(solution)/shard_map/ppermute | solution.py:33
  251.5 4.4 %collective-permute-start.11 = (bf16[32,2048]{1,0:T(8,128)(2,1)S(1)}, bf16[32,2048]{1,0:T(8,128)(2,1)S(1)}, u32[]{:S(2)}, u32[]{:S(2)}) collective-permute-start(bf16[32,2048]{1,0:T(8,128)(2,1)S(1)} %get-tuple-element.34), channel_id=1, source_target_pairs={{0,2},{2,4},{4,6},{6,8},{8,10},{10,12},{12,14},{14,16},{16,18},{18... | collective-permute-start | bytes 393224 | tf_op jit(solution)/shard_map/ppermute | solution.py:33
  255.9 3.8 %collective-permute-start.10 = (bf16[32,2048]{1,0:T(8,128)(2,1)S(1)}, bf16[32,2048]{1,0:T(8,128)(2,1)S(1)}, u32[]{:S(2)}, u32[]{:S(2)}) collective-permute-start(bf16[32,2048]{1,0:T(8,128)(2,1)S(1)} %get-tuple-element.33), channel_id=1, source_target_pairs={{0,4},{2,6},{4,8},{6,10},{8,12},{10,14},{12,16},{14,18},{16,20},{1... | collective-permute-start | bytes 393224 | tf_op jit(solution)/shard_map/ppermute | solution.py:33
  259.7 1.6 collective-permute-done.11
  261.3 7.0 %collective-permute-done.10 = bf16[32,2048]{1,0:T(8,128)(2,1)S(1)} collective-permute-done((bf16[32,2048]{1,0:T(8,128)(2,1)S(1)}, bf16[32,2048]{1,0:T(8,128)(2,1)S(1)}, u32[]{:S(2)}, u32[]{:S(2)}) %collective-permute-start.10) | collective-permute-done | bytes 131104 | tf_op jit(solution)/shard_map/ppermute | solution.py:33
  (107 shorter events, 18.8 us)
Async XLA Ops:
  6.5 20.5 %copy-start = (bf16[128,1024]{1,0:T(8,128)(2,1)S(1)}, bf16[128,1024]{1,0:T(8,128)(2,1)}, u32[]{:S(2)}) copy-start(bf16[128,1024]{1,0:T(8,128)(2,1)} %param.12) | copy-start | bytes 786436
  6.5 168.3 %all-gather.9.cloned.1.call-start = ((), (), s32[]{:S(2)}) async-start(), calls=%async_computation.4 | async-start | bytes 3932160 | tf_op jit(solution)/shard_map/all_gather | solution.py:189
  7.3 167.6 %all-gather.11.cloned.1.call-start = ((), (), s32[]{:S(2)}) async-start(), calls=%async_computation.5 | async-start | bytes 3932160 | tf_op jit(solution)/shard_map/all_gather | solution.py:190
  8.0 166.9 %all-gather.13.cloned.1.call-start = ((), (), s32[]{:S(2)}) async-start(), calls=%async_computation.6 | async-start | bytes 3932160 | tf_op jit(solution)/shard_map/all_gather | solution.py:191
  17.3 9.7 %collective-permute-start = (bf16[256,256]{1,0:T(8,128)(2,1)S(1)}, bf16[256,256]{1,0:T(8,128)(2,1)S(1)}, u32[]{:S(2)}, u32[]{:S(2)}) collective-permute-start(bf16[256,256]{1,0:T(8,128)(2,1)S(1)} %all_gather.18), channel_id=1, source_target_pairs={{0,4},{2,6},{4,8},{6,10},{8,12},{10,14},{12,16},{14,18},{16,20},{1... | collective-permute-start | bytes 393224 | tf_op jit(solution)/shard_map/ppermute | solution.py:28
  18.6 8.5 %collective-permute-start.1 = (bf16[256,256]{1,0:T(8,128)(2,1)S(1)}, bf16[256,256]{1,0:T(8,128)(2,1)S(1)}, u32[]{:S(2)}, u32[]{:S(2)}) collective-permute-start(bf16[256,256]{1,0:T(8,128)(2,1)S(1)} %all_gather.18), channel_id=1, source_target_pairs={{0,2},{2,4},{4,6},{6,8},{8,10},{10,12},{12,14},{14,16},{16,18},{18... | collective-permute-start | bytes 393224 | tf_op jit(solution)/shard_map/ppermute | solution.py:28
  21.1 5.8 %collective-permute-start.3 = (f16[8,2048]{1,0:T(8,128)(2,1)S(1)}, f16[8,2048]{1,0:T(8,128)(2,1)S(1)}, u32[]{:S(2)}, u32[]{:S(2)}) collective-permute-start(f16[8,2048]{1,0:T(8,128)(2,1)S(1)} %multiply_convert_fusion.2), channel_id=1, source_target_pairs={{0,32},{32,0},{1,33},{33,1},{2,34},{34,2},{3,35},{35,3},{4,36},{36... | collective-permute-start | bytes 98312 | tf_op jit(solution)/shard_map/ppermute | solution.py:33
  29.5 45.4 %collective-permute-start.2 = (bf16[128,512]{1,0:T(8,128)(2,1)S(1)}, bf16[128,512]{1,0:T(8,128)(2,1)S(1)}, u32[]{:S(2)}, u32[]{:S(2)}) collective-permute-start(bf16[128,512]{1,0:T(8,128)(2,1)S(1)} %broadcast_select_fusion.2), channel_id=1, source_target_pairs={{0,64},{64,0},{1,65},{65,1},{2,66},{66,2},{3,67},{67,3},{4,68},{68... | collective-permute-start | bytes 393224 | tf_op jit(solution)/shard_map/ppermute | solution.py:33
  74.9 2.1 copy-start.1
  77.0 24.0 %all-to-all-start = ((bf16[8,32,2048]{2,1,0:T(8,128)(2,1)}), bf16[8,32,2048]{2,1,0:T(8,128)(2,1)S(1)}, u32[]{:S(2)}, u32[]{:S(2)}) async-start(bf16[8,32,2048]{2,1,0:T(8,128)(2,1)} %bitcast.184), calls=%async_computation | async-start | bytes 2097152 | tf_op jit(solution)/shard_map/all_to_all | solution.py:223
  83.6 17.5 %copy-start.3 = (bf16[1,32,2048]{2,1,0:T(8,128)(2,1)S(1)}, bf16[1,32,2048]{2,1,0:T(8,128)(2,1)}, u32[]{:S(2)}) copy-start(bf16[1,32,2048]{2,1,0:T(8,128)(2,1)} %param.16) | copy-start | bytes 393220
  84.4 16.9 %copy-start.4 = (f32[2048]{0:T(1024)S(1)}, f32[2048]{0:T(1024)}, u32[]{:S(2)}) copy-start(f32[2048]{0:T(1024)} %param.18) | copy-start | bytes 24580
  147.9 25.6 %all-to-all-start.1 = ((bf16[4,96,2048]{2,1,0:T(8,128)(2,1)}), bf16[4,96,2048]{2,1,0:T(8,128)(2,1)S(1)}, u32[]{:S(2)}, u32[]{:S(2)}) async-start(bf16[4,96,2048]{2,1,0:T(8,128)(2,1)} %bitcast.183), calls=%async_computation.1 | async-start | bytes 3145728 | tf_op jit(solution)/shard_map/all_to_all | solution.py:257
  173.5 1.4 copy-start.2
  184.1 17.0 %all-to-all-start.2 = ((bf16[8,24,2048]{2,1,0:T(8,128)(2,1)}), bf16[8,24,2048]{2,1,0:T(8,128)(2,1)S(1)}, u32[]{:S(2)}, u32[]{:S(2)}) async-start(bf16[8,24,2048]{2,1,0:T(8,128)(2,1)} %bitcast.185), calls=%async_computation.2 | async-start | bytes 1572864 | tf_op jit(solution)/shard_map/all_to_all | solution.py:289
  201.7 13.0 %collective-permute-start.4 = (bf16[64,2048]{1,0:T(8,128)(2,1)S(1)}, bf16[64,2048]{1,0:T(8,128)(2,1)S(1)}, u32[]{:S(2)}, u32[]{:S(2)}) collective-permute-start(bf16[64,2048]{1,0:T(8,128)(2,1)S(1)} %concatenate.75), channel_id=1, source_target_pairs={{0,28},{2,30},{4,0},{6,2},{8,4},{10,6},{12,8},{14,10},{16,12},{18,... | collective-permute-start | bytes 786440 | tf_op jit(solution)/shard_map/ppermute | solution.py:33
  205.6 19.8 %copy-start.5 = (bf16[8,256]{1,0:T(8,128)(2,1)S(1)}, bf16[8,256]{1,0:T(8,128)(2,1)}, u32[]{:S(2)}) copy-start(bf16[8,256]{1,0:T(8,128)(2,1)} %concatenate.65) | copy-start | bytes 12292
  206.4 19.0 %all-to-all-start.3 = ((bf16[8,24,2048]{2,1,0:T(8,128)(2,1)}), bf16[8,24,2048]{2,1,0:T(8,128)(2,1)S(1)}, u32[]{:S(2)}, u32[]{:S(2)}) async-start(bf16[8,24,2048]{2,1,0:T(8,128)(2,1)} %bitcast.60), calls=%async_computation.3 | async-start | bytes 1572864 | tf_op jit(solution)/shard_map/all_to_all | solution.py:289
  211.0 11.9 %collective-permute-start.7 = (bf16[64,2048]{1,0:T(8,128)(2,1)S(1)}, bf16[64,2048]{1,0:T(8,128)(2,1)S(1)}, u32[]{:S(2)}, u32[]{:S(2)}) collective-permute-start(bf16[64,2048]{1,0:T(8,128)(2,1)S(1)} %pad_maximum_fusion), channel_id=1, source_target_pairs={{0,4},{2,6},{4,8},{6,10},{8,12},{10,14},{12,16},{14,18},{16,20},{1... | collective-permute-start | bytes 786440 | tf_op jit(solution)/shard_map/ppermute | solution.py:33
  214.8 11.2 %collective-permute-start.5 = (bf16[64,2048]{1,0:T(8,128)(2,1)S(1)}, bf16[64,2048]{1,0:T(8,128)(2,1)S(1)}, u32[]{:S(2)}, u32[]{:S(2)}) collective-permute-start(bf16[64,2048]{1,0:T(8,128)(2,1)S(1)} %add_convert_fusion.4), channel_id=1, source_target_pairs={{0,28},{2,30},{4,0},{6,2},{8,4},{10,6},{12,8},{14,10},{16,12},{18,... | collective-permute-start | bytes 786440 | tf_op jit(solution)/shard_map/ppermute | solution.py:33
  223.0 10.5 %collective-permute-start.8 = (bf16[64,2048]{1,0:T(8,128)(2,1)S(1)}, bf16[64,2048]{1,0:T(8,128)(2,1)S(1)}, u32[]{:S(2)}, u32[]{:S(2)}) collective-permute-start(bf16[64,2048]{1,0:T(8,128)(2,1)S(1)} %add_convert_fusion.2), channel_id=1, source_target_pairs={{0,4},{2,6},{4,8},{6,10},{8,12},{10,14},{12,16},{14,18},{16,20},{1... | collective-permute-start | bytes 786440 | tf_op jit(solution)/shard_map/ppermute | solution.py:33
  226.0 12.6 %collective-permute-start.6 = (bf16[64,2048]{1,0:T(8,128)(2,1)S(1)}, bf16[64,2048]{1,0:T(8,128)(2,1)S(1)}, u32[]{:S(2)}, u32[]{:S(2)}) collective-permute-start(bf16[64,2048]{1,0:T(8,128)(2,1)S(1)} %add_convert_fusion.3), channel_id=1, source_target_pairs={{0,28},{2,30},{4,0},{6,2},{8,4},{10,6},{12,8},{14,10},{16,12},{18,... | collective-permute-start | bytes 786440 | tf_op jit(solution)/shard_map/ppermute | solution.py:33
  233.5 17.8 %collective-permute-start.9 = (bf16[64,2048]{1,0:T(8,128)(2,1)S(1)}, bf16[64,2048]{1,0:T(8,128)(2,1)S(1)}, u32[]{:S(2)}, u32[]{:S(2)}) collective-permute-start(bf16[64,2048]{1,0:T(8,128)(2,1)S(1)} %add_convert_fusion.1), channel_id=1, source_target_pairs={{0,4},{2,6},{4,8},{6,10},{8,12},{10,14},{12,16},{14,18},{16,20},{1... | collective-permute-start | bytes 786440 | tf_op jit(solution)/shard_map/ppermute | solution.py:33
  238.6 21.1 %collective-permute-start.12 = (bf16[32,2048]{1,0:T(8,128)(2,1)S(1)}, bf16[32,2048]{1,0:T(8,128)(2,1)S(1)}, u32[]{:S(2)}, u32[]{:S(2)}) collective-permute-start(bf16[32,2048]{1,0:T(8,128)(2,1)S(1)} %add_convert_fusion.6), channel_id=1, source_target_pairs={{0,30},{2,0},{4,2},{6,4},{8,6},{10,8},{12,10},{14,12},{16,14},{18,... | collective-permute-start | bytes 393224 | tf_op jit(solution)/shard_map/ppermute | solution.py:33
  251.5 9.8 %collective-permute-start.11 = (bf16[32,2048]{1,0:T(8,128)(2,1)S(1)}, bf16[32,2048]{1,0:T(8,128)(2,1)S(1)}, u32[]{:S(2)}, u32[]{:S(2)}) collective-permute-start(bf16[32,2048]{1,0:T(8,128)(2,1)S(1)} %get-tuple-element.34), channel_id=1, source_target_pairs={{0,2},{2,4},{4,6},{6,8},{8,10},{10,12},{12,14},{14,16},{16,18},{18... | collective-permute-start | bytes 393224 | tf_op jit(solution)/shard_map/ppermute | solution.py:33
  255.9 12.4 %collective-permute-start.10 = (bf16[32,2048]{1,0:T(8,128)(2,1)S(1)}, bf16[32,2048]{1,0:T(8,128)(2,1)S(1)}, u32[]{:S(2)}, u32[]{:S(2)}) collective-permute-start(bf16[32,2048]{1,0:T(8,128)(2,1)S(1)} %get-tuple-element.33), channel_id=1, source_target_pairs={{0,4},{2,6},{4,8},{6,10},{8,12},{10,14},{12,16},{14,18},{16,20},{1... | collective-permute-start | bytes 393224 | tf_op jit(solution)/shard_map/ppermute | solution.py:33
Sparse Core Ops, SparseCore 0:
  9.5 52.5 all-gather.8
  64.1 58.2 all-gather.10
  124.6 43.7 all-gather.12
